TPU v7x, 512 devices: a whole 4x4x16 slice. The times are simulated.
512 devices in a mesh: section: 4 (over y_hi, core), phase: 8 (over x, y_lo), tp: 16 (over z).
Axes of the slice: x: 4, y: 4 (y_hi: 2, y_lo: 2; y = y_hi * 2 + y_lo), z: 16, core: 2. Of those that a mesh axis runs over, the one named last changes fastest.
Arguments:
- hidden_act: bfloat16 [1024, 28672], P(('section', 'phase'), 'tp'), may hold values from -6 to 6
- down_weight: bfloat16 [28672, 8192], P('tp', ('phase', 'section')), may hold values from -0.03125 to 0.03125
- residual: bfloat16 [1024, 8192], P('section', 'phase'), may hold values from -6 to 6
- head_weight: float32 [8192], P('phase'), may hold values from -0.011048543 to 0.011048543
- gain: float32 [8192], P('phase'), may hold values from 0.1 to 1.9
- behavior_policy_logprob: float32 [1024], replicated, may hold values from -6 to -0.05
- frozen_policy_logprob: float32 [1024], replicated, may hold values from -6 to -0.05
- old_values: float32 [1024], replicated, may hold values from -5 to 5
- judge_ratings: float32 [16], replicated, may hold values from -8 to 8
- lengths: int32 [16], replicated, may hold values from 1 to 192, 1024 in all
Outputs:
- total_loss: float32 [], replicated
- head_grad: float32 [8192], P('phase')
- down_projection_gradient: float32 [28672, 8192], P('tp', ('phase', 'section'))
- hidden_grad: bfloat16 [1024, 28672], P(('section', 'phase'), 'tp')
Inputs may be any that keep to these rules, and one draw needn't show every extreme that they name: The 16 lengths sum to 1024; the longest is exactly 192.
All inputs are finite; a program needn't handle non-finite values.
Results may differ from a plain program's by a relative error of at most 0.0049.
Values may be sent and summed in bfloat16 or wider, within the bound.
No kernel may reach another device: no remote copies, remote signals or barrier semaphores. Data moves between devices by JAX's collectives and lax.ppermute only.
A program may use at most 64 MiB of HBM per device.

v0:
```python
import jax
import jax.numpy as jnp
from jax import lax
from jax.sharding import PartitionSpec as P

D = 8192


KL_PENALTY_SCALE = 0.1
TRACE_DECAY = 0.95
CLIP_RANGE = 0.2
EPSILON = 1e-05


def section_returns(
    behavior_policy_logprob,
    frozen_policy_logprob,
    old_values,
    judge_ratings,
    lengths,
    first_row,
    count,
):
    total = behavior_policy_logprob.shape[0]
    position = jnp.arange(total, dtype=jnp.int32)
    ends = jnp.cumsum(lengths)
    closes_sequence = position[:, None] == ends[None, :] - 1
    final = jnp.any(closes_sequence, axis=1)
    terminal_payoff_extra = jnp.sum(
        jnp.where(closes_sequence, judge_ratings[None, :], jnp.zeros_like(judge_ratings)[None, :]),
        axis=1,
    )
    per_position_payoff = terminal_payoff_extra - KL_PENALTY_SCALE * (
        behavior_policy_logprob - frozen_policy_logprob
    )
    following = jnp.concatenate([old_values[1:], jnp.zeros_like(old_values[:1])])
    following = jnp.where(final, jnp.zeros_like(following), following)
    delta = per_position_payoff + following - old_values
    segment = jnp.sum((position[:, None] >= ends[None, :]).astype(jnp.int32), axis=1)
    row_pos = first_row + jnp.arange(count, dtype=jnp.int32)
    row_seg = lax.dynamic_slice_in_dim(segment, first_row, count, 0)
    gap = position[None, :] - row_pos[:, None]
    inside = (row_seg[:, None] == segment[None, :]) & (gap >= 0)
    powers = jnp.power(
        jnp.full_like(delta[:1], TRACE_DECAY)[0], jnp.maximum(gap, 0).astype(delta.dtype)
    )
    weights = jnp.where(inside, powers, jnp.zeros_like(powers))
    advantage = jnp.dot(weights, delta, precision=lax.Precision.HIGHEST)
    return advantage + lax.dynamic_slice_in_dim(old_values, first_row, count, 0)


def head_terms(combined, scale, target_returns, old_values):
    square_sum, product_sum = lax.psum(
        (
            jnp.sum(combined * combined, axis=1),
            jnp.dot(combined, scale, precision=lax.Precision.HIGHEST),
        ),
        "phase",
    )
    rinv = lax.rsqrt(square_sum / D + EPSILON)
    values = rinv * product_sum
    normed = combined * rinv[:, None]
    squash = jnp.tanh((values - old_values) / CLIP_RANGE)
    clipped = old_values + CLIP_RANGE * squash
    first = (values - target_returns) ** 2
    second = (clipped - target_returns) ** 2
    loss_part = 0.25 * jnp.sum(first + second)
    dvalue = 0.5 * (values - target_returns) + 0.5 * (clipped - target_returns) * (
        1.0 - squash * squash
    )
    head_part = jnp.sum(normed * dvalue[:, None], axis=0)
    grad_rows = (
        (dvalue * rinv)[:, None] * (scale[None, :] - normed * (values / D)[:, None])
    ).astype(jnp.bfloat16)
    return (loss_part, head_part, grad_rows)


def on_device(
    hidden_act,
    down_weight,
    residual,
    head_weight,
    gain,
    behavior_policy_logprob,
    frozen_policy_logprob,
    old_values,
    judge_ratings,
    lengths,
):
    scale = gain * head_weight
    hidden_all = lax.all_gather(hidden_act, "phase", axis=0, tiled=True)
    weight_all = lax.all_gather(down_weight, "section", axis=1, tiled=True)
    count = hidden_all.shape[0]
    section_row = lax.axis_index("section") * count
    target_returns = section_returns(
        behavior_policy_logprob,
        frozen_policy_logprob,
        old_values,
        judge_ratings,
        lengths,
        section_row,
        count,
    )
    own_old = lax.dynamic_slice_in_dim(old_values, section_row, count, 0)
    partial_out = jnp.dot(hidden_all, weight_all, preferred_element_type=jnp.float32)
    block_out = lax.psum(partial_out, "tp")
    combined = residual.astype(jnp.float32) + block_out
    loss_part, head_part, grad_all = head_terms(combined, scale, target_returns, own_old)
    total_loss, head_sum = lax.psum((loss_part, head_part), "section")
    head_grad = gain * head_sum
    width = down_weight.shape[1]
    column_start = lax.axis_index("section") * width
    rows_hidden = lax.all_gather(hidden_all, "section", axis=0, tiled=True)
    rows_grad = lax.all_gather(grad_all, "section", axis=0, tiled=True)
    columns = lax.dynamic_slice_in_dim(rows_grad, column_start, width, 1)
    down_projection_gradient = lax.dot_general(
        rows_hidden, columns, (((0,), (0,)), ((), ())), preferred_element_type=jnp.float32
    )
    hidden_grad = lax.psum_scatter(
        lax.dot_general(
            grad_all, weight_all, (((1,), (1,)), ((), ())), preferred_element_type=jnp.float32
        ),
        "phase",
        scatter_dimension=0,
        tiled=True,
    ).astype(jnp.bfloat16)
    return (total_loss, head_grad, down_projection_gradient, hidden_grad)


def solution(mesh):
    in_specs = (
        P(("section", "phase"), "tp"),
        P("tp", ("phase", "section")),
        P("section", "phase"),
        P("phase"),
        P("phase"),
        P(),
        P(),
        P(),
        P(),
        P(),
    )
    out_specs = (P(), P("phase"), P("tp", ("phase", "section")), P(("section", "phase"), "tp"))
    return jax.shard_map(
        on_device, mesh=mesh, in_specs=in_specs, out_specs=out_specs, check_vma=False
    )
```

profile of v0, /device:TPU:1, one launch (start us, length us, event | category | flops | bytes accessed | tf_op | source)
XLA Modules:
  0.0 347.2 jit_solution(16376566789764249375)
XLA Ops:
  7.2 0.7 all-gather.4.cloned.1.call-update
  7.9 25.2 %all_gather.12 = bf16[256,1792]{1,0:T(8,128)(2,1)S(1)} all-gather(bf16[32,1792]{1,0:T(8,128)(2,1)} %param.10), channel_id=1, replica_groups=mesh['section'=4,'phase'=8,'tp'=16] {'phase'}, dimensions={0}, use_global_device_ids=true | all-gather | bytes 1032192 | tf_op jit(solution)/shard_map/all_gather | solution.py:91
  33.2 27.6 %all-gather.4.cloned.1.call-done = bf16[1792,1024]{1,0:T(8,128)(2,1)} async-done(((bf16[1792,256]{1,0:T(8,128)(2,1)}), bf16[1792,1024]{1,0:T(8,128)(2,1)}) %all-gather.4.cloned.1.call-update) | async-done | bytes 3670032 | tf_op jit(solution)/shard_map/all_gather | solution.py:92
  60.8 4.2 %fusion.24 = f32[256,1024]{1,0:T(8,128)} fusion(bf16[256,1792]{1,0:T(8,128)(2,1)S(1)} %all_gather.12, bf16[1792,1024]{1,0:T(8,128)(2,1)} %all-gather.4.cloned.1.call-done), kind=kOutput, calls=%fused_computation.42 | convolution fusion | flops 939524096 | bytes 5636096 | tf_op jit(solution)/shard_map/dot_general | solution.py:105
  65.1 0.7 all-gather.8.cloned.1.call-update
  66.0 0.1 reduce
  66.3 0.1 fusion.16
  66.4 0.1 select_reduce_fusion
  66.6 1.4 fusion
  68.0 126.6 %all-reduce.4.cloned.1.call-done = f32[256,1024]{1,0:T(8,128)} async-done(((f32[256,1024]{1,0:T(8,128)}), f32[256,1024]{1,0:T(8,128)}) %all-reduce.4.cloned.1.call-update) | async-done | bytes 1048592 | tf_op jit(solution)/shard_map/psum | solution.py:106
  194.5 1.5 multiply_reduce_fusion.1
  196.1 2.2 fusion.15
  198.2 15.8 %all-reduce = (f32[256]{0:T(256)S(1)}, f32[256]{0:T(256)S(1)}) all-reduce(f32[256]{0:T(256)S(1)} %bitcast.16, f32[256]{0:T(256)S(1)} %multiply_reduce_fusion.1), channel_id=1, replica_groups=mesh['section'=4,'phase'=8,'tp'=16] {'phase'}, use_global_device_ids=true, to_apply=%region_3.4 | all-reduce | flops 512 | bytes 4096 | tf_op jit(solution)/shard_map/psum | solution.py:53
  214.0 0.7 fusion.23
  214.7 1.2 multiply_convert_fusion
  216.0 4.6 %fusion.25 = f32[256,1792]{1,0:T(8,128)} fusion(bf16[256,1024]{1,0:T(8,128)(2,1)} %get-tuple-element.22, bf16[1792,1024]{1,0:T(8,128)(2,1)} %all-gather.4.cloned.1.call-done), kind=kOutput, calls=%fused_computation.43 | convolution fusion | flops 939524096 | bytes 6029312 | tf_op jit(solution)/shard_map/dot_general | solution.py:120
  221.2 21.4 %all-reduce.1 = (f32[]{:T(128)}, f32[1024]{0:T(1024)S(1)}) all-reduce(f32[]{:T(128)S(6)} %mul_shard_map.3, f32[1024]{0:T(1024)S(1)} %get-tuple-element.23), channel_id=1, replica_groups=mesh['section'=4,'phase'=8,'tp'=16] {'section'}, use_global_device_ids=true, to_apply=%region_9.10 | all-reduce | flops 1025 | bytes 8200 | tf_op jit(solution)/shard_map/psum | solution.py:109
  242.7 0.6 mul.87
  243.3 3.7 %all-gather.8.cloned.1.call-done = bf16[1024,1792]{1,0:T(8,128)(2,1)} async-done(((bf16[256,1792]{1,0:T(8,128)(2,1)}), bf16[1024,1792]{1,0:T(8,128)(2,1)}) %all-gather.8.cloned.1.call-update) | async-done | bytes 3670032 | tf_op jit(solution)/shard_map/all_gather | solution.py:113
  247.0 36.5 %all-gather.6.cloned.1.call-done = bf16[1024,1024]{1,0:T(8,128)(2,1)} async-done(((bf16[256,1024]{1,0:T(8,128)(2,1)}), bf16[1024,1024]{1,0:T(8,128)(2,1)}) %all-gather.6.cloned.1.call-update) | async-done | bytes 2097168 | tf_op jit(solution)/shard_map/all_gather | solution.py:114
  283.5 3.4 convolution_bitcast_fusion
  286.9 1.7 copy.19
  288.6 50.5 %reduce-scatter.2.cloned.1.call-done = f32[32,1792]{1,0:T(8,128)} async-done(((f32[256,1792]{1,0:T(8,128)}), f32[32,1792]{1,0:T(8,128)}) %reduce-scatter.2.cloned.1.call-update) | async-done | bytes 229392 | tf_op jit(solution)/shard_map/reduce_scatter | solution.py:119
  339.0 1.6 convert_element_type.19
  (37 shorter events, 0.7 us)
Async XLA Ops:
  7.2 53.6 %all-gather.4.cloned.1.call-start = ((), (), s32[]{:S(2)}) async-start(), calls=%async_computation.1 | async-start | bytes 4587520 | tf_op jit(solution)/shard_map/all_gather | solution.py:92
  7.9 186.6 %all-reduce.4.cloned.1.call-start = ((), (), s32[]{:S(2)}) async-start(), calls=%async_computation.2 | async-start | bytes 2097152 | tf_op jit(solution)/shard_map/psum | solution.py:106
  33.2 31.8 %copy-start.2 = (bf16[256,1792]{1,0:T(8,128)(2,1)}, bf16[256,1792]{1,0:T(8,128)(2,1)S(1)}, u32[]{:S(2)}) copy-start(bf16[256,1792]{1,0:T(8,128)(2,1)S(1)} %all_gather.12) | copy-start | bytes 2752516
  33.2 32.6 %copy-start.3 = (f32[1024]{0:T(1024)S(1)}, f32[1024]{0:T(1024)}, u32[]{:S(2)}) copy-start(f32[1024]{0:T(1024)} %param.17) | copy-start | bytes 12292
  33.2 32.7 %copy-start.8 = (s32[16]{0:T(128)S(1)}, s32[16]{0:T(128)}, u32[]{:S(2)}) copy-start(s32[16]{0:T(128)} %param.19) | copy-start | bytes 196
  33.2 33.0 %copy-start.4 = (f32[1024]{0:T(1024)S(1)}, f32[1024]{0:T(1024)}, u32[]{:S(2)}) copy-start(f32[1024]{0:T(1024)} %param.14) | copy-start | bytes 12292
  33.2 33.0 %copy-start.5 = (f32[1024]{0:T(1024)S(1)}, f32[1024]{0:T(1024)}, u32[]{:S(2)}) copy-start(f32[1024]{0:T(1024)} %param.13) | copy-start | bytes 12292
  33.2 33.2 %copy-start.9 = (f32[16]{0:T(128)S(1)}, f32[16]{0:T(128)}, u32[]{:S(2)}) copy-start(f32[16]{0:T(128)} %param.18) | copy-start | bytes 196
  33.2 33.3 %copy-start.6 = (f32[1024]{0:T(1024)S(1)}, f32[1024]{0:T(1024)}, u32[]{:S(2)}) copy-start(f32[1024]{0:T(1024)} %param.15) | copy-start | bytes 12292
  33.2 33.3 %copy-start.7 = (f32[1024]{0:T(1024)S(1)}, f32[1024]{0:T(1024)}, u32[]{:S(2)}) copy-start(f32[1024]{0:T(1024)} %param.16) | copy-start | bytes 12292
  65.0 129.6 %copy-start.1 = (bf16[256,1024]{1,0:T(8,128)(2,1)S(1)}, bf16[256,1024]{1,0:T(8,128)(2,1)}, u32[]{:S(2)}) copy-start(bf16[256,1024]{1,0:T(8,128)(2,1)} %param.12) | copy-start | bytes 1572868
  65.0 182.0 %all-gather.8.cloned.1.call-start = ((), (), s32[]{:S(2)}) async-start(), calls=%async_computation.4 | async-start | bytes 4587520 | tf_op jit(solution)/shard_map/all_gather | solution.py:113
  65.7 217.8 %all-gather.6.cloned.1.call-start = ((), (), s32[]{:S(2)}) async-start(), calls=%async_computation.3 | async-start | bytes 2621440 | tf_op jit(solution)/shard_map/all_gather | solution.py:114
  194.5 20.2 %copy-start = (f32[256,1024]{1,0:T(8,128)S(1)}, f32[256,1024]{1,0:T(8,128)}, u32[]{:S(2)}) copy-start(f32[256,1024]{1,0:T(8,128)} %all-reduce.4.cloned.1.call-done) | copy-start | bytes 3145732
  215.9 123.1 %reduce-scatter.2.cloned.1.call-start = ((), (), s32[]{:S(2)}) async-start(), calls=%async_computation.5 | async-start | bytes 2064384 | tf_op jit(solution)/shard_map/reduce_scatter | solution.py:119
Sparse Core Ops, SparseCore 0:
  10.1 50.6 all-gather.3
  65.1 129.3 all-reduce.3
  196.9 50.0 all-gather.7
  249.7 33.7 all-gather.5
  286.5 52.5 reduce-scatter.1
where the time goes:
time: 348 us; the launch traced here: 347 us
  waiting for transfers between devices  246 us (71%)
  blocking collectives  62.4 us (18%)
  matrix products  15.6 us (4%)
  between operations  14.5 us (4%)
  other arithmetic  6.11 us (2%)
    psum x1, waiting for transfers between devices, on_device(): block_out = lax.psum(partial_out, 'tp')  127 us
    reduce_scatter x1, waiting for transfers between devices, on_device(): lax.psum_scatter(lax.dot_general(grad_all, weight_all, (((1,), (1,)), (()...  50.5 us
    all_gather x1, waiting for transfers between devices, on_device(): rows_grad = lax.all_gather(grad_all, 'section', axis=0, tiled=True)  36.5 us
    all_gather x1, waiting for transfers between devices, on_device(): weight_all = lax.all_gather(down_weight, 'section', axis=1, tiled=True)  27.6 us
    all_gather x1, blocking collectives, on_device(): hidden_all = lax.all_gather(hidden_act, 'phase', axis=0, tiled=True)  25.2 us
    psum x1, blocking collectives, on_device(): total_loss, head_sum = lax.psum((loss_part, head_part), 'section')  21.4 us
    psum x1, blocking collectives, head_terms(): lax.psum((jnp.sum(combined * combined, axis=1), jnp.dot(combined, scale,...  15.8 us
  transfers between devices with their start and end apart: 5, of which 5 were waited for; matrix products, arithmetic and copies ran while one was open for 5% of the time, Pallas kernels for 0%

commit v1 on v0

v1 whole, which is shorter than its diff:
```python
import jax
import jax.numpy as jnp
from jax import lax
from jax.sharding import Mesh, PartitionSpec as P

D = 8192
KL_PENALTY_SCALE = 0.1
TRACE_DECAY = 0.95
CLIP_RANGE = 0.2
EPSILON = 1e-05

PLANE = ("yh", "x", "yl")
SWAP = [(0, 1), (1, 0)]
f32, bf16 = jnp.float32, jnp.bfloat16


def returns_of(behavior, frozen, old_values, judge_ratings, lengths, rows):
    total = behavior.shape[0]
    position = jnp.arange(total, dtype=jnp.int32)
    ends = jnp.cumsum(lengths)
    closes = position[:, None] == ends[None, :] - 1
    final = jnp.any(closes, axis=1)
    extra = jnp.sum(jnp.where(closes, judge_ratings[None, :], 0.0), axis=1)
    rewards = extra - KL_PENALTY_SCALE * (behavior - frozen)
    following = jnp.concatenate([old_values[1:], jnp.zeros_like(old_values[:1])])
    delta = rewards + jnp.where(final, 0.0, following) - old_values
    segment = jnp.sum((position[:, None] >= ends[None, :]).astype(jnp.int32), axis=1)
    row_seg = jnp.sum((rows[:, None] >= ends[None, :]).astype(jnp.int32), axis=1)
    gap = position[None, :] - rows[:, None]
    inside = (row_seg[:, None] == segment[None, :]) & (gap >= 0)
    powers = jnp.power(jnp.float32(TRACE_DECAY), jnp.maximum(gap, 0).astype(f32))
    return jnp.sum(jnp.where(inside, powers, 0.0) * delta[None, :], axis=1)


def pieces(x, count):
    out = []
    for _ in range(count):
        top = lax.reduce_precision(x, 8, 7)
        out.append(top.astype(bf16))
        x = x - top
    return out


def gather_all_to_all(x, axes, count):
    spread = jnp.broadcast_to(x[None], (count,) + x.shape)
    return lax.all_to_all(spread, axes, 0, 0, tiled=True)


def on_device(
    hidden_act,
    down_weight,
    residual,
    head_weight,
    gain,
    behavior,
    frozen,
    old_values,
    judge_ratings,
    lengths,
):
    yh, core, z = lax.axis_index("yh"), lax.axis_index("core"), lax.axis_index("z")
    spot = lax.axis_index(PLANE)
    rows_each, units = hidden_act.shape
    width = down_weight.shape[1]
    chip = 2 * width
    group = 16 * rows_each
    section_rows = 8 * rows_each

    other_weight = lax.ppermute(down_weight, "core", SWAP)
    weight = jnp.concatenate(
        [
            jnp.where(core == 0, down_weight, other_weight),
            jnp.where(core == 0, other_weight, down_weight),
        ],
        axis=1,
    )
    scale = lax.dynamic_slice_in_dim(gain * head_weight, yh * chip, chip, 0)
    own_scale = lax.dynamic_slice_in_dim(scale, core * width, width, 0)

    holder, block = z // 8, z % 8
    kept = lax.dynamic_slice_in_dim(residual, block * rows_each, rows_each, 0)
    sent = lax.dynamic_slice_in_dim(kept, (1 - yh) * chip, chip, 1)
    mine = lax.dynamic_slice_in_dim(kept, yh * chip, chip, 1)
    got = lax.ppermute(sent, "yh", SWAP)
    stream = jnp.where(yh == holder, mine, got)

    hidden = gather_all_to_all(hidden_act, PLANE, 16).reshape(group, units)
    other_hidden = lax.ppermute(hidden, "core", SWAP)

    partial = jnp.dot(hidden, weight, preferred_element_type=f32).astype(bf16)
    parts = lax.all_to_all(partial.reshape(16, rows_each, chip), "z", 0, 0, tiled=True)
    combined = (jnp.sum(parts.astype(f32), axis=0) + stream.astype(f32)).astype(bf16)
    combined = lax.all_gather(combined, "z", axis=0, tiled=True)

    left, right = combined[:, :width], combined[:, width:]
    own_columns = jnp.where(core == 0, left, right)
    other_columns = lax.ppermute(jnp.where(core == 0, right, left), "core", SWAP)

    wide = combined.astype(f32)
    square_part = jnp.sum(wide * wide, axis=1)
    product_part = jnp.sum(wide * scale[None, :], axis=1)
    back = (((1,), (1,)), ((), ()))
    scale_rows = jnp.stack(pieces(scale, 3) + [jnp.zeros_like(scale, dtype=bf16)] * 5)
    scale_back = jnp.sum(
        lax.dot_general(scale_rows, weight, back, preferred_element_type=f32), axis=0
    )
    back_part = lax.dot_general(combined, weight, back, preferred_element_type=f32).astype(bf16)
    small = pieces(square_part, 3) + pieces(product_part, 3) + pieces(scale_back, 2)
    small = jnp.concatenate(small)
    small = jnp.pad(small, (0, rows_each * 256 - small.shape[0])).reshape(rows_each, 256)
    payload = jnp.concatenate(
        [
            back_part.reshape(16, rows_each, units),
            jnp.broadcast_to(small[None], (16, rows_each, 256)),
        ],
        axis=2,
    )
    arrived = lax.all_to_all(payload, PLANE, 0, 0, tiled=True)
    back_sum = jnp.sum(arrived[:, :, :units].astype(f32), axis=0)
    small = jnp.sum(arrived[:, :, units:].astype(f32), axis=0).reshape(-1)
    cut = [small[i * group : (i + 1) * group] for i in range(6)]
    square_sum = cut[0] + cut[1] + cut[2]
    product_sum = cut[3] + cut[4] + cut[5]
    tail = small[6 * group : 6 * group + 2 * units].reshape(2, units)
    scale_back = tail[0] + tail[1]

    slot = jnp.arange(group, dtype=jnp.int32)
    token = slot + section_rows * (slot // section_rows + core)
    own_old = jnp.concatenate(
        [
            lax.dynamic_slice_in_dim(old_values, core * section_rows, section_rows, 0),
            lax.dynamic_slice_in_dim(old_values, (2 + core) * section_rows, section_rows, 0),
        ]
    )
    returns = own_old + returns_of(behavior, frozen, old_values, judge_ratings, lengths, token)
    rinv = lax.rsqrt(square_sum / D + EPSILON)
    values = rinv * product_sum
    squash = jnp.tanh((values - own_old) / CLIP_RANGE)
    clipped = own_old + CLIP_RANGE * squash
    first = (values - returns) ** 2
    second = (clipped - returns) ** 2
    loss = 0.25 * jnp.sum(first + second)
    dvalue = 0.5 * (values - returns) + 0.5 * (clipped - returns) * (1.0 - squash * squash)
    up = dvalue * rinv
    down = up * rinv * values / D

    own_up = lax.dynamic_slice_in_dim(up, spot * rows_each, rows_each, 0)
    own_down = lax.dynamic_slice_in_dim(down, spot * rows_each, rows_each, 0)
    hidden_grad = (own_up[:, None] * scale_back[None, :] - own_down[:, None] * back_sum).astype(bf16)

    head_part = jnp.sum(up[:, None] * wide, axis=0)
    packed = jnp.stack([up, down, head_part, jnp.full_like(up, loss)])
    other = lax.ppermute(packed, "core", SWAP)
    total_loss = loss + other[3, 0]
    head_chip = head_part + other[2]
    head_far = lax.ppermute(head_chip, "yh", SWAP)
    head_sum = jnp.concatenate(
        [jnp.where(yh == 0, head_chip, head_far), jnp.where(yh == 0, head_far, head_chip)]
    )
    head_grad = gain * head_sum

    def rows_of(up, down, columns):
        return (up[:, None] * own_scale[None, :] - down[:, None] * columns.astype(f32)).astype(bf16)

    over_tokens = (((0,), (0,)), ((), ()))
    weight_grad = lax.dot_general(
        hidden, rows_of(up, down, own_columns), over_tokens, preferred_element_type=f32
    ) + lax.dot_general(
        other_hidden,
        rows_of(other[0], other[1], other_columns),
        over_tokens,
        preferred_element_type=f32,
    )
    return (total_loss, head_grad, weight_grad, hidden_grad)


def solution(mesh):
    fine = Mesh(mesh.devices.reshape(2, 2, 4, 2, 16), ("yh", "core", "x", "yl", "z"))
    in_specs = (
        P(("yh", "core", "x", "yl"), "z"),
        P("z", ("x", "yl", "yh", "core")),
        P(("yh", "core"), ("x", "yl")),
        P(("x", "yl")),
        P(("x", "yl")),
        P(),
        P(),
        P(),
        P(),
        P(),
    )
    out_specs = (
        P(),
        P(("x", "yl")),
        P("z", ("x", "yl", "yh", "core")),
        P(("yh", "core", "x", "yl"), "z"),
    )
    return jax.shard_map(
        on_device, mesh=fine, in_specs=in_specs, out_specs=out_specs, check_vma=False
    )
```

time: 348 us -> 168 us (0.48)
  waiting for transfers between devices: 246 us -> 33.3 us
  starting transfers between devices: 0.2 us -> 73.2 us
  blocking collectives: 62.4 us -> 28 us
  between operations: 14.5 us -> 3.55 us
  local copies, waits for them, and re-layouts: 1.97 us -> 7.91 us
  matrix products: 15.6 us -> 11.3 us
  other arithmetic: 6.11 us -> 10 us
    psum x1 -> x0, waiting for transfers between devices: 127 us -> none  [on_device(): block_out = lax.psum(partial_out, 'tp')]
    all_gather x3 -> x0, waiting for transfers between devices: 67.8 us -> none  [the longest x1 36.5 us: on_device(): rows_grad = lax.all_gather(grad_all, 'section', axis=0, tiled=True)]
    reduce_scatter x1 -> x0, waiting for transfers between devices: 50.5 us -> none  [on_device(): lax.psum_scatter(lax.dot_general(grad_all, weight_all, (((1,), (1,)), (()...]
    ppermute x0 -> x6, starting transfers between devices: none -> 42 us  [the longest x1 15.8 us: on_device(): other = lax.ppermute(packed, 'core', SWAP)]
    psum x2 -> x0, blocking collectives: 37.2 us -> none  [the longest x1 21.4 us: on_device(): total_loss, head_sum = lax.psum((loss_part, head_part), 'section')]
    all_to_all x0 -> x3, waiting for transfers between devices: none -> 31.1 us  [the longest x1 17.6 us: on_device(): lax.all_to_all(partial.reshape(16, rows_each, chip), 'z', 0, 0, tiled=True)]
    all_to_all x0 -> x3, starting transfers between devices: none -> 31.1 us  [the longest x1 19.5 us: on_device(): lax.all_to_all(partial.reshape(16, rows_each, chip), 'z', 0, 0, tiled=True)]
    dot_general x5, matrix products: 15.6 us -> 11.3 us  [the longest x1 4.08 us: on_device(): partial = jnp.dot(hidden, weight, preferred_element_type=f32).astype(bf16)]
  transfers between devices with their start and end apart: 5 -> 9, of which waited for: 5 -> 3; matrix products, arithmetic and copies ran while one was open for 5% -> 9% of each run, Pallas kernels for 0% -> 0%
where the time goes in v1:
time: 168 us; the launch traced here: 167 us
  starting transfers between devices  73.2 us (44%)
  waiting for transfers between devices  33.3 us (20%)
  blocking collectives  28 us (17%)
  matrix products  11.3 us (7%)
  other arithmetic  10 us (6%)
  local copies, waits for them, and re-layouts  7.91 us (5%)
  between operations  3.55 us (2%)
    all_gather x1, blocking collectives, on_device(): combined = lax.all_gather(combined, 'z', axis=0, tiled=True)  28 us
    all_to_all x1, starting transfers between devices, on_device(): lax.all_to_all(partial.reshape(16, rows_each, chip), 'z', 0, 0, tiled=True)  19.5 us
    all_to_all x1, waiting for transfers between devices, on_device(): lax.all_to_all(partial.reshape(16, rows_each, chip), 'z', 0, 0, tiled=True)  17.6 us
    ppermute x1, starting transfers between devices, on_device(): other = lax.ppermute(packed, 'core', SWAP)  15.8 us
    ppermute x1, starting transfers between devices, on_device(): other_hidden = lax.ppermute(hidden, 'core', SWAP)  14.4 us
    all_to_all x1, waiting for transfers between devices, gather_all_to_all(): return lax.all_to_all(spread, axes, 0, 0, tiled=True)  13.5 us
    all_to_all x1, starting transfers between devices, gather_all_to_all(): return lax.all_to_all(spread, axes, 0, 0, tiled=True)  7.72 us
    ppermute x1, starting transfers between devices, on_device(): other_weight = lax.ppermute(down_weight, 'core', SWAP)  4.92 us
  transfers between devices with their start and end apart: 9, of which 3 were waited for; matrix products, arithmetic and copies ran while one was open for 9% of the time, Pallas kernels for 0%

profile of v1, /device:TPU:1, one launch (start us, length us, event | category | flops | bytes accessed | tf_op | source)
XLA Modules:
  0.0 167.3 jit_solution(6131986597461020178)
XLA Ops:
  0.6 2.3 %broadcast_in_dim.25 = bf16[16,32,1792]{2,1,0:T(8,128)(2,1)} broadcast(bf16[32,1792]{1,0:T(8,128)(2,1)} %param.10), dimensions={1,2} | broadcast | bytes 1949696 | tf_op jit(solution)/shard_map/broadcast_in_dim | solution.py:45
  2.9 7.7 %all-to-all-start = ((bf16[16,32,1792]{2,1,0:T(8,128)(2,1)}), bf16[16,32,1792]{2,1,0:T(8,128)(2,1)S(1)}, u32[]{:S(2)}, u32[]{:S(2)}) async-start(bf16[16,32,1792]{2,1,0:T(8,128)(2,1)} %broadcast_in_dim.25), calls=%async_computation | async-start | bytes 3670016 | tf_op jit(solution)/shard_map/all_to_all | solution.py:46
  10.7 4.9 %collective-permute-start = (bf16[1792,256]{1,0:T(8,128)(2,1)S(1)}, bf16[1792,256]{1,0:T(8,128)(2,1)}, u32[]{:S(2)}, u32[]{:S(2)}) collective-permute-start(bf16[1792,256]{1,0:T(8,128)(2,1)S(1)} %copy-done.2), channel_id=1, source_target_pairs={{0,128},{128,0},{1,129},{129,1},{2,130},{130,2},{3,131},{131,3},{4... | collective-permute-start | bytes 2752520 | tf_op jit(solution)/shard_map/ppermute | solution.py:69
  15.6 2.2 %collective-permute-done = bf16[1792,256]{1,0:T(8,128)(2,1)} collective-permute-done((bf16[1792,256]{1,0:T(8,128)(2,1)S(1)}, bf16[1792,256]{1,0:T(8,128)(2,1)}, u32[]{:S(2)}, u32[]{:S(2)}) %collective-permute-start) | collective-permute-done | bytes 917536 | tf_op jit(solution)/shard_map/ppermute | solution.py:69
  17.8 2.5 %broadcast_select_fusion.1 = (bf16[1792,256]{1,0:T(8,128)(2,1)}, bf16[1792,256]{1,0:T(8,128)(2,1)}) fusion(bf16[1792,256]{1,0:T(8,128)(2,1)S(1)} %copy-done.2, bf16[1792,256]{1,0:T(8,128)(2,1)} %collective-permute-done, pred[]{:T(512)S(6)} %eq.18), kind=kLoop, calls=%fused_computation.20 | loop fusion | flops 917504 | bytes 3670017 | tf_op jit(solution)/shard_map/jit(_where)/select_n | solution.py:72
  20.4 13.5 %all-to-all-done = bf16[16,32,1792]{2,1,0:T(8,128)(2,1)S(1)} async-done(((bf16[16,32,1792]{2,1,0:T(8,128)(2,1)}), bf16[16,32,1792]{2,1,0:T(8,128)(2,1)S(1)}, u32[]{:S(2)}, u32[]{:S(2)}) %all-to-all-start) | async-done | bytes 1835040 | tf_op jit(solution)/shard_map/all_to_all | solution.py:46
  33.9 4.1 %convolution_convert_fusion.1 = bf16[512,512]{0,1:T(8,128)(2,1)} fusion(bf16[512,1792]{1,0:T(8,128)(2,1)S(1)} %bitcast.32, bf16[1792,256]{1,0:T(8,128)(2,1)} %get-tuple-element.28, bf16[1792,256]{1,0:T(8,128)(2,1)} %get-tuple-element.27), kind=kOutput, calls=%fused_computation.13 | convolution fusion | flops 943456256 | bytes 4194304 | tf_op jit(solution)/shard_map/dot_general | solution.py:90
  37.9 19.5 %all-to-all-start.1 = ((bf16[16,32,512]{2,1,0:T(8,128)(2,1)}), bf16[16,32,512]{2,1,0:T(8,128)(2,1)S(1)}, u32[]{:S(2)}, u32[]{:S(2)}) async-start(bf16[16,32,512]{2,1,0:T(8,128)(2,1)} %bitcast.2), calls=%async_computation.1 | async-start | bytes 1048576 | tf_op jit(solution)/shard_map/all_to_all | solution.py:91
  57.5 0.9 dynamic_slice.28
  58.4 2.2 %collective-permute-start.1 = (bf16[32,512]{1,0:T(8,128)(2,1)S(1)}, bf16[32,512]{1,0:T(8,128)(2,1)S(1)}, u32[]{:S(2)}, u32[]{:S(2)}) collective-permute-start(bf16[32,512]{1,0:T(8,128)(2,1)S(1)} %dynamic_slice.28), channel_id=1, source_target_pairs={{0,256},{256,0},{1,257},{257,1},{2,258},{258,2},{3,259},{259,3},{4... | collective-permute-start | bytes 98312 | tf_op jit(solution)/shard_map/ppermute | solution.py:84
  60.9 1.8 %convolution_reduce_fusion = f32[1792]{0:T(1024)S(1)} fusion(bf16[8,512]{1,0:T(8,128)(2,1)S(1)} %stack.27, bf16[1792,256]{1,0:T(8,128)(2,1)} %get-tuple-element.28, bf16[1792,256]{1,0:T(8,128)(2,1)S(1)} %copy-done.3), kind=kOutput, calls=%fused_computation.14 | convolution fusion | flops 18362624 | bytes 1850368 | tf_op jit(solution)/shard_map/dot_general | solution.py:105
  62.7 17.6 %all-to-all-done.1 = bf16[16,32,512]{2,1,0:T(8,128)(2,1)S(1)} async-done(((bf16[16,32,512]{2,1,0:T(8,128)(2,1)}), bf16[16,32,512]{2,1,0:T(8,128)(2,1)S(1)}, u32[]{:S(2)}, u32[]{:S(2)}) %all-to-all-start.1) | async-done | bytes 524320 | tf_op jit(solution)/shard_map/all_to_all | solution.py:91
  80.4 0.9 add_convert_fusion
  81.3 28.0 %all_gather.3 = bf16[512,512]{1,0:T(8,128)(2,1)S(1)} all-gather(bf16[32,512]{1,0:T(8,128)(2,1)S(1)} %add_convert_fusion), channel_id=1, replica_groups=mesh['yh'=2,'core'=2,'x'=4,'yl'=2,'z'=16] {'z'}, dimensions={0}, use_global_device_ids=true | all-gather | bytes 557056 | tf_op jit(solution)/shard_map/all_gather | solution.py:93
  109.3 2.3 %convolution_convert_fusion = bf16[512,1792]{1,0:T(8,128)(2,1)S(1)} fusion(bf16[512,512]{1,0:T(8,128)(2,1)S(1)} %all_gather.3, bf16[1792,256]{1,0:T(8,128)(2,1)} %get-tuple-element.28, bf16[1792,256]{1,0:T(8,128)(2,1)S(1)} %copy-done.3), kind=kOutput, calls=%fused_computation.1 | convolution fusion | flops 944111616 | bytes 4194304 | tf_op jit(solution)/shard_map/dot_general | solution.py:107
  113.8 1.6 pad_maximum_fusion
  115.4 3.9 %all-to-all-start.2 = ((bf16[16,32,2048]{2,1,0:T(8,128)(2,1)}), bf16[16,32,2048]{2,1,0:T(8,128)(2,1)S(1)}, u32[]{:S(2)}, u32[]{:S(2)}) async-start(bf16[16,32,2048]{2,1,0:T(8,128)(2,1)} %pad_maximum_fusion), calls=%async_computation.2 | async-start | bytes 4194304 | tf_op jit(solution)/shard_map/all_to_all | solution.py:118
  120.2 1.2 multiply_reduce_fusion
  121.5 14.4 %collective-permute-start.5 = (bf16[512,1792]{1,0:T(8,128)(2,1)}, bf16[512,1792]{1,0:T(8,128)(2,1)}, u32[]{:S(2)}, u32[]{:S(2)}) collective-permute-start(bf16[512,1792]{1,0:T(8,128)(2,1)} %bitcast.33), channel_id=1, source_target_pairs={{0,128},{128,0},{1,129},{129,1},{2,130},{130,2},{3,131},{131,3},{4... | collective-permute-start | bytes 5505032 | tf_op jit(solution)/shard_map/ppermute | solution.py:88
  135.9 1.9 %collective-permute-start.4 = (bf16[512,256]{1,0:T(8,128)(2,1)S(1)}, bf16[512,256]{1,0:T(8,128)(2,1)S(1)}, u32[]{:S(2)}, u32[]{:S(2)}) collective-permute-start(bf16[512,256]{1,0:T(8,128)(2,1)S(1)} %broadcast_select_fusion.2), channel_id=1, source_target_pairs={{0,128},{128,0},{1,129},{129,1},{2,130},{130,2},{3,131},{131,3},{4... | collective-permute-start | bytes 786440 | tf_op jit(solution)/shard_map/ppermute | solution.py:97
  139.8 15.8 %collective-permute-start.2 = (f32[4,512]{1,0:T(4,128)S(1)}, f32[4,512]{1,0:T(4,128)S(1)}, u32[]{:S(2)}, u32[]{:S(2)}) collective-permute-start(f32[4,512]{1,0:T(4,128)S(1)} %maximum_maximum_fusion), channel_id=1, source_target_pairs={{0,128},{128,0},{1,129},{129,1},{2,130},{130,2},{3,131},{131,3},{4... | collective-permute-start | bytes 24584 | tf_op jit(solution)/shard_map/ppermute | solution.py:153
  157.5 2.8 %collective-permute-start.3 = (f32[512]{0:T(512)S(1)}, f32[512]{0:T(512)S(1)}, u32[]{:S(2)}, u32[]{:S(2)}) collective-permute-start(f32[512]{0:T(512)S(1)} %add.342), channel_id=1, source_target_pairs={{0,256},{256,0},{1,257},{257,1},{2,258},{258,2},{3,259},{259,3},{4... | collective-permute-start | bytes 6152 | tf_op jit(solution)/shard_map/ppermute | solution.py:156
  160.4 2.3 %fusion = f32[1792,256]{0,1:T(8,128)S(1)} fusion(f32[256,1792]{1,0:T(8,128)S(1)} %fusion.6, bf16[512,1792]{1,0:T(8,128)(2,1)} %collective-permute-done.5, bf16[512,256]{1,0:T(8,128)(2,1)S(1)} %collective-permute-done.4, f32[512]{0:T(512)S(1)} %bitcast.45, f32[512]{0:T(512)S(1)} %bitcast.44, f32[256]{0:T(256)S(1)} %dynamic_slice.33), kind=kOutput, calls=%fused_computation.3 | convolution fusion | flops 470876160 | bytes 5772288 | tf_op jit(solution)/shard_map/dot_general | solution.py:168
  162.7 1.7 %copy.19 = f32[1792,256]{1,0:T(8,128)} copy(f32[1792,256]{0,1:T(8,128)S(1)} %fusion) | data formatting | bytes 3670016
  (93 shorter events, 7.6 us)
Async XLA Ops:
  2.9 7.7 %copy-start.2 = (bf16[1792,256]{1,0:T(8,128)(2,1)S(1)}, bf16[1792,256]{1,0:T(8,128)(2,1)}, u32[]{:S(2)}) copy-start(bf16[1792,256]{1,0:T(8,128)(2,1)} %param.11) | copy-start | bytes 2752516
  2.9 30.9 %all-to-all-start = ((bf16[16,32,1792]{2,1,0:T(8,128)(2,1)}), bf16[16,32,1792]{2,1,0:T(8,128)(2,1)S(1)}, u32[]{:S(2)}, u32[]{:S(2)}) async-start(bf16[16,32,1792]{2,1,0:T(8,128)(2,1)} %broadcast_in_dim.25), calls=%async_computation | async-start | bytes 3670016 | tf_op jit(solution)/shard_map/all_to_all | solution.py:46
  10.7 7.1 %collective-permute-start = (bf16[1792,256]{1,0:T(8,128)(2,1)S(1)}, bf16[1792,256]{1,0:T(8,128)(2,1)}, u32[]{:S(2)}, u32[]{:S(2)}) collective-permute-start(bf16[1792,256]{1,0:T(8,128)(2,1)S(1)} %copy-done.2), channel_id=1, source_target_pairs={{0,128},{128,0},{1,129},{129,1},{2,130},{130,2},{3,131},{131,3},{4... | collective-permute-start | bytes 2752520 | tf_op jit(solution)/shard_map/ppermute | solution.py:69
  33.8 4.1 %copy-start = (bf16[16,32,1792]{2,1,0:T(8,128)(2,1)}, bf16[16,32,1792]{2,1,0:T(8,128)(2,1)S(1)}, u32[]{:S(2)}) copy-start(bf16[16,32,1792]{2,1,0:T(8,128)(2,1)S(1)} %all-to-all-done) | copy-start | bytes 5505028
  33.8 26.8 %copy-start.5 = (f32[1024]{0:T(1024)S(1)}, f32[1024]{0:T(1024)}, u32[]{:S(2)}) copy-start(f32[1024]{0:T(1024)} %param.14) | copy-start | bytes 12292
  33.9 26.8 %copy-start.6 = (f32[1024]{0:T(1024)S(1)}, f32[1024]{0:T(1024)}, u32[]{:S(2)}) copy-start(f32[1024]{0:T(1024)} %param.13) | copy-start | bytes 12292
  33.9 27.0 %copy-start.3 = (bf16[1792,256]{1,0:T(8,128)(2,1)S(1)}, bf16[1792,256]{1,0:T(8,128)(2,1)}, u32[]{:S(2)}) copy-start(bf16[1792,256]{1,0:T(8,128)(2,1)} %get-tuple-element.27) | copy-start | bytes 2752516
  37.9 42.4 %all-to-all-start.1 = ((bf16[16,32,512]{2,1,0:T(8,128)(2,1)}), bf16[16,32,512]{2,1,0:T(8,128)(2,1)S(1)}, u32[]{:S(2)}, u32[]{:S(2)}) async-start(bf16[16,32,512]{2,1,0:T(8,128)(2,1)} %bitcast.2), calls=%async_computation.1 | async-start | bytes 1048576 | tf_op jit(solution)/shard_map/all_to_all | solution.py:91
  58.4 22.0 %collective-permute-start.1 = (bf16[32,512]{1,0:T(8,128)(2,1)S(1)}, bf16[32,512]{1,0:T(8,128)(2,1)S(1)}, u32[]{:S(2)}, u32[]{:S(2)}) collective-permute-start(bf16[32,512]{1,0:T(8,128)(2,1)S(1)} %dynamic_slice.28), channel_id=1, source_target_pairs={{0,256},{256,0},{1,257},{257,1},{2,258},{258,2},{3,259},{259,3},{4... | collective-permute-start | bytes 98312 | tf_op jit(solution)/shard_map/ppermute | solution.py:84
  115.4 3.9 %copy-start.4 = (f32[1024]{0:T(1024)S(1)}, f32[1024]{0:T(1024)}, u32[]{:S(2)}) copy-start(f32[1024]{0:T(1024)} %param.17) | copy-start | bytes 12292
  115.4 4.1 %copy-start.9 = (s32[16]{0:T(128)S(1)}, s32[16]{0:T(128)}, u32[]{:S(2)}) copy-start(s32[16]{0:T(128)} %param.19) | copy-start | bytes 196
  115.4 4.6 %copy-start.10 = (f32[16]{0:T(128)S(1)}, f32[16]{0:T(128)}, u32[]{:S(2)}) copy-start(f32[16]{0:T(128)} %param.18) | copy-start | bytes 196
  115.4 4.7 %copy-start.7 = (f32[1024]{0:T(1024)S(1)}, f32[1024]{0:T(1024)}, u32[]{:S(2)}) copy-start(f32[1024]{0:T(1024)} %param.15) | copy-start | bytes 12292
  115.4 4.7 %copy-start.8 = (f32[1024]{0:T(1024)S(1)}, f32[1024]{0:T(1024)}, u32[]{:S(2)}) copy-start(f32[1024]{0:T(1024)} %param.16) | copy-start | bytes 12292
  115.4 22.4 %all-to-all-start.2 = ((bf16[16,32,2048]{2,1,0:T(8,128)(2,1)}), bf16[16,32,2048]{2,1,0:T(8,128)(2,1)S(1)}, u32[]{:S(2)}, u32[]{:S(2)}) async-start(bf16[16,32,2048]{2,1,0:T(8,128)(2,1)} %pad_maximum_fusion), calls=%async_computation.2 | async-start | bytes 4194304 | tf_op jit(solution)/shard_map/all_to_all | solution.py:118
  121.5 38.8 %collective-permute-start.5 = (bf16[512,1792]{1,0:T(8,128)(2,1)}, bf16[512,1792]{1,0:T(8,128)(2,1)}, u32[]{:S(2)}, u32[]{:S(2)}) collective-permute-start(bf16[512,1792]{1,0:T(8,128)(2,1)} %bitcast.33), channel_id=1, source_target_pairs={{0,128},{128,0},{1,129},{129,1},{2,130},{130,2},{3,131},{131,3},{4... | collective-permute-start | bytes 5505032 | tf_op jit(solution)/shard_map/ppermute | solution.py:88
  135.9 24.4 %collective-permute-start.4 = (bf16[512,256]{1,0:T(8,128)(2,1)S(1)}, bf16[512,256]{1,0:T(8,128)(2,1)S(1)}, u32[]{:S(2)}, u32[]{:S(2)}) collective-permute-start(bf16[512,256]{1,0:T(8,128)(2,1)S(1)} %broadcast_select_fusion.2), channel_id=1, source_target_pairs={{0,128},{128,0},{1,129},{129,1},{2,130},{130,2},{3,131},{131,3},{4... | collective-permute-start | bytes 786440 | tf_op jit(solution)/shard_map/ppermute | solution.py:97
  139.4 17.3 %copy-start.1 = (bf16[16,32,1792]{2,1,0:T(8,128)(2,1)S(1)}, bf16[16,32,1792]{2,1,0:T(8,128)(2,1)}, u32[]{:S(2)}) copy-start(bf16[16,32,1792]{2,1,0:T(8,128)(2,1)} %copy-done) | copy-start | bytes 5505028
  139.8 17.7 %collective-permute-start.2 = (f32[4,512]{1,0:T(4,128)S(1)}, f32[4,512]{1,0:T(4,128)S(1)}, u32[]{:S(2)}, u32[]{:S(2)}) collective-permute-start(f32[4,512]{1,0:T(4,128)S(1)} %maximum_maximum_fusion), channel_id=1, source_target_pairs={{0,128},{128,0},{1,129},{129,1},{2,130},{130,2},{3,131},{131,3},{4... | collective-permute-start | bytes 24584 | tf_op jit(solution)/shard_map/ppermute | solution.py:153
  157.5 8.0 %collective-permute-start.3 = (f32[512]{0:T(512)S(1)}, f32[512]{0:T(512)S(1)}, u32[]{:S(2)}, u32[]{:S(2)}) collective-permute-start(f32[512]{0:T(512)S(1)} %add.342), channel_id=1, source_target_pairs={{0,256},{256,0},{1,257},{257,1},{2,258},{258,2},{3,259},{259,3},{4... | collective-permute-start | bytes 6152 | tf_op jit(solution)/shard_map/ppermute | solution.py:156

commit v2 on v1

v2 whole, which is shorter than its diff:
```python
import jax
import jax.numpy as jnp
from jax import lax
from jax.experimental import pallas as pl
from jax.experimental.pallas import tpu as pltpu
from jax.sharding import Mesh, PartitionSpec as P

D = 8192
KL_PENALTY_SCALE = 0.1
TRACE_DECAY = 0.95
CLIP_RANGE = 0.2
EPSILON = 1e-05

PLANE = ("yh", "x", "yl")
SWAP = [(0, 1), (1, 0)]
f32, bf16 = jnp.float32, jnp.bfloat16


def returns_of(behavior, frozen, old_values, judge_ratings, lengths, rows):
    total = behavior.shape[0]
    position = jnp.arange(total, dtype=jnp.int32)
    ends = jnp.cumsum(lengths)
    closes = position[:, None] == ends[None, :] - 1
    final = jnp.any(closes, axis=1)
    extra = jnp.sum(jnp.where(closes, judge_ratings[None, :], 0.0), axis=1)
    rewards = extra - KL_PENALTY_SCALE * (behavior - frozen)
    following = jnp.concatenate([old_values[1:], jnp.zeros_like(old_values[:1])])
    delta = rewards + jnp.where(final, 0.0, following) - old_values
    segment = jnp.sum((position[:, None] >= ends[None, :]).astype(jnp.int32), axis=1)
    row_seg = jnp.sum((rows[:, None] >= ends[None, :]).astype(jnp.int32), axis=1)
    gap = position[None, :] - rows[:, None]
    inside = (row_seg[:, None] == segment[None, :]) & (gap >= 0)
    powers = jnp.power(jnp.float32(TRACE_DECAY), jnp.maximum(gap, 0).astype(f32))
    return jnp.sum(jnp.where(inside, powers, 0.0) * delta[None, :], axis=1)


def pieces(x, count):
    out = []
    for _ in range(count):
        top = lax.reduce_precision(x, 8, 7)
        out.append(top)
        x = x - top
    return out


def kernel_params():
    return pltpu.CompilerParams(vmem_limit_bytes=16 * 1024 * 1024)


NT = (((1,), (1,)), ((), ()))


def forward_kernel(half_ref, hidden_ref, own_ref, other_ref, out_ref):
    rows = hidden_ref[...].reshape(out_ref.shape[0], hidden_ref.shape[-1])
    width = own_ref.shape[1]
    for i, w_ref in enumerate((own_ref, other_ref)):
        product = jnp.dot(rows, w_ref[...], preferred_element_type=f32)
        out_ref[:, i * width : (i + 1) * width] = product.astype(out_ref.dtype)


def forward(hidden, own_weight, other_weight, half, dtype):
    count, rows, units = hidden.shape
    width = own_weight.shape[1]
    tokens = count // 2 * rows
    whole = pl.BlockSpec((units, width), lambda i, half: (0, 0))
    return pl.pallas_call(
        forward_kernel,
        grid_spec=pltpu.PrefetchScalarGridSpec(
            num_scalar_prefetch=1,
            grid=(1,),
            in_specs=[
                pl.BlockSpec((count // 2, 1, rows, units), lambda i, half: (0, half[0], 0, 0)),
                whole,
                whole,
            ],
            out_specs=pl.BlockSpec((tokens, 2 * width), lambda i, half: (0, 0)),
        ),
        out_shape=jax.ShapeDtypeStruct((tokens, 2 * width), dtype),
        compiler_params=kernel_params(),
        cost_estimate=pl.CostEstimate(
            flops=4 * tokens * units * width, bytes_accessed=4 * units * width, transcendentals=0
        ),
        name="forward",
    )(half.reshape(1), hidden.reshape(count // 2, 2, rows, units), own_weight, other_weight)


def back_kernel(combined_ref, own_ref, other_ref, scale_ref, base_ref, out_ref, rows_ref):
    step = pl.program_id(0)
    last = pl.num_programs(0) - 1
    width = own_ref.shape[1]
    peers, rows, lanes = out_ref.shape
    tail = own_ref.shape[0] - 3 * lanes

    def product(start, size):
        total = lax.dot_general(
            combined_ref[:, :width], own_ref[pl.ds(start, size), :], NT, preferred_element_type=f32
        ) + lax.dot_general(
            combined_ref[:, width:], other_ref[pl.ds(start, size), :], NT, preferred_element_type=f32
        )
        return total.astype(bf16).reshape(peers, rows, size)

    @pl.when(step < last)
    def _():
        out_ref[...] = product(pl.multiple_of(step * lanes, lanes), lanes)

    @pl.when(step == last)
    def _():
        out_ref[:, :, :tail] = product(3 * lanes, tail)
        both = combined_ref[...]
        wide = both.astype(f32)
        square = wide * wide
        top = square.astype(bf16)
        rest = (square - top.astype(f32)).astype(bf16)
        ones = jnp.ones((16, both.shape[1]), bf16)
        squares = lax.dot_general(ones, top, NT, preferred_element_type=f32)
        squares += lax.dot_general(ones, rest, NT, preferred_element_type=f32)
        products = lax.dot_general(scale_ref[...], both, NT, preferred_element_type=f32)
        place = 0
        for line in (squares[0:1], jnp.sum(products, axis=0, keepdims=True)):
            top = line.astype(bf16).astype(f32)
            for part in (top, line - top):
                for i in range(4):
                    rows_ref[place : place + 1, :] = part[:, i * 128 : (i + 1) * 128]
                    place += 1
        out_ref[:, :, tail:] = jnp.broadcast_to(base_ref[...][None], (peers, rows, lanes - tail))
        sums = rows_ref[...].astype(bf16)
        out_ref[:, 0:16, tail : tail + 128] = jnp.broadcast_to(sums[None], (peers, 16, 128))


def back(combined, own_weight, other_weight, scale_rows, base, peers):
    tokens, chip = combined.shape
    units, width = own_weight.shape
    rows, extra = base.shape
    lanes = (units + extra) // 4
    full = lambda a: pl.BlockSpec(a.shape, lambda j: (0, 0))
    return pl.pallas_call(
        back_kernel,
        grid=(4,),
        in_specs=[full(a) for a in (combined, own_weight, other_weight, scale_rows, base)],
        out_specs=pl.BlockSpec((peers, rows, lanes), lambda j: (0, 0, j)),
        out_shape=jax.ShapeDtypeStruct((peers, rows, units + extra), bf16),
        scratch_shapes=[pltpu.VMEM((16, 128), f32)],
        compiler_params=kernel_params(),
        cost_estimate=pl.CostEstimate(
            flops=4 * tokens * units * width, bytes_accessed=8 * units * width, transcendentals=0
        ),
        name="back",
    )(combined, own_weight, other_weight, scale_rows, base)


def token_kernel(spot_ref, arrived_ref, old_ref, returns_ref, combined_ref, grad_ref, pack_ref, up_ref):
    spot = spot_ref[0]
    peers, rows, lanes = arrived_ref.shape
    units = grad_ref.shape[1]

    def total(start, size):
        out = arrived_ref[0, :, start : start + size].astype(f32)
        for p in range(1, peers):
            out += arrived_ref[p, :, start : start + size].astype(f32)
        return out

    left = total(units, 128)
    right = total(units + 128, 128)
    square_sum = left[0:4] + left[4:8]
    product_sum = left[8:12] + left[12:16]
    old, returns = old_ref[...], returns_ref[...]
    rinv = lax.rsqrt(square_sum / D + EPSILON)
    values = rinv * product_sum
    squash = jnp.tanh((values - old) / CLIP_RANGE)
    clipped = old + CLIP_RANGE * squash
    first = (values - returns) ** 2
    second = (clipped - returns) ** 2
    loss = 0.25 * jnp.sum(first + second)
    dvalue = 0.5 * (values - returns) + 0.5 * (clipped - returns) * (1.0 - squash * squash)
    up = dvalue * rinv
    down = up * rinv * values / D
    pack_ref[0:4, :] = up
    pack_ref[4:8, :] = down
    pack_ref[12:16, :] = jnp.full((4, 128), loss, f32)

    up_ref[...] = jnp.zeros_like(up_ref)
    rest = up
    for i in range(3):
        top = rest.astype(bf16).astype(f32)
        rest = rest - top
        for r in range(4):
            up_ref[i : i + 1, r * 128 : (r + 1) * 128] = top[r : r + 1, :]
    head = jnp.dot(up_ref[...].astype(bf16), combined_ref[...], preferred_element_type=f32)
    head = jnp.sum(head, axis=0, keepdims=True)
    for r in range(4):
        pack_ref[8 + r : 9 + r, :] = head[:, r * 128 : (r + 1) * 128]

    which = lax.broadcasted_iota(jnp.int32, (4, 128), 0) == spot // 4
    lane = lax.broadcasted_iota(jnp.int32, (rows, 128), 1)
    sub = lax.broadcasted_iota(jnp.int32, (rows, 128), 0)
    pick = lane == sub + lax.rem(spot, 4) * rows

    def column(x):
        line = jnp.sum(jnp.where(which, x, 0.0), axis=0, keepdims=True)
        return jnp.sum(jnp.where(pick, line, 0.0), axis=1, keepdims=True)

    own_up, own_down = column(up), column(down)
    scale_back = left[16:32] + right[0:16]
    for k in range(units // 128):
        part = own_up * scale_back[k : k + 1, :] - own_down * total(k * 128, 128)
        grad_ref[:, k * 128 : (k + 1) * 128] = part.astype(bf16)


def token_terms(spot, arrived, old, returns, combined, units):
    full = lambda a: pl.BlockSpec(a.shape, lambda i, s: (0,) * a.ndim)
    grad = jax.ShapeDtypeStruct((arrived.shape[1], units), bf16)
    pack = jax.ShapeDtypeStruct((16, 128), f32)
    return pl.pallas_call(
        token_kernel,
        grid_spec=pltpu.PrefetchScalarGridSpec(
            num_scalar_prefetch=1,
            grid=(1,),
            in_specs=[full(a) for a in (arrived, old, returns, combined)],
            out_specs=[full(grad), full(pack)],
            scratch_shapes=[pltpu.VMEM((16, combined.shape[0]), f32)],
        ),
        out_shape=[grad, pack],
        compiler_params=kernel_params(),
        cost_estimate=pl.CostEstimate(
            flops=4 * arrived.size, bytes_accessed=2 * arrived.size, transcendentals=0
        ),
        name="token_terms",
    )(spot.reshape(1), arrived, old, returns, combined)


def weight_kernel(
    own_hidden_ref, other_hidden_ref, own_pack_ref, other_pack_ref, own_ref, other_ref, scale_ref,
    out_ref, rows_ref,
):
    tokens, width = own_ref.shape

    @pl.when(pl.program_id(0) == 0)
    def _():
        for s, (pack_ref, part_ref) in enumerate(
            ((own_pack_ref, own_ref), (other_pack_ref, other_ref))
        ):
            for r in range(tokens // 128):
                up = jnp.transpose(jnp.broadcast_to(pack_ref[r : r + 1, :], (128, 128)))
                down = jnp.transpose(jnp.broadcast_to(pack_ref[4 + r : 5 + r, :], (128, 128)))
                for h in range(width // 128):
                    cut = slice(h * 128, (h + 1) * 128)
                    part = part_ref[r * 128 : (r + 1) * 128, cut].astype(f32)
                    line = up * scale_ref[0:1, cut] - down * part
                    rows_ref[s * tokens + r * 128 : s * tokens + (r + 1) * 128, cut] = line.astype(bf16)

    out_ref[...] = jnp.dot(
        own_hidden_ref[...], rows_ref[:tokens, :], preferred_element_type=f32
    ) + jnp.dot(other_hidden_ref[...], rows_ref[tokens:, :], preferred_element_type=f32)


def weight_gradient(own_hidden, other_hidden, own_pack, other_pack, own, other, scale):
    units, tokens = own_hidden.shape
    width = own.shape[1]
    block = 256
    full = lambda a: pl.BlockSpec(a.shape, lambda i: (0, 0))
    strip = pl.BlockSpec((block, tokens), lambda i: (i, 0))
    return pl.pallas_call(
        weight_kernel,
        grid=(units // block,),
        in_specs=[strip, strip] + [full(a) for a in (own_pack, other_pack, own, other, scale)],
        out_specs=pl.BlockSpec((block, width), lambda i: (i, 0)),
        out_shape=jax.ShapeDtypeStruct((units, width), f32),
        scratch_shapes=[pltpu.VMEM((2 * tokens, width), bf16)],
        compiler_params=kernel_params(),
        cost_estimate=pl.CostEstimate(
            flops=4 * units * tokens * width, bytes_accessed=8 * units * width, transcendentals=0
        ),
        name="weight_gradient",
    )(own_hidden, other_hidden, own_pack, other_pack, own, other, scale)


def neighbours():
    pairs = [(z, z ^ 1) for z in range(16)]
    return pairs + [(16 + z, 16 + (z + (1 if z % 2 else -1)) % 16) for z in range(16)]


def on_device(
    hidden_act,
    down_weight,
    residual,
    head_weight,
    gain,
    behavior,
    frozen,
    old_values,
    judge_ratings,
    lengths,
):
    yh, core = lax.axis_index("yh"), lax.axis_index("core")
    parity = lax.axis_index("zl")
    z = 2 * lax.axis_index("zh") + parity
    spot = lax.axis_index(PLANE)
    rows_each, units = hidden_act.shape
    width = down_weight.shape[1]
    chip = 2 * width
    group = 16 * rows_each
    section_rows = 8 * rows_each

    spread = jnp.broadcast_to(hidden_act[None], (16, rows_each, units))
    hidden = lax.all_to_all(spread, PLANE, 0, 0, tiled=True)
    other_weight = lax.ppermute(down_weight, "core", SWAP)

    chip_scale = lax.dynamic_slice_in_dim(gain * head_weight, yh * chip, chip, 0)
    own_scale = lax.dynamic_slice_in_dim(chip_scale, core * width, width, 0)
    other_scale = lax.dynamic_slice_in_dim(chip_scale, (1 - core) * width, width, 0)
    scale = jnp.concatenate([own_scale, other_scale])

    kept = lax.dynamic_slice_in_dim(residual, z % 8 * rows_each, rows_each, 0)
    sent = lax.dynamic_slice_in_dim(kept, (1 - yh) * chip, chip, 1)
    mine = lax.dynamic_slice_in_dim(kept, yh * chip, chip, 1)
    stream = jnp.where(yh == z // 8, mine, lax.ppermute(sent, "yh", SWAP))
    left, right = stream[:, :width], stream[:, width:]
    stream = jnp.concatenate(
        [jnp.where(core == 0, left, right), jnp.where(core == 0, right, left)], axis=1
    )

    away = forward(hidden, down_weight, other_weight, 1 - parity, bf16)
    near = lax.ppermute(away, ("core", "zh", "zl"), neighbours())
    kept_half = forward(hidden, down_weight, other_weight, parity, f32)
    pair = (kept_half + near.astype(f32)).astype(bf16)
    parts = lax.all_to_all(pair.reshape(8, rows_each, chip), "zh", 0, 0, tiled=True)
    combined = (jnp.sum(parts.astype(f32), axis=0) + stream.astype(f32)).astype(bf16)
    combined = lax.all_gather(combined, ("zh", "zl"), axis=0, tiled=True)
    own_columns, other_columns = combined[:, :width], combined[:, width:]

    hidden_t = lax.optimization_barrier(jnp.transpose(hidden.reshape(group, units)))
    other_hidden_t = lax.ppermute(hidden_t, "core", SWAP)
    scale_rows = jnp.pad(jnp.stack(pieces(scale, 3)), ((0, 13), (0, 0))).astype(bf16)
    scale_back = lax.dot_general(
        scale_rows[:, :width], down_weight, NT, preferred_element_type=f32
    ) + lax.dot_general(scale_rows[:, width:], other_weight, NT, preferred_element_type=f32)
    high, low = pieces(jnp.sum(scale_back, axis=0).reshape(-1, 128), 2)
    base = jnp.concatenate(
        [jnp.pad(high, ((16, 16 - high.shape[0]), (0, 0))), jnp.pad(low, ((0, 32 - low.shape[0]), (0, 0)))],
        axis=1,
    ).astype(bf16)

    payload = back(combined, down_weight, other_weight, scale_rows, base, 16)
    arrived = lax.all_to_all(payload, PLANE, 0, 0, tiled=True)

    slot = jnp.arange(group, dtype=jnp.int32)
    token = slot + section_rows * (slot // section_rows + core)
    own_old = jnp.concatenate(
        [
            lax.dynamic_slice_in_dim(old_values, core * section_rows, section_rows, 0),
            lax.dynamic_slice_in_dim(old_values, (2 + core) * section_rows, section_rows, 0),
        ]
    )
    returns = own_old + returns_of(behavior, frozen, old_values, judge_ratings, lengths, token)
    hidden_grad, pack = token_terms(
        spot, arrived, own_old.reshape(4, 128), returns.reshape(4, 128), combined, units
    )
    other_pack = lax.ppermute(pack, "core", SWAP)
    total_loss = pack[12, 0] + other_pack[12, 0]
    own_head = pack[8:10] + other_pack[10:12]
    other_head = pack[10:12] + other_pack[8:10]
    head_chip = jnp.concatenate(
        [jnp.where(core == 0, own_head, other_head), jnp.where(core == 0, other_head, own_head)]
    )
    head_far = lax.ppermute(head_chip, "yh", SWAP)
    head_sum = jnp.concatenate(
        [jnp.where(yh == 0, head_chip, head_far), jnp.where(yh == 0, head_far, head_chip)]
    )
    head_grad = gain * head_sum.reshape(-1)

    weight_grad = weight_gradient(
        hidden_t,
        other_hidden_t,
        pack,
        other_pack,
        own_columns,
        lax.ppermute(other_columns, "core", SWAP),
        own_scale.reshape(1, -1),
    )
    return (total_loss, head_grad, weight_grad, hidden_grad)


def solution(mesh):
    axes = ("yh", "core", "x", "yl", "zh", "zl")
    fine = Mesh(mesh.devices.reshape(2, 2, 4, 2, 8, 2), axes)
    tp = ("zh", "zl")
    in_specs = (
        P(("yh", "core", "x", "yl"), tp),
        P(tp, ("x", "yl", "yh", "core")),
        P(("yh", "core"), ("x", "yl")),
        P(("x", "yl")),
        P(("x", "yl")),
        P(),
        P(),
        P(),
        P(),
        P(),
    )
    out_specs = (
        P(),
        P(("x", "yl")),
        P(tp, ("x", "yl", "yh", "core")),
        P(("yh", "core", "x", "yl"), tp),
    )
    return jax.shard_map(
        on_device, mesh=fine, in_specs=in_specs, out_specs=out_specs, check_vma=False
    )
```

time: 168 us -> 170 us (1.012)
  Pallas kernels: 0 us -> 16.3 us
  matrix products: 11.3 us -> 1.94 us
  starting transfers between devices: 73.2 us -> 79.8 us
  other arithmetic: 10 us -> 4.19 us
  waiting for transfers between devices: 33.3 us -> 28.9 us
  blocking collectives: 28 us -> 23.8 us
  local copies, waits for them, and re-layouts: 7.91 us -> 9.73 us
    ppermute x4 -> x5, starting transfers between devices: 34.3 us -> 51.8 us  [the longest x1 16.7 us: on_device(): other_pack = lax.ppermute(pack, 'core', SWAP)]
    pallas_call x0 -> x5, Pallas kernels: none -> 16.3 us  [the longest x1 6.42 us: weight_gradient(): pl.pallas_call(weight_kernel, grid=(units // block,), in_specs=[strip, st...]
    all_to_all x2, starting transfers between devices: 27.3 us -> 16 us  [the longest x1 8.26 us: on_device(): lax.all_to_all(pair.reshape(8, rows_each, chip), 'zh', 0, 0, tiled=True)]
    dot_general x5 -> x2, matrix products: 11.3 us -> 1.94 us  [the longest x1 1.57 us: on_device(): lax.dot_general(scale_rows[:, width:], other_weight, NT, preferred_elemen...]
    all_to_all x2, waiting for transfers between devices: 31.1 us -> 26.8 us  [the longest x1 14.7 us: on_device(): lax.all_to_all(pair.reshape(8, rows_each, chip), 'zh', 0, 0, tiled=True)]
    all_gather x1, blocking collectives: 28 us -> 23.8 us  [on_device(): combined = lax.all_gather(combined, ('zh', 'zl'), axis=0, tiled=True)]
    reshape x0 -> x1, local copies, waits for them, and re-layouts: none -> 2.32 us  [on_device(): hidden.reshape(group, units)]
    ppermute x1, waiting for transfers between devices: 2.2 us -> 0.01 us  [on_device(): other_weight = lax.ppermute(down_weight, 'core', SWAP)]
  transfers between devices with their start and end apart: 9 -> 10, of which waited for: 3 -> 4; matrix products, arithmetic and copies ran while one was open for 9% -> 6% of each run, Pallas kernels for 0% -> 8%
where the time goes in v2:
time: 170 us; the launch traced here: 168 us
  starting transfers between devices  79.8 us (47%)
  waiting for transfers between devices  28.9 us (17%)
  blocking collectives  23.8 us (14%)
  Pallas kernels  16.3 us (10%)
  local copies, waits for them, and re-layouts  9.73 us (6%)
  other arithmetic  4.19 us (2%)
  between operations  3.47 us (2%)
  matrix products  1.94 us (1%)
    all_gather x1, blocking collectives, on_device(): combined = lax.all_gather(combined, ('zh', 'zl'), axis=0, tiled=True)  23.8 us
    ppermute x1, starting transfers between devices, on_device(): other_pack = lax.ppermute(pack, 'core', SWAP)  16.7 us
    ppermute x1, starting transfers between devices, on_device(): near = lax.ppermute(away, ('core', 'zh', 'zl'), neighbours())  15.8 us
    all_to_all x1, waiting for transfers between devices, on_device(): lax.all_to_all(pair.reshape(8, rows_each, chip), 'zh', 0, 0, tiled=True)  14.7 us
    ppermute x1, starting transfers between devices, on_device(): other_hidden_t = lax.ppermute(hidden_t, 'core', SWAP)  12.4 us
    all_to_all x1, waiting for transfers between devices, on_device(): hidden = lax.all_to_all(spread, PLANE, 0, 0, tiled=True)  12.1 us
    all_to_all x1, starting transfers between devices, on_device(): lax.all_to_all(pair.reshape(8, rows_each, chip), 'zh', 0, 0, tiled=True)  8.26 us
    all_to_all x1, starting transfers between devices, on_device(): hidden = lax.all_to_all(spread, PLANE, 0, 0, tiled=True)  7.72 us
  transfers between devices with their start and end apart: 10, of which 4 were waited for; matrix products, arithmetic and copies ran while one was open for 6% of the time, Pallas kernels for 8%

profile of v2, /device:TPU:1, one launch (start us, length us, event | category | flops | bytes accessed | tf_op | source)
XLA Modules:
  0.0 168.2 jit_solution(7991653763849986962)
XLA Ops:
  0.6 2.3 %broadcast_in_dim.21 = bf16[16,32,1792]{2,1,0:T(8,128)(2,1)} broadcast(bf16[32,1792]{1,0:T(8,128)(2,1)} %param.10), dimensions={1,2} | broadcast | bytes 1949696 | tf_op jit(solution)/shard_map/broadcast_in_dim | solution.py:304
  3.0 7.7 %all-to-all-start = ((bf16[16,32,1792]{2,1,0:T(8,128)(2,1)}), bf16[16,32,1792]{2,1,0:T(8,128)(2,1)S(1)}, u32[]{:S(2)}, u32[]{:S(2)}) async-start(bf16[16,32,1792]{2,1,0:T(8,128)(2,1)} %broadcast_in_dim.21), calls=%async_computation | async-start | bytes 3670016 | tf_op jit(solution)/shard_map/all_to_all | solution.py:305
  10.7 4.9 %collective-permute-start = (bf16[1792,256]{1,0:T(8,128)(2,1)S(1)}, bf16[1792,256]{1,0:T(8,128)(2,1)}, u32[]{:S(2)}, u32[]{:S(2)}) collective-permute-start(bf16[1792,256]{1,0:T(8,128)(2,1)S(1)} %copy-done), channel_id=1, source_target_pairs={{0,128},{128,0},{1,129},{129,1},{2,130},{130,2},{3,131},{131,3},{4... | collective-permute-start | bytes 2752520 | tf_op jit(solution)/shard_map/ppermute | solution.py:306
  16.5 5.0 %collective-permute-start.2 = (bf16[32,512]{1,0:T(8,128)(2,1)S(1)}, bf16[32,512]{1,0:T(8,128)(2,1)S(1)}, u32[]{:S(2)}, u32[]{:S(2)}) collective-permute-start(bf16[32,512]{1,0:T(8,128)(2,1)S(1)} %dynamic_slice.25), channel_id=1, source_target_pairs={{0,256},{256,0},{1,257},{257,1},{2,258},{258,2},{3,259},{259,3},{4... | collective-permute-start | bytes 98312 | tf_op jit(solution)/shard_map/ppermute | solution.py:316
  21.7 12.1 %all-to-all-done = bf16[16,32,1792]{2,1,0:T(8,128)(2,1)S(1)} async-done(((bf16[16,32,1792]{2,1,0:T(8,128)(2,1)}), bf16[16,32,1792]{2,1,0:T(8,128)(2,1)S(1)}, u32[]{:S(2)}, u32[]{:S(2)}) %all-to-all-start) | async-done | bytes 1835040 | tf_op jit(solution)/shard_map/all_to_all | solution.py:305
  33.9 1.9 %forward.3 = bf16[256,512]{1,0:T(8,128)(2,1)S(1)} custom-call(s32[1]{0:T(128)} %bitcast.3.half_ref, bf16[8,2,32,1792]{3,2,1,0:T(8,128)(2,1)S(1)} %bitcast.26, bf16[1792,256]{1,0:T(8,128)(2,1)S(1)} %copy-done, bf16[1792,256]{1,0:T(8,128)(2,1)} %collective-permute-done.other_ref), custom_call_target="tpu_custom_call" | custom-call | flops 469762048 | bytes 1835008 | tf_op jit(solution)/shard_map/forward/pallas_call | solution.py:66
  35.7 15.8 %collective-permute-start.1 = (bf16[256,512]{1,0:T(8,128)(2,1)S(1)}, bf16[256,512]{1,0:T(8,128)(2,1)S(1)}, u32[]{:S(2)}, u32[]{:S(2)}) collective-permute-start(bf16[256,512]{1,0:T(8,128)(2,1)S(1)} %forward.3), channel_id=1, source_target_pairs={{0,1},{1,0},{2,3},{3,2},{4,5},{5,4},{6,7},{7,6},{8,9},{9,8},{10,11... | collective-permute-start | bytes 786440 | tf_op jit(solution)/shard_map/ppermute | solution.py:323
  51.9 1.9 %forward.2 = f32[256,512]{1,0:T(8,128)S(1)} custom-call(s32[1]{0:T(128)} %bitcast.1.half_ref, bf16[8,2,32,1792]{3,2,1,0:T(8,128)(2,1)S(1)} %bitcast.27, bf16[1792,256]{1,0:T(8,128)(2,1)S(1)} %copy-done, bf16[1792,256]{1,0:T(8,128)(2,1)} %collective-permute-done.other_ref), custom_call_target="tpu_custom_call" | custom-call | flops 469762048 | bytes 1835008 | tf_op jit(solution)/shard_map/forward/pallas_call | solution.py:66
  53.8 1.5 collective-permute-done.1
  56.0 8.3 %all-to-all-start.1 = ((bf16[8,32,512]{2,1,0:T(8,128)(2,1)}), bf16[8,32,512]{2,1,0:T(8,128)(2,1)S(1)}, u32[]{:S(2)}, u32[]{:S(2)}) async-start(bf16[8,32,512]{2,1,0:T(8,128)(2,1)} %bitcast.4), calls=%async_computation.1 | async-start | bytes 524288 | tf_op jit(solution)/shard_map/all_to_all | solution.py:326
  65.2 1.6 fusion.2
  66.8 14.7 %all-to-all-done.1 = bf16[8,32,512]{2,1,0:T(8,128)(2,1)S(1)} async-done(((bf16[8,32,512]{2,1,0:T(8,128)(2,1)}), bf16[8,32,512]{2,1,0:T(8,128)(2,1)S(1)}, u32[]{:S(2)}, u32[]{:S(2)}) %all-to-all-start.1) | async-done | bytes 262176 | tf_op jit(solution)/shard_map/all_to_all | solution.py:326
  81.5 23.8 %all_gather.3.combined_ref = bf16[512,512]{1,0:T(8,128)(2,1)S(1)} all-gather(bf16[32,512]{1,0:T(8,128)(2,1)S(1)} %add_convert_fusion.1), channel_id=1, replica_groups=mesh['yh'=2,'core'=2,'x'=4,'yl'=2,'zh'=8,'zl'=2] {'zh','zl'}, dimensions={0}, use_global_device_ids=true | all-gather | bytes 557056 | tf_op jit(solution)/shard_map/all_gather | solution.py:328
  105.4 3.5 %back.1 = bf16[16,32,2048]{2,1,0:T(8,128)(2,1)S(1)} custom-call(bf16[512,512]{1,0:T(8,128)(2,1)S(1)} %all_gather.3.combined_ref, bf16[1792,256]{1,0:T(8,128)(2,1)S(1)} %copy-done, bf16[1792,256]{1,0:T(8,128)(2,1)} %collective-permute-done.other_ref, bf16[16,512]{1,0:T(8,128)(2,1)S(1)} %fusion.11.scale_ref, bf16[32,256]{1,0:T(8,128)(2,1)S(1)} %fusion.9.base_ref), custom_call_target="tpu_custom_call" | custom-call | flops 939524096 | bytes 3670016 | tf_op jit(solution)/shard_map/back/pallas_call | solution.py:136
  108.9 1.3 copy-done.1
  110.2 4.6 %all-to-all-start.2 = ((bf16[16,32,2048]{2,1,0:T(8,128)(2,1)}), bf16[16,32,2048]{2,1,0:T(8,128)(2,1)}, u32[]{:S(2)}, u32[]{:S(2)}) async-start(bf16[16,32,2048]{2,1,0:T(8,128)(2,1)} %copy-done.1), calls=%async_computation.2 | async-start | bytes 4194304 | tf_op jit(solution)/shard_map/all_to_all | solution.py:344
  115.3 2.3 %copy.20 = bf16[512,1792]{0,1:T(8,128)(2,1)} copy(bf16[512,1792]{1,0:T(8,128)(2,1)S(1)} %bitcast.28) | data formatting | bytes 3670016 | tf_op jit(solution)/shard_map/reshape | solution.py:331
  117.7 12.4 %collective-permute-start.5 = (bf16[1792,512]{1,0:T(8,128)(2,1)}, bf16[1792,512]{1,0:T(8,128)(2,1)}, u32[]{:S(2)}, u32[]{:S(2)}) collective-permute-start(bf16[1792,512]{1,0:T(8,128)(2,1)} %bitcast.29), channel_id=1, source_target_pairs={{0,128},{128,0},{1,129},{129,1},{2,130},{130,2},{3,131},{131,3},{4... | collective-permute-start | bytes 5505032 | tf_op jit(solution)/shard_map/ppermute | solution.py:332
  132.2 2.6 %token_terms.1 = (bf16[32,1792]{1,0:T(8,128)(2,1)}, f32[16,128]{1,0:T(8,128)S(1)}) custom-call(s32[1]{0:T(128)} %bitcast.spot_ref, bf16[16,32,2048]{2,1,0:T(8,128)(2,1)} %all-to-all-done.2.arrived_ref, f32[4,128]{1,0:T(4,128)S(1)} %get-tuple-element.23.old_ref, f32[4,128]{1,0:T(4,128)S(1)} %get-tuple-element.22.returns_ref, ...), custom_call_target="tpu_custom_call" | custom-call | flops 4194304 | bytes 2097152 | tf_op jit(solution)/shard_map/token_terms/pallas_call | solution.py:213
  134.8 16.7 %collective-permute-start.3 = (f32[16,128]{1,0:T(8,128)S(1)}, f32[16,128]{1,0:T(8,128)S(1)}, u32[]{:S(2)}, u32[]{:S(2)}) collective-permute-start(f32[16,128]{1,0:T(8,128)S(1)} %get-tuple-element.6.own_pack_ref), channel_id=1, source_target_pairs={{0,128},{128,0},{1,129},{129,1},{2,130},{130,2},{3,131},{131,3},{4... | collective-permute-start | bytes 24584 | tf_op jit(solution)/shard_map/ppermute | solution.py:358
  151.6 1.9 %collective-permute-start.6 = (bf16[512,256]{1,0:T(8,128)(2,1)S(1)}, bf16[512,256]{1,0:T(8,128)(2,1)S(1)}, u32[]{:S(2)}, u32[]{:S(2)}) collective-permute-start(bf16[512,256]{1,0:T(8,128)(2,1)S(1)} %get-tuple-element.8), channel_id=1, source_target_pairs={{0,128},{128,0},{1,129},{129,1},{2,130},{130,2},{3,131},{131,3},{4... | collective-permute-start | bytes 786440 | tf_op jit(solution)/shard_map/ppermute | solution.py:377
  154.0 2.6 %collective-permute-start.4 = (f32[4,128]{1,0:T(4,128)S(1)}, f32[4,128]{1,0:T(4,128)S(1)}, u32[]{:S(2)}, u32[]{:S(2)}) collective-permute-start(f32[4,128]{1,0:T(4,128)S(1)} %pad_maximum_fusion.2), channel_id=1, source_target_pairs={{0,256},{256,0},{1,257},{257,1},{2,258},{258,2},{3,259},{259,3},{4... | collective-permute-start | bytes 6152 | tf_op jit(solution)/shard_map/ppermute | solution.py:365
  156.7 1.5 copy-done.2
  158.2 6.4 %weight_gradient.1 = f32[1792,256]{1,0:T(8,128)} custom-call(bf16[1792,512]{1,0:T(8,128)(2,1)S(1)} %bitcast.30, bf16[1792,512]{1,0:T(8,128)(2,1)} %collective-permute-done.5.other_hidden_ref, f32[16,128]{1,0:T(8,128)S(1)} %get-tuple-element.6.own_pack_ref, f32[16,128]{1,0:T(8,128)S(1)} %collective-permute-done.3.other_pack_ref, ...), custom_call_target="tpu_custom_call" | custom-call | flops 939524096 | bytes 3670016 | tf_op jit(solution)/shard_map/weight_gradient/pallas_call | solution.py:262
  (59 shorter events, 7.5 us)
Async XLA Ops:
  2.9 7.7 %copy-start = (bf16[1792,256]{1,0:T(8,128)(2,1)S(1)}, bf16[1792,256]{1,0:T(8,128)(2,1)}, u32[]{:S(2)}) copy-start(bf16[1792,256]{1,0:T(8,128)(2,1)} %own_ref.5) | copy-start | bytes 2752516
  2.9 18.6 %copy-start.4 = (f32[1024]{0:T(1024)S(1)}, f32[1024]{0:T(1024)}, u32[]{:S(2)}) copy-start(f32[1024]{0:T(1024)} %param.14) | copy-start | bytes 12292
  3.0 18.6 %copy-start.5 = (f32[1024]{0:T(1024)S(1)}, f32[1024]{0:T(1024)}, u32[]{:S(2)}) copy-start(f32[1024]{0:T(1024)} %param.13) | copy-start | bytes 12292
  3.0 30.9 %all-to-all-start = ((bf16[16,32,1792]{2,1,0:T(8,128)(2,1)}), bf16[16,32,1792]{2,1,0:T(8,128)(2,1)S(1)}, u32[]{:S(2)}, u32[]{:S(2)}) async-start(bf16[16,32,1792]{2,1,0:T(8,128)(2,1)} %broadcast_in_dim.21), calls=%async_computation | async-start | bytes 3670016 | tf_op jit(solution)/shard_map/all_to_all | solution.py:305
  10.7 11.0 %collective-permute-start = (bf16[1792,256]{1,0:T(8,128)(2,1)S(1)}, bf16[1792,256]{1,0:T(8,128)(2,1)}, u32[]{:S(2)}, u32[]{:S(2)}) collective-permute-start(bf16[1792,256]{1,0:T(8,128)(2,1)S(1)} %copy-done), channel_id=1, source_target_pairs={{0,128},{128,0},{1,129},{129,1},{2,130},{130,2},{3,131},{131,3},{4... | collective-permute-start | bytes 2752520 | tf_op jit(solution)/shard_map/ppermute | solution.py:306
  16.5 47.8 %collective-permute-start.2 = (bf16[32,512]{1,0:T(8,128)(2,1)S(1)}, bf16[32,512]{1,0:T(8,128)(2,1)S(1)}, u32[]{:S(2)}, u32[]{:S(2)}) collective-permute-start(bf16[32,512]{1,0:T(8,128)(2,1)S(1)} %dynamic_slice.25), channel_id=1, source_target_pairs={{0,256},{256,0},{1,257},{257,1},{2,258},{258,2},{3,259},{259,3},{4... | collective-permute-start | bytes 98312 | tf_op jit(solution)/shard_map/ppermute | solution.py:316
  35.7 19.5 %collective-permute-start.1 = (bf16[256,512]{1,0:T(8,128)(2,1)S(1)}, bf16[256,512]{1,0:T(8,128)(2,1)S(1)}, u32[]{:S(2)}, u32[]{:S(2)}) collective-permute-start(bf16[256,512]{1,0:T(8,128)(2,1)S(1)} %forward.3), channel_id=1, source_target_pairs={{0,1},{1,0},{2,3},{3,2},{4,5},{5,4},{6,7},{7,6},{8,9},{9,8},{10,11... | collective-permute-start | bytes 786440 | tf_op jit(solution)/shard_map/ppermute | solution.py:323
  56.0 25.5 %all-to-all-start.1 = ((bf16[8,32,512]{2,1,0:T(8,128)(2,1)}), bf16[8,32,512]{2,1,0:T(8,128)(2,1)S(1)}, u32[]{:S(2)}, u32[]{:S(2)}) async-start(bf16[8,32,512]{2,1,0:T(8,128)(2,1)} %bitcast.4), calls=%async_computation.1 | async-start | bytes 524288 | tf_op jit(solution)/shard_map/all_to_all | solution.py:326
  108.9 1.3 copy-start.1
  110.2 4.6 %copy-start.8 = (s32[16]{0:T(128)S(1)}, s32[16]{0:T(128)}, u32[]{:S(2)}) copy-start(s32[16]{0:T(128)} %param.19) | copy-start | bytes 196
  110.2 4.9 %copy-start.3 = (f32[1024]{0:T(1024)S(1)}, f32[1024]{0:T(1024)}, u32[]{:S(2)}) copy-start(f32[1024]{0:T(1024)} %param.17) | copy-start | bytes 12292
  110.2 22.0 %all-to-all-start.2 = ((bf16[16,32,2048]{2,1,0:T(8,128)(2,1)}), bf16[16,32,2048]{2,1,0:T(8,128)(2,1)}, u32[]{:S(2)}, u32[]{:S(2)}) async-start(bf16[16,32,2048]{2,1,0:T(8,128)(2,1)} %copy-done.1), calls=%async_computation.2 | async-start | bytes 4194304 | tf_op jit(solution)/shard_map/all_to_all | solution.py:344
  114.8 15.4 %copy-start.9 = (f32[16]{0:T(128)S(1)}, f32[16]{0:T(128)}, u32[]{:S(2)}) copy-start(f32[16]{0:T(128)} %param.18) | copy-start | bytes 196
  114.8 15.5 %copy-start.6 = (f32[1024]{0:T(1024)S(1)}, f32[1024]{0:T(1024)}, u32[]{:S(2)}) copy-start(f32[1024]{0:T(1024)} %param.15) | copy-start | bytes 12292
  114.8 15.5 %copy-start.7 = (f32[1024]{0:T(1024)S(1)}, f32[1024]{0:T(1024)}, u32[]{:S(2)}) copy-start(f32[1024]{0:T(1024)} %param.16) | copy-start | bytes 12292
  117.7 39.0 %collective-permute-start.5 = (bf16[1792,512]{1,0:T(8,128)(2,1)}, bf16[1792,512]{1,0:T(8,128)(2,1)}, u32[]{:S(2)}, u32[]{:S(2)}) collective-permute-start(bf16[1792,512]{1,0:T(8,128)(2,1)} %bitcast.29), channel_id=1, source_target_pairs={{0,128},{128,0},{1,129},{129,1},{2,130},{130,2},{3,131},{131,3},{4... | collective-permute-start | bytes 5505032 | tf_op jit(solution)/shard_map/ppermute | solution.py:332
  134.8 19.2 %collective-permute-start.3 = (f32[16,128]{1,0:T(8,128)S(1)}, f32[16,128]{1,0:T(8,128)S(1)}, u32[]{:S(2)}, u32[]{:S(2)}) collective-permute-start(f32[16,128]{1,0:T(8,128)S(1)} %get-tuple-element.6.own_pack_ref), channel_id=1, source_target_pairs={{0,128},{128,0},{1,129},{129,1},{2,130},{130,2},{3,131},{131,3},{4... | collective-permute-start | bytes 24584 | tf_op jit(solution)/shard_map/ppermute | solution.py:358
  151.6 5.1 %collective-permute-start.6 = (bf16[512,256]{1,0:T(8,128)(2,1)S(1)}, bf16[512,256]{1,0:T(8,128)(2,1)S(1)}, u32[]{:S(2)}, u32[]{:S(2)}) collective-permute-start(bf16[512,256]{1,0:T(8,128)(2,1)S(1)} %get-tuple-element.8), channel_id=1, source_target_pairs={{0,128},{128,0},{1,129},{129,1},{2,130},{130,2},{3,131},{131,3},{4... | collective-permute-start | bytes 786440 | tf_op jit(solution)/shard_map/ppermute | solution.py:377
  154.0 12.4 %collective-permute-start.4 = (f32[4,128]{1,0:T(4,128)S(1)}, f32[4,128]{1,0:T(4,128)S(1)}, u32[]{:S(2)}, u32[]{:S(2)}) collective-permute-start(f32[4,128]{1,0:T(4,128)S(1)} %pad_maximum_fusion.2), channel_id=1, source_target_pairs={{0,256},{256,0},{1,257},{257,1},{2,258},{258,2},{3,259},{259,3},{4... | collective-permute-start | bytes 6152 | tf_op jit(solution)/shard_map/ppermute | solution.py:365
  156.7 1.5 copy-start.2

commit v3 on v2

v3 whole, which is shorter than its diff:
```python
import jax
import jax.numpy as jnp
from jax import lax
from jax.experimental import pallas as pl
from jax.experimental.pallas import tpu as pltpu
from jax.sharding import Mesh, PartitionSpec as P

D = 8192
KL_PENALTY_SCALE = 0.1
TRACE_DECAY = 0.95
CLIP_RANGE = 0.2
EPSILON = 1e-05

PLANE = ("yh", "x", "yl")
SWAP = [(0, 1), (1, 0)]
f32, bf16 = jnp.float32, jnp.bfloat16


def returns_of(behavior, frozen, old_values, judge_ratings, lengths, rows):
    total = behavior.shape[0]
    position = jnp.arange(total, dtype=jnp.int32)
    ends = jnp.cumsum(lengths)
    closes = position[:, None] == ends[None, :] - 1
    final = jnp.any(closes, axis=1)
    extra = jnp.sum(jnp.where(closes, judge_ratings[None, :], 0.0), axis=1)
    rewards = extra - KL_PENALTY_SCALE * (behavior - frozen)
    following = jnp.concatenate([old_values[1:], jnp.zeros_like(old_values[:1])])
    delta = rewards + jnp.where(final, 0.0, following) - old_values
    segment = jnp.sum((position[:, None] >= ends[None, :]).astype(jnp.int32), axis=1)
    row_seg = jnp.sum((rows[:, None] >= ends[None, :]).astype(jnp.int32), axis=1)
    gap = position[None, :] - rows[:, None]
    inside = (row_seg[:, None] == segment[None, :]) & (gap >= 0)
    powers = jnp.power(jnp.float32(TRACE_DECAY), jnp.maximum(gap, 0).astype(f32))
    return jnp.sum(jnp.where(inside, powers, 0.0) * delta[None, :], axis=1)


def pieces(x, count):
    out = []
    for _ in range(count):
        top = lax.reduce_precision(x, 8, 7)
        out.append(top)
        x = x - top
    return out


def kernel_params():
    return pltpu.CompilerParams(vmem_limit_bytes=16 * 1024 * 1024)


NT = (((1,), (1,)), ((), ()))
TN = (((0,), (0,)), ((), ()))
INSIDE = pl.BlockSpec(memory_space=pltpu.VMEM)


def near(*arrays):
    return [pltpu.with_memory_space_constraint(a, pltpu.VMEM) for a in arrays]


def spread_kernel(in_ref, out_ref, held_ref, sem, sems):
    first = pltpu.make_async_copy(in_ref, held_ref, sem)
    first.start()
    first.wait()
    copies = [
        pltpu.make_async_copy(held_ref, out_ref.at[i], sems.at[i]) for i in range(out_ref.shape[0])
    ]
    for copy in copies:
        copy.start()
    for copy in copies:
        copy.wait()


def spread(x, count):
    return pl.pallas_call(
        spread_kernel,
        in_specs=[pl.BlockSpec(memory_space=pl.ANY)],
        out_specs=pl.BlockSpec(memory_space=pltpu.HBM),
        out_shape=pltpu.HBM((count,) + x.shape, x.dtype),
        scratch_shapes=[
            pltpu.VMEM(x.shape, x.dtype),
            pltpu.SemaphoreType.DMA,
            pltpu.SemaphoreType.DMA((count,)),
        ],
        compiler_params=kernel_params(),
        cost_estimate=pl.CostEstimate(flops=0, bytes_accessed=2 * count * x.size, transcendentals=0),
        name="spread",
    )(x)


def forward_kernel(half_ref, hidden_ref, own_ref, other_ref, out_ref):
    half = hidden_ref[:, pl.ds(half_ref[0], 1)]
    rows = half.reshape(out_ref.shape[0], hidden_ref.shape[-1])
    width = own_ref.shape[1]
    for i, w_ref in enumerate((own_ref, other_ref)):
        product = jnp.dot(rows, w_ref[...], preferred_element_type=f32)
        out_ref[:, i * width : (i + 1) * width] = product.astype(out_ref.dtype)


def forward(hidden, own_weight, other_weight, half, dtype):
    count, rows, units = hidden.shape
    width = own_weight.shape[1]
    tokens = count // 2 * rows
    return pl.pallas_call(
        forward_kernel,
        in_specs=[pl.BlockSpec(memory_space=pltpu.SMEM)] + [INSIDE] * 3,
        out_specs=INSIDE,
        out_shape=jax.ShapeDtypeStruct((tokens, 2 * width), dtype),
        compiler_params=kernel_params(),
        cost_estimate=pl.CostEstimate(
            flops=4 * tokens * units * width, bytes_accessed=4 * units * width, transcendentals=0
        ),
        name="forward",
    )(half.reshape(1), *near(hidden.reshape(count // 2, 2, rows, units), own_weight, other_weight))


def back_kernel(combined_ref, own_ref, other_ref, scale_ref, base_ref, out_ref, held_ref, rows_ref, sems):
    width = own_ref.shape[1]
    parts, peers, rows, lanes = held_ref.shape
    units = own_ref.shape[0]
    both = combined_ref[...]

    def send(j):
        target = out_ref.at[:, :, j * lanes : (j + 1) * lanes]
        return pltpu.make_async_copy(held_ref.at[j], target, sems.at[j])

    for j in range(parts):
        start = j * lanes
        size = min(lanes, units - start)
        total = lax.dot_general(
            both[:, :width], own_ref[start : start + size, :], NT, preferred_element_type=f32
        ) + lax.dot_general(
            both[:, width:], other_ref[start : start + size, :], NT, preferred_element_type=f32
        )
        held_ref[j, :, :, :size] = total.astype(bf16).reshape(peers, rows, size)
        if j == parts - 1:
            wide = both.astype(f32)
            square = wide * wide
            top = square.astype(bf16)
            rest = (square - top.astype(f32)).astype(bf16)
            ones = jnp.ones((16, both.shape[1]), bf16)
            squares = lax.dot_general(ones, top, NT, preferred_element_type=f32)
            squares += lax.dot_general(ones, rest, NT, preferred_element_type=f32)
            products = lax.dot_general(scale_ref[...], both, NT, preferred_element_type=f32)
            place = 0
            for line in (squares[0:1], jnp.sum(products, axis=0, keepdims=True)):
                top = line.astype(bf16).astype(f32)
                for part in (top, line - top):
                    for i in range(4):
                        rows_ref[place : place + 1, :] = part[:, i * 128 : (i + 1) * 128]
                        place += 1
            sums = rows_ref[...].astype(bf16)
            held_ref[j, :, :16, size:] = jnp.broadcast_to(sums[None], (peers, 16, 128))
            held_ref[j, :, 16:, size:] = jnp.broadcast_to(base_ref[...][None], (peers, rows - 16, 128))
        send(j).start()
    for j in range(parts):
        send(j).wait()


def back(combined, own_weight, other_weight, scale_rows, base, peers):
    tokens, chip = combined.shape
    units, width = own_weight.shape
    rows, lanes, parts = 32, units + 128, 3
    return pl.pallas_call(
        back_kernel,
        in_specs=[INSIDE] * 5,
        out_specs=pl.BlockSpec(memory_space=pltpu.HBM),
        out_shape=pltpu.HBM((peers, rows, lanes), bf16),
        scratch_shapes=[
            pltpu.VMEM((parts, peers, rows, lanes // parts), bf16),
            pltpu.VMEM((16, 128), f32),
            pltpu.SemaphoreType.DMA((parts,)),
        ],
        compiler_params=kernel_params(),
        cost_estimate=pl.CostEstimate(
            flops=4 * tokens * units * width, bytes_accessed=8 * units * width, transcendentals=0
        ),
        name="back",
    )(*near(combined, own_weight, other_weight), scale_rows, base)


def token_kernel(spot_ref, arrived_ref, old_ref, returns_ref, combined_ref, grad_ref, pack_ref, up_ref):
    spot = spot_ref[0]
    peers, rows, lanes = arrived_ref.shape
    units = grad_ref.shape[1]

    def total(start, size):
        out = arrived_ref[0, :, start : start + size].astype(f32)
        for p in range(1, peers):
            out += arrived_ref[p, :, start : start + size].astype(f32)
        return out

    left = total(units, 128)
    square_sum = left[0:4] + left[4:8]
    product_sum = left[8:12] + left[12:16]
    old, returns = old_ref[...], returns_ref[...]
    rinv = lax.rsqrt(square_sum / D + EPSILON)
    values = rinv * product_sum
    squash = jnp.tanh((values - old) / CLIP_RANGE)
    clipped = old + CLIP_RANGE * squash
    first = (values - returns) ** 2
    second = (clipped - returns) ** 2
    loss = 0.25 * jnp.sum(first + second)
    dvalue = 0.5 * (values - returns) + 0.5 * (clipped - returns) * (1.0 - squash * squash)
    up = dvalue * rinv
    down = up * rinv * values / D
    pack_ref[0:4, :] = up
    pack_ref[4:8, :] = down
    pack_ref[12:16, :] = jnp.full((4, 128), loss, f32)

    up_ref[...] = jnp.zeros_like(up_ref)
    rest = up
    for i in range(3):
        top = rest.astype(bf16).astype(f32)
        rest = rest - top
        for r in range(4):
            up_ref[i : i + 1, r * 128 : (r + 1) * 128] = top[r : r + 1, :]
    head = jnp.dot(up_ref[...].astype(bf16), combined_ref[...], preferred_element_type=f32)
    head = jnp.sum(head, axis=0, keepdims=True)
    for r in range(4):
        pack_ref[8 + r : 9 + r, :] = head[:, r * 128 : (r + 1) * 128]

    which = lax.broadcasted_iota(jnp.int32, (4, 128), 0) == spot // 4
    lane = lax.broadcasted_iota(jnp.int32, (rows, 128), 1)
    sub = lax.broadcasted_iota(jnp.int32, (rows, 128), 0)
    pick = lane == sub + lax.rem(spot, 4) * rows

    def column(x):
        line = jnp.sum(jnp.where(which, x, 0.0), axis=0, keepdims=True)
        return jnp.sum(jnp.where(pick, line, 0.0), axis=1, keepdims=True)

    own_up, own_down = column(up), column(down)
    scale_back = left[16:32]
    for k in range(units // 128):
        part = own_up * scale_back[k : k + 1, :] - own_down * total(k * 128, 128)
        grad_ref[:, k * 128 : (k + 1) * 128] = part.astype(bf16)


def token_terms(spot, arrived, old, returns, combined, units):
    full = lambda a: pl.BlockSpec(a.shape, lambda i, s: (0,) * a.ndim)
    grad = jax.ShapeDtypeStruct((arrived.shape[1], units), bf16)
    pack = jax.ShapeDtypeStruct((16, 128), f32)
    return pl.pallas_call(
        token_kernel,
        grid_spec=pltpu.PrefetchScalarGridSpec(
            num_scalar_prefetch=1,
            grid=(1,),
            in_specs=[INSIDE] * 4,
            out_specs=[full(grad), full(pack)],
            scratch_shapes=[pltpu.VMEM((16, combined.shape[0]), f32)],
        ),
        out_shape=[grad, pack],
        compiler_params=kernel_params(),
        cost_estimate=pl.CostEstimate(
            flops=4 * arrived.size, bytes_accessed=2 * arrived.size, transcendentals=0
        ),
        name="token_terms",
    )(spot.reshape(1), *near(arrived), old, returns, *near(combined))


def weight_kernel(
    own_hidden_ref, other_hidden_ref, own_pack_ref, other_pack_ref, own_ref, other_ref, scale_ref,
    out_ref, loss_ref, rows_ref,
):
    tokens, width = own_ref.shape

    @pl.when(pl.program_id(0) == 0)
    def _():
        loss_ref[0, 0] = jnp.max(own_pack_ref[12:13, :]) + jnp.max(other_pack_ref[12:13, :])
        packs = jnp.concatenate(
            [own_pack_ref[...], other_pack_ref[...], jnp.zeros((96, 128), f32)], axis=0
        )
        columns = jnp.transpose(packs)
        for s, part_ref in enumerate((own_ref, other_ref)):
            for r in range(tokens // 128):
                up = columns[:, 16 * s + r : 16 * s + r + 1]
                down = columns[:, 16 * s + 4 + r : 16 * s + 5 + r]
                part = part_ref[r * 128 : (r + 1) * 128, :].astype(f32)
                line = up * scale_ref[0:1, :] - down * part
                rows_ref[s * tokens + r * 128 : s * tokens + (r + 1) * 128, :] = line.astype(bf16)

    block = out_ref.shape[0]
    part = pl.ds(pl.multiple_of(pl.program_id(0) * block, block), block)
    out_ref[...] = lax.dot_general(
        own_hidden_ref[:, part], rows_ref[:tokens, :], TN, preferred_element_type=f32
    ) + lax.dot_general(
        other_hidden_ref[:, part], rows_ref[tokens:, :], TN, preferred_element_type=f32
    )


def weight_gradient(own_hidden, other_hidden, own_pack, other_pack, own, other, scale):
    tokens, units = own_hidden.shape
    width = own.shape[1]
    block = units // 2
    return pl.pallas_call(
        weight_kernel,
        grid=(units // block,),
        in_specs=[INSIDE] * 7,
        out_specs=[
            pl.BlockSpec((block, width), lambda i: (i, 0)),
            pl.BlockSpec(memory_space=pltpu.SMEM),
        ],
        out_shape=[
            jax.ShapeDtypeStruct((units, width), f32),
            jax.ShapeDtypeStruct((1, 1), f32),
        ],
        scratch_shapes=[pltpu.VMEM((2 * tokens, width), bf16)],
        compiler_params=kernel_params(),
        cost_estimate=pl.CostEstimate(
            flops=4 * units * tokens * width, bytes_accessed=8 * units * width, transcendentals=0
        ),
        name="weight_gradient",
    )(*near(own_hidden, other_hidden), own_pack, other_pack, *near(own, other), scale)


def neighbours():
    pairs = [(z, z ^ 1) for z in range(16)]
    return pairs + [(16 + z, 16 + (z + (1 if z % 2 else -1)) % 16) for z in range(16)]


def on_device(
    hidden_act,
    down_weight,
    residual,
    head_weight,
    gain,
    behavior,
    frozen,
    old_values,
    judge_ratings,
    lengths,
):
    yh, core = lax.axis_index("yh"), lax.axis_index("core")
    parity = lax.axis_index("zl")
    z = 2 * lax.axis_index("zh") + parity
    spot = lax.axis_index(PLANE)
    rows_each, units = hidden_act.shape
    width = down_weight.shape[1]
    chip = 2 * width
    group = 16 * rows_each
    section_rows = 8 * rows_each

    hidden = lax.all_to_all(spread(hidden_act, 16), PLANE, 0, 0, tiled=True)
    other_weight = lax.ppermute(down_weight, "core", SWAP)

    chip_scale = lax.dynamic_slice_in_dim(gain * head_weight, yh * chip, chip, 0)
    own_scale = lax.dynamic_slice_in_dim(chip_scale, core * width, width, 0)
    other_scale = lax.dynamic_slice_in_dim(chip_scale, (1 - core) * width, width, 0)
    scale = jnp.concatenate([own_scale, other_scale])

    kept = lax.dynamic_slice_in_dim(residual, z % 8 * rows_each, rows_each, 0)
    sent = lax.dynamic_slice_in_dim(kept, (1 - yh) * chip, chip, 1)
    mine = lax.dynamic_slice_in_dim(kept, yh * chip, chip, 1)
    stream = jnp.where(yh == z // 8, mine, lax.ppermute(sent, "yh", SWAP))
    left, right = stream[:, :width], stream[:, width:]
    stream = jnp.concatenate(
        [jnp.where(core == 0, left, right), jnp.where(core == 0, right, left)], axis=1
    )

    scale_rows = jnp.pad(jnp.stack(pieces(scale, 3)), ((0, 13), (0, 0))).astype(bf16)
    scale_back = lax.dot_general(
        scale_rows[:, :width], down_weight, NT, preferred_element_type=f32
    ) + lax.dot_general(scale_rows[:, width:], other_weight, NT, preferred_element_type=f32)
    base = jnp.sum(scale_back, axis=0).reshape(-1, 128)
    base = jnp.pad(base, ((0, 16 - base.shape[0]), (0, 0))).astype(bf16)
    slot = jnp.arange(group, dtype=jnp.int32)
    token = slot + section_rows * (slot // section_rows + core)
    own_old = jnp.concatenate(
        [
            lax.dynamic_slice_in_dim(old_values, core * section_rows, section_rows, 0),
            lax.dynamic_slice_in_dim(old_values, (2 + core) * section_rows, section_rows, 0),
        ]
    )
    returns = own_old + returns_of(behavior, frozen, old_values, judge_ratings, lengths, token)
    returns, own_old = returns.reshape(4, 128), own_old.reshape(4, 128)
    hidden, returns, own_old = lax.optimization_barrier((hidden, returns, own_old))

    away = forward(hidden, down_weight, other_weight, 1 - parity, bf16)
    met = lax.ppermute(away, ("core", "zh", "zl"), neighbours())
    kept_half = forward(hidden, down_weight, other_weight, parity, f32)
    pair = (kept_half + met.astype(f32)).astype(bf16)
    parts = lax.all_to_all(pair.reshape(8, rows_each, chip), "zh", 0, 0, tiled=True)
    combined = (jnp.sum(parts.astype(f32), axis=0) + stream.astype(f32)).astype(bf16)
    combined = lax.all_gather(combined, ("zh", "zl"), axis=0, tiled=True)
    own_columns, other_columns = combined[:, :width], combined[:, width:]

    payload = back(combined, down_weight, other_weight, scale_rows, base, 16)
    arrived = lax.all_to_all(payload, PLANE, 0, 0, tiled=True)
    far_columns = lax.ppermute(other_columns, "core", SWAP)
    hidden = hidden.reshape(group, units)
    far_hidden = lax.ppermute(hidden, "core", SWAP)
    arrived, far_columns, far_hidden = lax.optimization_barrier((arrived, far_columns, far_hidden))

    hidden_grad, pack = token_terms(spot, arrived, own_old, returns, combined, units)
    other_pack = lax.ppermute(pack, "core", SWAP)
    own_head = pack[8:10] + other_pack[10:12]
    other_head = pack[10:12] + other_pack[8:10]
    head_chip = jnp.concatenate(
        [jnp.where(core == 0, own_head, other_head), jnp.where(core == 0, other_head, own_head)]
    )
    head_far = lax.ppermute(head_chip, "yh", SWAP)
    head_sum = jnp.concatenate(
        [jnp.where(yh == 0, head_chip, head_far), jnp.where(yh == 0, head_far, head_chip)]
    )
    head_grad = gain * head_sum.reshape(-1)

    weight_grad, total_loss = weight_gradient(
        hidden, far_hidden, pack, other_pack, own_columns, far_columns, own_scale.reshape(1, -1)
    )
    return (total_loss[0, 0], head_grad, weight_grad, hidden_grad)


def solution(mesh):
    axes = ("yh", "core", "x", "yl", "zh", "zl")
    fine = Mesh(mesh.devices.reshape(2, 2, 4, 2, 8, 2), axes)
    tp = ("zh", "zl")
    in_specs = (
        P(("yh", "core", "x", "yl"), tp),
        P(tp, ("x", "yl", "yh", "core")),
        P(("yh", "core"), ("x", "yl")),
        P(("x", "yl")),
        P(("x", "yl")),
        P(),
        P(),
        P(),
        P(),
        P(),
    )
    out_specs = (
        P(),
        P(("x", "yl")),
        P(tp, ("x", "yl", "yh", "core")),
        P(("yh", "core", "x", "yl"), tp),
    )
    return jax.shard_map(
        on_device, mesh=fine, in_specs=in_specs, out_specs=out_specs, check_vma=False
    )
```

time: 170 us -> 158 us (0.929)
  local copies, waits for them, and re-layouts: 9.73 us -> 2.17 us
  between operations: 3.47 us -> 1.01 us
    ppermute x1, starting transfers between devices: 16.7 us -> 14.3 us  [on_device(): other_pack = lax.ppermute(pack, 'core', SWAP)]
    reshape x1 -> x0, local copies, waits for them, and re-layouts: 2.32 us -> none  [on_device(): hidden.reshape(group, units)]
    broadcast_in_dim x1 -> x0, local copies, waits for them, and re-layouts: 2.32 us -> none  [on_device(): spread = jnp.broadcast_to(hidden_act[None], (16, rows_each, units))]
    ppermute x3, waiting for transfers between devices: 1.49 us -> 3.61 us  [the longest x1 1.83 us: on_device(): met = lax.ppermute(away, ('core', 'zh', 'zl'), neighbours())]
    ppermute x1, starting transfers between devices: 2.61 us -> 4.7 us  [on_device(): head_far = lax.ppermute(head_chip, 'yh', SWAP)]
    all_to_all x1, waiting for transfers between devices: 12.1 us -> 10.2 us  [on_device(): hidden = lax.all_to_all(spread(hidden_act, 16), PLANE, 0, 0, tiled=True)]
    unnamed x20 -> x18, local copies, waits for them, and re-layouts: 2.84 us -> 0.94 us
    pallas_call x4 -> x5, Pallas kernels: 13.7 us -> 13.2 us  [the longest x1 4.33 us: weight_gradient(): pl.pallas_call(weight_kernel, grid=(units // block,), in_specs=[INSIDE] *...]
  transfers between devices with their start and end apart: 10 -> 10, of which waited for: 4 -> 6; matrix products, arithmetic and copies ran while one was open for 6% -> 4% of each run, Pallas kernels for 8% -> 5%
where the time goes in v3:
time: 158 us
  starting transfers between devices  79.4 us (50%)
  waiting for transfers between devices  29.3 us (19%)
  blocking collectives  23.8 us (15%)
  Pallas kernels  15.7 us (10%)
  other arithmetic  4.19 us (3%)
  local copies, waits for them, and re-layouts  2.17 us (1%)
  matrix products  1.95 us (1%)
    all_gather x1, blocking collectives, on_device(): combined = lax.all_gather(combined, ('zh', 'zl'), axis=0, tiled=True)  23.8 us
    ppermute x1, starting transfers between devices, on_device(): met = lax.ppermute(away, ('core', 'zh', 'zl'), neighbours())  15.8 us
    ppermute x1, starting transfers between devices, on_device(): other_pack = lax.ppermute(pack, 'core', SWAP)  14.3 us
    all_to_all x1, waiting for transfers between devices, on_device(): lax.all_to_all(pair.reshape(8, rows_each, chip), 'zh', 0, 0, tiled=True)  14.3 us
    ppermute x1, starting transfers between devices, on_device(): far_hidden = lax.ppermute(hidden, 'core', SWAP)  12.4 us
    all_to_all x1, waiting for transfers between devices, on_device(): hidden = lax.all_to_all(spread(hidden_act, 16), PLANE, 0, 0, tiled=True)  10.2 us
    all_to_all x1, starting transfers between devices, on_device(): lax.all_to_all(pair.reshape(8, rows_each, chip), 'zh', 0, 0, tiled=True)  8.26 us
    all_to_all x1, starting transfers between devices, on_device(): hidden = lax.all_to_all(spread(hidden_act, 16), PLANE, 0, 0, tiled=True)  7.73 us
  transfers between devices with their start and end apart: 10, of which 6 were waited for; matrix products, arithmetic and copies ran while one was open for 4% of the time, Pallas kernels for 5%

profile of v3, /device:TPU:1, one launch (start us, length us, event | category | flops | bytes accessed | tf_op | source)
XLA Modules:
  0.0 157.6 jit_solution(9411048578863734361)
XLA Ops:
  1.5 1.5 spread.1
  3.1 7.7 %all-to-all-start = ((bf16[16,32,1792]{2,1,0:T(8,128)(2,1)}), bf16[16,32,1792]{2,1,0:T(8,128)(2,1)S(1)}, u32[]{:S(2)}, u32[]{:S(2)}) async-start(bf16[16,32,1792]{2,1,0:T(8,128)(2,1)} %spread.1), calls=%async_computation | async-start | bytes 3670016 | tf_op jit(solution)/shard_map/all_to_all | solution.py:341
  10.9 4.9 %collective-permute-start = (bf16[1792,256]{1,0:T(8,128)(2,1)S(1)}, bf16[1792,256]{1,0:T(8,128)(2,1)}, u32[]{:S(2)}, u32[]{:S(2)}) collective-permute-start(bf16[1792,256]{1,0:T(8,128)(2,1)S(1)} %copy-done), channel_id=1, source_target_pairs={{0,128},{128,0},{1,129},{129,1},{2,130},{130,2},{3,131},{131,3},{4... | collective-permute-start | bytes 2752520 | tf_op jit(solution)/shard_map/ppermute | solution.py:342
  16.7 5.0 %collective-permute-start.2 = (bf16[32,512]{1,0:T(8,128)(2,1)S(1)}, bf16[32,512]{1,0:T(8,128)(2,1)S(1)}, u32[]{:S(2)}, u32[]{:S(2)}) collective-permute-start(bf16[32,512]{1,0:T(8,128)(2,1)S(1)} %dynamic_slice.27), channel_id=1, source_target_pairs={{0,256},{256,0},{1,257},{257,1},{2,258},{258,2},{3,259},{259,3},{4... | collective-permute-start | bytes 98312 | tf_op jit(solution)/shard_map/ppermute | solution.py:352
  22.6 1.2 multiply_reduce_fusion
  23.8 10.2 %all-to-all-done = bf16[16,32,1792]{2,1,0:T(8,128)(2,1)S(1)} async-done(((bf16[16,32,1792]{2,1,0:T(8,128)(2,1)}), bf16[16,32,1792]{2,1,0:T(8,128)(2,1)S(1)}, u32[]{:S(2)}, u32[]{:S(2)}) %all-to-all-start) | async-done | bytes 1835040 | tf_op jit(solution)/shard_map/all_to_all | solution.py:341
  34.0 1.8 %forward.3 = bf16[256,512]{1,0:T(8,128)(2,1)S(1)} custom-call(s32[1]{0:T(128)} %bitcast.7.half_ref, bf16[8,2,32,1792]{3,2,1,0:T(8,128)(2,1)S(1)} %bitcast.25, bf16[1792,256]{1,0:T(8,128)(2,1)S(1)} %copy-done, bf16[1792,256]{1,0:T(8,128)(2,1)} %collective-permute-done.other_ref), custom_call_target="tpu_custom_call" | custom-call | flops 469762048 | bytes 1835008 | tf_op jit(solution)/shard_map/forward/pallas_call | solution.py:102
  35.8 15.8 %collective-permute-start.1 = (bf16[256,512]{1,0:T(8,128)(2,1)S(1)}, bf16[256,512]{1,0:T(8,128)(2,1)S(1)}, u32[]{:S(2)}, u32[]{:S(2)}) collective-permute-start(bf16[256,512]{1,0:T(8,128)(2,1)S(1)} %forward.3), channel_id=1, source_target_pairs={{0,1},{1,0},{2,3},{3,2},{4,5},{5,4},{6,7},{7,6},{8,9},{9,8},{10,11... | collective-permute-start | bytes 786440 | tf_op jit(solution)/shard_map/ppermute | solution.py:377
  51.7 1.8 %forward.2 = f32[256,512]{1,0:T(8,128)S(1)} custom-call(s32[1]{0:T(128)} %bitcast.5.half_ref, bf16[8,2,32,1792]{3,2,1,0:T(8,128)(2,1)S(1)} %bitcast.26, bf16[1792,256]{1,0:T(8,128)(2,1)S(1)} %copy-done, bf16[1792,256]{1,0:T(8,128)(2,1)} %collective-permute-done.other_ref), custom_call_target="tpu_custom_call" | custom-call | flops 469762048 | bytes 1835008 | tf_op jit(solution)/shard_map/forward/pallas_call | solution.py:102
  53.5 1.8 %collective-permute-done.1 = bf16[256,512]{1,0:T(8,128)(2,1)S(1)} collective-permute-done((bf16[256,512]{1,0:T(8,128)(2,1)S(1)}, bf16[256,512]{1,0:T(8,128)(2,1)S(1)}, u32[]{:S(2)}, u32[]{:S(2)}) %collective-permute-start.1) | collective-permute-done | bytes 262176 | tf_op jit(solution)/shard_map/ppermute | solution.py:377
  56.1 8.3 %all-to-all-start.1 = ((bf16[8,32,512]{2,1,0:T(8,128)(2,1)}), bf16[8,32,512]{2,1,0:T(8,128)(2,1)S(1)}, u32[]{:S(2)}, u32[]{:S(2)}) async-start(bf16[8,32,512]{2,1,0:T(8,128)(2,1)} %bitcast.8), calls=%async_computation.1 | async-start | bytes 524288 | tf_op jit(solution)/shard_map/all_to_all | solution.py:380
  64.8 0.9 dynamic-slice_select_fusion
  65.7 1.6 %fusion.2 = bf16[1792]{0:T(1024)(128)(2,1)S(1)} fusion(f32[16,1792]{1,0:T(8,128)S(1)} %fusion.10, bf16[1792,256]{1,0:T(8,128)(2,1)} %collective-permute-done.other_ref, bf16[16,512]{1,0:T(8,128)(2,1)S(1)} %fusion.8.scale_ref), kind=kOutput, calls=%fused_computation.5 | convolution fusion | flops 14735616 | bytes 1043968 | tf_op jit(solution)/shard_map/dot_general | solution.py:361
  67.3 14.3 %all-to-all-done.1 = bf16[8,32,512]{2,1,0:T(8,128)(2,1)S(1)} async-done(((bf16[8,32,512]{2,1,0:T(8,128)(2,1)}), bf16[8,32,512]{2,1,0:T(8,128)(2,1)S(1)}, u32[]{:S(2)}, u32[]{:S(2)}) %all-to-all-start.1) | async-done | bytes 262176 | tf_op jit(solution)/shard_map/all_to_all | solution.py:380
  81.6 23.8 %all_gather.3.combined_ref = bf16[512,512]{1,0:T(8,128)(2,1)S(1)} all-gather(bf16[32,512]{1,0:T(8,128)(2,1)S(1)} %add_convert_fusion.1), channel_id=1, replica_groups=mesh['yh'=2,'core'=2,'x'=4,'yl'=2,'zh'=8,'zl'=2] {'zh','zl'}, dimensions={0}, use_global_device_ids=true | all-gather | bytes 557056 | tf_op jit(solution)/shard_map/all_gather | solution.py:382
  105.5 3.8 %back.1 = bf16[16,32,1920]{2,1,0:T(8,128)(2,1)} custom-call(bf16[512,512]{1,0:T(8,128)(2,1)S(1)} %all_gather.3.combined_ref, bf16[1792,256]{1,0:T(8,128)(2,1)S(1)} %copy-done, bf16[1792,256]{1,0:T(8,128)(2,1)} %collective-permute-done.other_ref, bf16[16,512]{1,0:T(8,128)(2,1)S(1)} %fusion.8.scale_ref, bf16[16,128]{1,0:T(8,128)(2,1)S(1)} %pad.11.base_ref), custom_call_target="tpu_custom_call" | custom-call | flops 939524096 | bytes 3670016 | tf_op jit(solution)/shard_map/back/pallas_call | solution.py:162
  109.3 4.4 %all-to-all-start.2 = ((bf16[16,32,1920]{2,1,0:T(8,128)(2,1)}), bf16[16,32,1920]{2,1,0:T(8,128)(2,1)}, u32[]{:S(2)}, u32[]{:S(2)}) async-start(bf16[16,32,1920]{2,1,0:T(8,128)(2,1)} %back.1), calls=%async_computation.2 | async-start | bytes 3932160 | tf_op jit(solution)/shard_map/all_to_all | solution.py:386
  113.7 12.4 %collective-permute-start.4 = (bf16[512,1792]{1,0:T(8,128)(2,1)S(1)}, bf16[512,1792]{1,0:T(8,128)(2,1)}, u32[]{:S(2)}, u32[]{:S(2)}) collective-permute-start(bf16[512,1792]{1,0:T(8,128)(2,1)S(1)} %bitcast.27), channel_id=1, source_target_pairs={{0,128},{128,0},{1,129},{129,1},{2,130},{130,2},{3,131},{131,3},{4... | collective-permute-start | bytes 5505032 | tf_op jit(solution)/shard_map/ppermute | solution.py:389
  126.1 1.9 %collective-permute-start.3 = (bf16[512,256]{1,0:T(8,128)(2,1)S(1)}, bf16[512,256]{1,0:T(8,128)(2,1)S(1)}, u32[]{:S(2)}, u32[]{:S(2)}) collective-permute-start(bf16[512,256]{1,0:T(8,128)(2,1)S(1)} %get-tuple-element.25), channel_id=1, source_target_pairs={{0,128},{128,0},{1,129},{129,1},{2,130},{130,2},{3,131},{131,3},{4... | collective-permute-start | bytes 786440 | tf_op jit(solution)/shard_map/ppermute | solution.py:387
  128.1 1.8 %collective-permute-done.3.other_ref = bf16[512,256]{1,0:T(8,128)(2,1)S(1)} collective-permute-done((bf16[512,256]{1,0:T(8,128)(2,1)S(1)}, bf16[512,256]{1,0:T(8,128)(2,1)S(1)}, u32[]{:S(2)}, u32[]{:S(2)}) %collective-permute-start.3) | collective-permute-done | bytes 262176 | tf_op jit(solution)/shard_map/ppermute | solution.py:387
  130.2 2.6 %token_terms.1 = (bf16[32,1792]{1,0:T(8,128)(2,1)}, f32[16,128]{1,0:T(8,128)S(1)}) custom-call(s32[1]{0:T(128)} %bitcast.12.spot_ref, bf16[16,32,1920]{2,1,0:T(8,128)(2,1)} %all-to-all-done.2.arrived_ref, f32[4,128]{1,0:T(4,128)S(1)} %get-tuple-element.17.old_ref, f32[4,128]{1,0:T(4,128)S(1)} %get-tuple-element.18.returns_ref, ...), custom_call_target="tpu_custom_call" | custom-call | flops 3932160 | bytes 1966080 | tf_op jit(solution)/shard_map/token_terms/pallas_call | solution.py:241
  132.8 14.3 %collective-permute-start.5 = (f32[16,128]{1,0:T(8,128)S(1)}, f32[16,128]{1,0:T(8,128)S(1)}, u32[]{:S(2)}, u32[]{:S(2)}) collective-permute-start(f32[16,128]{1,0:T(8,128)S(1)} %get-tuple-element.19.own_pack_ref), channel_id=1, source_target_pairs={{0,128},{128,0},{1,129},{129,1},{2,130},{130,2},{3,131},{131,3},{4... | collective-permute-start | bytes 24584 | tf_op jit(solution)/shard_map/ppermute | solution.py:393
  147.9 4.7 %collective-permute-start.6 = (f32[4,128]{1,0:T(4,128)S(1)}, f32[4,128]{1,0:T(4,128)S(1)}, u32[]{:S(2)}, u32[]{:S(2)}) collective-permute-start(f32[4,128]{1,0:T(4,128)S(1)} %pad_maximum_fusion.2), channel_id=1, source_target_pairs={{0,256},{256,0},{1,257},{257,1},{2,258},{258,2},{3,259},{259,3},{4... | collective-permute-start | bytes 6152 | tf_op jit(solution)/shard_map/ppermute | solution.py:399
  152.6 4.3 %weight_gradient.1 = (f32[1792,256]{1,0:T(8,128)}, f32[1,1]{1,0:T(1,128)}) custom-call(bf16[512,1792]{1,0:T(8,128)(2,1)S(1)} %bitcast.28, bf16[512,1792]{1,0:T(8,128)(2,1)} %collective-permute-done.4.other_hidden_ref, f32[16,128]{1,0:T(8,128)S(1)} %get-tuple-element.19.own_pack_ref, f32[16,128]{1,0:T(8,128)S(1)} %collective-permute-done.5.other_pack_ref, ...), custom_call_target="tpu_custom_call" | custom-call | flops 939524096 | bytes 3670016 | tf_op jit(solution)/shard_map/weight_gradient/pallas_call | solution.py:293
  (53 shorter events, 5.9 us)
Async XLA Ops:
  0.6 0.9 copy-start.1
  3.0 7.8 %copy-start = (bf16[1792,256]{1,0:T(8,128)(2,1)S(1)}, bf16[1792,256]{1,0:T(8,128)(2,1)}, u32[]{:S(2)}) copy-start(bf16[1792,256]{1,0:T(8,128)(2,1)} %own_ref.5) | copy-start | bytes 2752516
  3.0 18.7 %copy-start.7 = (s32[16]{0:T(128)S(1)}, s32[16]{0:T(128)}, u32[]{:S(2)}) copy-start(s32[16]{0:T(128)} %param.19) | copy-start | bytes 196
  3.0 18.9 %copy-start.2 = (f32[1024]{0:T(1024)S(1)}, f32[1024]{0:T(1024)}, u32[]{:S(2)}) copy-start(f32[1024]{0:T(1024)} %param.17) | copy-start | bytes 12292
  3.0 19.3 %copy-start.3 = (f32[1024]{0:T(1024)S(1)}, f32[1024]{0:T(1024)}, u32[]{:S(2)}) copy-start(f32[1024]{0:T(1024)} %param.14) | copy-start | bytes 12292
  3.1 19.3 %copy-start.4 = (f32[1024]{0:T(1024)S(1)}, f32[1024]{0:T(1024)}, u32[]{:S(2)}) copy-start(f32[1024]{0:T(1024)} %param.13) | copy-start | bytes 12292
  3.1 19.4 %copy-start.8 = (f32[16]{0:T(128)S(1)}, f32[16]{0:T(128)}, u32[]{:S(2)}) copy-start(f32[16]{0:T(128)} %param.18) | copy-start | bytes 196
  3.1 19.5 %copy-start.5 = (f32[1024]{0:T(1024)S(1)}, f32[1024]{0:T(1024)}, u32[]{:S(2)}) copy-start(f32[1024]{0:T(1024)} %param.15) | copy-start | bytes 12292
  3.1 19.5 %copy-start.6 = (f32[1024]{0:T(1024)S(1)}, f32[1024]{0:T(1024)}, u32[]{:S(2)}) copy-start(f32[1024]{0:T(1024)} %param.16) | copy-start | bytes 12292
  3.1 30.9 %all-to-all-start = ((bf16[16,32,1792]{2,1,0:T(8,128)(2,1)}), bf16[16,32,1792]{2,1,0:T(8,128)(2,1)S(1)}, u32[]{:S(2)}, u32[]{:S(2)}) async-start(bf16[16,32,1792]{2,1,0:T(8,128)(2,1)} %spread.1), calls=%async_computation | async-start | bytes 3670016 | tf_op jit(solution)/shard_map/all_to_all | solution.py:341
  10.9 23.2 %collective-permute-start = (bf16[1792,256]{1,0:T(8,128)(2,1)S(1)}, bf16[1792,256]{1,0:T(8,128)(2,1)}, u32[]{:S(2)}, u32[]{:S(2)}) collective-permute-start(bf16[1792,256]{1,0:T(8,128)(2,1)S(1)} %copy-done), channel_id=1, source_target_pairs={{0,128},{128,0},{1,129},{129,1},{2,130},{130,2},{3,131},{131,3},{4... | collective-permute-start | bytes 2752520 | tf_op jit(solution)/shard_map/ppermute | solution.py:342
  16.7 48.1 %collective-permute-start.2 = (bf16[32,512]{1,0:T(8,128)(2,1)S(1)}, bf16[32,512]{1,0:T(8,128)(2,1)S(1)}, u32[]{:S(2)}, u32[]{:S(2)}) collective-permute-start(bf16[32,512]{1,0:T(8,128)(2,1)S(1)} %dynamic_slice.27), channel_id=1, source_target_pairs={{0,256},{256,0},{1,257},{257,1},{2,258},{258,2},{3,259},{259,3},{4... | collective-permute-start | bytes 98312 | tf_op jit(solution)/shard_map/ppermute | solution.py:352
  35.8 19.5 %collective-permute-start.1 = (bf16[256,512]{1,0:T(8,128)(2,1)S(1)}, bf16[256,512]{1,0:T(8,128)(2,1)S(1)}, u32[]{:S(2)}, u32[]{:S(2)}) collective-permute-start(bf16[256,512]{1,0:T(8,128)(2,1)S(1)} %forward.3), channel_id=1, source_target_pairs={{0,1},{1,0},{2,3},{3,2},{4,5},{5,4},{6,7},{7,6},{8,9},{9,8},{10,11... | collective-permute-start | bytes 786440 | tf_op jit(solution)/shard_map/ppermute | solution.py:377
  56.1 25.5 %all-to-all-start.1 = ((bf16[8,32,512]{2,1,0:T(8,128)(2,1)}), bf16[8,32,512]{2,1,0:T(8,128)(2,1)S(1)}, u32[]{:S(2)}, u32[]{:S(2)}) async-start(bf16[8,32,512]{2,1,0:T(8,128)(2,1)} %bitcast.8), calls=%async_computation.1 | async-start | bytes 524288 | tf_op jit(solution)/shard_map/all_to_all | solution.py:380
  109.3 21.0 %all-to-all-start.2 = ((bf16[16,32,1920]{2,1,0:T(8,128)(2,1)}), bf16[16,32,1920]{2,1,0:T(8,128)(2,1)}, u32[]{:S(2)}, u32[]{:S(2)}) async-start(bf16[16,32,1920]{2,1,0:T(8,128)(2,1)} %back.1), calls=%async_computation.2 | async-start | bytes 3932160 | tf_op jit(solution)/shard_map/all_to_all | solution.py:386
  113.7 16.1 %collective-permute-start.4 = (bf16[512,1792]{1,0:T(8,128)(2,1)S(1)}, bf16[512,1792]{1,0:T(8,128)(2,1)}, u32[]{:S(2)}, u32[]{:S(2)}) collective-permute-start(bf16[512,1792]{1,0:T(8,128)(2,1)S(1)} %bitcast.27), channel_id=1, source_target_pairs={{0,128},{128,0},{1,129},{129,1},{2,130},{130,2},{3,131},{131,3},{4... | collective-permute-start | bytes 5505032 | tf_op jit(solution)/shard_map/ppermute | solution.py:389
  126.1 3.7 %collective-permute-start.3 = (bf16[512,256]{1,0:T(8,128)(2,1)S(1)}, bf16[512,256]{1,0:T(8,128)(2,1)S(1)}, u32[]{:S(2)}, u32[]{:S(2)}) collective-permute-start(bf16[512,256]{1,0:T(8,128)(2,1)S(1)} %get-tuple-element.25), channel_id=1, source_target_pairs={{0,128},{128,0},{1,129},{129,1},{2,130},{130,2},{3,131},{131,3},{4... | collective-permute-start | bytes 786440 | tf_op jit(solution)/shard_map/ppermute | solution.py:387
  132.8 15.1 %collective-permute-start.5 = (f32[16,128]{1,0:T(8,128)S(1)}, f32[16,128]{1,0:T(8,128)S(1)}, u32[]{:S(2)}, u32[]{:S(2)}) collective-permute-start(f32[16,128]{1,0:T(8,128)S(1)} %get-tuple-element.19.own_pack_ref), channel_id=1, source_target_pairs={{0,128},{128,0},{1,129},{129,1},{2,130},{130,2},{3,131},{131,3},{4... | collective-permute-start | bytes 24584 | tf_op jit(solution)/shard_map/ppermute | solution.py:393
  147.9 9.0 %collective-permute-start.6 = (f32[4,128]{1,0:T(4,128)S(1)}, f32[4,128]{1,0:T(4,128)S(1)}, u32[]{:S(2)}, u32[]{:S(2)}) collective-permute-start(f32[4,128]{1,0:T(4,128)S(1)} %pad_maximum_fusion.2), channel_id=1, source_target_pairs={{0,256},{256,0},{1,257},{257,1},{2,258},{258,2},{3,259},{259,3},{4... | collective-permute-start | bytes 6152 | tf_op jit(solution)/shard_map/ppermute | solution.py:399

commit v4 on v3

--- a/solution.py
+++ b/solution.py
@@ -50,10 +50,34 @@
 NT = (((1,), (1,)), ((), ()))
 TN = (((0,), (0,)), ((), ()))
 INSIDE = pl.BlockSpec(memory_space=pltpu.VMEM)
+OUTSIDE = pl.BlockSpec(memory_space=pl.ANY)
 
 
 def near(*arrays):
     return [pltpu.with_memory_space_constraint(a, pltpu.VMEM) for a in arrays]
+
+
+def far(array):
+    return pltpu.with_memory_space_constraint(array, pltpu.HBM)
+
+
+def hold_kernel(in_ref, out_ref, sem):
+    copy = pltpu.make_async_copy(in_ref, out_ref, sem)
+    copy.start()
+    copy.wait()
+
+
+def hold(x):
+    return pl.pallas_call(
+        hold_kernel,
+        in_specs=[pl.BlockSpec(memory_space=pl.ANY)],
+        out_specs=INSIDE,
+        out_shape=pltpu.VMEM(x.shape, x.dtype),
+        scratch_shapes=[pltpu.SemaphoreType.DMA],
+        compiler_params=kernel_params(),
+        cost_estimate=pl.CostEstimate(flops=0, bytes_accessed=4 * x.size, transcendentals=0),
+        name="hold",
+    )(x)
 
 
 def spread_kernel(in_ref, out_ref, held_ref, sem, sems):
@@ -112,61 +136,85 @@
     )(half.reshape(1), *near(hidden.reshape(count // 2, 2, rows, units), own_weight, other_weight))
 
 
-def back_kernel(combined_ref, own_ref, other_ref, scale_ref, base_ref, out_ref, held_ref, rows_ref, sems):
+def sums_kernel(combined_ref, scale_ref, base_ref, out_ref, held_ref, rows_ref, sem):
+    peers, rows, lanes = out_ref.shape
+    both = combined_ref[...]
+    wide = both.astype(f32)
+    square = wide * wide
+    top = square.astype(bf16)
+    rest = (square - top.astype(f32)).astype(bf16)
+    ones = jnp.ones((16, both.shape[1]), bf16)
+    squares = lax.dot_general(ones, top, NT, preferred_element_type=f32)
+    squares += lax.dot_general(ones, rest, NT, preferred_element_type=f32)
+    products = lax.dot_general(scale_ref[...], both, NT, preferred_element_type=f32)
+    place = 0
+    for line in (squares[0:1], jnp.sum(products, axis=0, keepdims=True)):
+        top = line.astype(bf16).astype(f32)
+        for part in (top, line - top):
+            for i in range(4):
+                rows_ref[place : place + 1, :] = part[:, i * lanes : (i + 1) * lanes]
+                place += 1
+    sums = rows_ref[...].astype(bf16)
+    held_ref[:, :16, :] = jnp.broadcast_to(sums[None], (peers, 16, lanes))
+    held_ref[:, 16:, :] = jnp.broadcast_to(base_ref[...][None], (peers, rows - 16, lanes))
+    copy = pltpu.make_async_copy(held_ref, out_ref, sem)
+    copy.start()
+    copy.wait()
+
+
+def token_sums(combined, scale_rows, base, peers):
+    shape = (peers, 32, 128)
+    return pl.pallas_call(
+        sums_kernel,
+        in_specs=[INSIDE] * 3,
+        out_specs=pl.BlockSpec(memory_space=pltpu.HBM),
+        out_shape=pltpu.HBM(shape, bf16),
+        scratch_shapes=[pltpu.VMEM(shape, bf16), pltpu.VMEM((16, 128), f32), pltpu.SemaphoreType.DMA],
+        compiler_params=kernel_params(),
+        cost_estimate=pl.CostEstimate(flops=96 * combined.size, bytes_accessed=2 * combined.size, transcendentals=0),
+        name="token_sums",
+    )(*near(combined), scale_rows, base)
+
+
+def back_kernel(combined_ref, outer_ref, other_ref, out_ref, own_ref, held_ref, sem, sems):
+    copy = pltpu.make_async_copy(outer_ref, own_ref, sem)
+    copy.start()
     width = own_ref.shape[1]
     parts, peers, rows, lanes = held_ref.shape
-    units = own_ref.shape[0]
-    both = combined_ref[...]
 
     def send(j):
         target = out_ref.at[:, :, j * lanes : (j + 1) * lanes]
         return pltpu.make_async_copy(held_ref.at[j], target, sems.at[j])
 
     for j in range(parts):
-        start = j * lanes
-        size = min(lanes, units - start)
+        cut = slice(j * lanes, (j + 1) * lanes)
         total = lax.dot_general(
-            both[:, :width], own_ref[start : start + size, :], NT, preferred_element_type=f32
-        ) + lax.dot_general(
-            both[:, width:], other_ref[start : start + size, :], NT, preferred_element_type=f32
+            combined_ref[:, width:], other_ref[cut, :], NT, preferred_element_type=f32
         )
-        held_ref[j, :, :, :size] = total.astype(bf16).reshape(peers, rows, size)
-        if j == parts - 1:
-            wide = both.astype(f32)
-            square = wide * wide
-            top = square.astype(bf16)
-            rest = (square - top.astype(f32)).astype(bf16)
-            ones = jnp.ones((16, both.shape[1]), bf16)
-            squares = lax.dot_general(ones, top, NT, preferred_element_type=f32)
-            squares += lax.dot_general(ones, rest, NT, preferred_element_type=f32)
-            products = lax.dot_general(scale_ref[...], both, NT, preferred_element_type=f32)
-            place = 0
-            for line in (squares[0:1], jnp.sum(products, axis=0, keepdims=True)):
-                top = line.astype(bf16).astype(f32)
-                for part in (top, line - top):
-                    for i in range(4):
-                        rows_ref[place : place + 1, :] = part[:, i * 128 : (i + 1) * 128]
-                        place += 1
-            sums = rows_ref[...].astype(bf16)
-            held_ref[j, :, :16, size:] = jnp.broadcast_to(sums[None], (peers, 16, 128))
-            held_ref[j, :, 16:, size:] = jnp.broadcast_to(base_ref[...][None], (peers, rows - 16, 128))
+        if j == 0:
+            copy.wait()
+        total += lax.dot_general(
+            combined_ref[:, :width], own_ref[cut, :], NT, preferred_element_type=f32
+        )
+        held_ref[j] = total.astype(bf16).reshape(peers, rows, lanes)
         send(j).start()
     for j in range(parts):
         send(j).wait()
 
 
-def back(combined, own_weight, other_weight, scale_rows, base, peers):
+def back(combined, own_weight, other_weight, peers):
     tokens, chip = combined.shape
     units, width = own_weight.shape
-    rows, lanes, parts = 32, units + 128, 3
+    rows, parts = tokens // peers, 2
     return pl.pallas_call(
         back_kernel,
-        in_specs=[INSIDE] * 5,
+        in_specs=[INSIDE, OUTSIDE, INSIDE],
         out_specs=pl.BlockSpec(memory_space=pltpu.HBM),
-        out_shape=pltpu.HBM((peers, rows, lanes), bf16),
+        out_shape=pltpu.HBM((peers, rows, units), bf16),
         scratch_shapes=[
-            pltpu.VMEM((parts, peers, rows, lanes // parts), bf16),
-            pltpu.VMEM((16, 128), f32),
+            pltpu.VMEM((units, width), bf16),
+            pltpu.VMEM((parts, peers, rows, units // parts), bf16),
+            pltpu.SemaphoreType.DMA,
             pltpu.SemaphoreType.DMA((parts,)),
         ],
         compiler_params=kernel_params(),
@@ -174,23 +222,14 @@
             flops=4 * tokens * units * width, bytes_accessed=8 * units * width, transcendentals=0
         ),
         name="back",
-    )(*near(combined, own_weight, other_weight), scale_rows, base)
-
-
-def token_kernel(spot_ref, arrived_ref, old_ref, returns_ref, combined_ref, grad_ref, pack_ref, up_ref):
-    spot = spot_ref[0]
-    peers, rows, lanes = arrived_ref.shape
-    units = grad_ref.shape[1]
-
-    def total(start, size):
-        out = arrived_ref[0, :, start : start + size].astype(f32)
-        for p in range(1, peers):
-            out += arrived_ref[p, :, start : start + size].astype(f32)
-        return out
-
-    left = total(units, 128)
-    square_sum = left[0:4] + left[4:8]
-    product_sum = left[8:12] + left[12:16]
+    )(*near(combined), far(own_weight), *near(other_weight))
+
+
+def token_kernel(sums_ref, old_ref, returns_ref, combined_ref, pack_ref, up_ref):
+    sums = jnp.sum(sums_ref[...].astype(f32), axis=0)
+    square_sum = sums[0:4] + sums[4:8]
+    product_sum = sums[8:12] + sums[12:16]
+    pack_ref[16:32, :] = sums[16:32]
     old, returns = old_ref[...], returns_ref[...]
     rinv = lax.rsqrt(square_sum / D + EPSILON)
     values = rinv * product_sum
@@ -218,6 +257,23 @@
     for r in range(4):
         pack_ref[8 + r : 9 + r, :] = head[:, r * 128 : (r + 1) * 128]
 
+
+def token_terms(sums, old, returns, combined):
+    return pl.pallas_call(
+        token_kernel,
+        in_specs=[INSIDE] * 4,
+        out_specs=INSIDE,
+        out_shape=jax.ShapeDtypeStruct((32, 128), f32),
+        scratch_shapes=[pltpu.VMEM((16, combined.shape[0]), f32)],
+        compiler_params=kernel_params(),
+        cost_estimate=pl.CostEstimate(flops=4 * combined.size, bytes_accessed=2 * combined.size, transcendentals=0),
+        name="token_terms",
+    )(sums, old, returns, combined)
+
+
+def hidden_kernel(spot_ref, arrived_ref, pack_ref, grad_ref):
+    spot = spot_ref[0]
+    peers, rows, units = arrived_ref.shape
     which = lax.broadcasted_iota(jnp.int32, (4, 128), 0) == spot // 4
     lane = lax.broadcasted_iota(jnp.int32, (rows, 128), 1)
     sub = lax.broadcasted_iota(jnp.int32, (rows, 128), 0)
@@ -227,88 +283,97 @@
         line = jnp.sum(jnp.where(which, x, 0.0), axis=0, keepdims=True)
         return jnp.sum(jnp.where(pick, line, 0.0), axis=1, keepdims=True)
 
-    own_up, own_down = column(up), column(down)
-    scale_back = left[16:32]
+    own_up, own_down = column(pack_ref[0:4, :]), column(pack_ref[4:8, :])
     for k in range(units // 128):
-        part = own_up * scale_back[k : k + 1, :] - own_down * total(k * 128, 128)
-        grad_ref[:, k * 128 : (k + 1) * 128] = part.astype(bf16)
-
-
-def token_terms(spot, arrived, old, returns, combined, units):
-    full = lambda a: pl.BlockSpec(a.shape, lambda i, s: (0,) * a.ndim)
-    grad = jax.ShapeDtypeStruct((arrived.shape[1], units), bf16)
-    pack = jax.ShapeDtypeStruct((16, 128), f32)
-    return pl.pallas_call(
-        token_kernel,
-        grid_spec=pltpu.PrefetchScalarGridSpec(
-            num_scalar_prefetch=1,
-            grid=(1,),
-            in_specs=[INSIDE] * 4,
-            out_specs=[full(grad), full(pack)],
-            scratch_shapes=[pltpu.VMEM((16, combined.shape[0]), f32)],
-        ),
-        out_shape=[grad, pack],
+        cut = slice(k * 128, (k + 1) * 128)
+        total = arrived_ref[0, :, cut].astype(f32)
+        for p in range(1, peers):
+            total += arrived_ref[p, :, cut].astype(f32)
+        part = own_up * pack_ref[16 + k : 17 + k, :] - own_down * total
+        grad_ref[:, cut] = part.astype(bf16)
+
+
+def hidden_gradient(spot, arrived, pack):
+    peers, rows, units = arrived.shape
+    return pl.pallas_call(
+        hidden_kernel,
+        grid=(1,),
+        in_specs=[pl.BlockSpec(memory_space=pltpu.SMEM), pl.BlockSpec(arrived.shape, lambda i: (0, 0, 0)), INSIDE],
+        out_specs=INSIDE,
+        out_shape=jax.ShapeDtypeStruct((rows, units), bf16),
         compiler_params=kernel_params(),
         cost_estimate=pl.CostEstimate(
             flops=4 * arrived.size, bytes_accessed=2 * arrived.size, transcendentals=0
         ),
-        name="token_terms",
-    )(spot.reshape(1), *near(arrived), old, returns, *near(combined))
+        name="hidden_gradient",
+    )(spot.reshape(1), arrived, pack)
 
 
 def weight_kernel(
-    own_hidden_ref, other_hidden_ref, own_pack_ref, other_pack_ref, own_ref, other_ref, scale_ref,
-    out_ref, loss_ref, rows_ref,
+    own_pack_ref, other_pack_ref, own_ref, other_ref, scale_ref, hidden_ref, other_hidden_ref,
+    out_ref, loss_ref, held_ref, rows_ref, result_ref, in_sems, out_sems,
 ):
     tokens, width = own_ref.shape
-
-    @pl.when(pl.program_id(0) == 0)
-    def _():
-        loss_ref[0, 0] = jnp.max(own_pack_ref[12:13, :]) + jnp.max(other_pack_ref[12:13, :])
-        packs = jnp.concatenate(
-            [own_pack_ref[...], other_pack_ref[...], jnp.zeros((96, 128), f32)], axis=0
+    parts, units = result_ref.shape[:2]
+    sources = (hidden_ref, other_hidden_ref)
+
+    def fetch(s):
+        return pltpu.make_async_copy(sources[s], held_ref.at[s], in_sems.at[s])
+
+    def send(j):
+        part = out_ref.at[j * units : (j + 1) * units, :]
+        return pltpu.make_async_copy(result_ref.at[j], part, out_sems.at[j])
+
+    for s in range(2):
+        fetch(s).start()
+    loss_ref[0, 0] = jnp.max(own_pack_ref[12:13, :]) + jnp.max(other_pack_ref[12:13, :])
+    packs = jnp.concatenate(
+        [own_pack_ref[0:16, :], other_pack_ref[0:16, :], jnp.zeros((96, 128), f32)], axis=0
+    )
+    columns = jnp.transpose(packs)
+    for s, part_ref in enumerate((own_ref, other_ref)):
+        for r in range(tokens // 128):
+            up = columns[:, 16 * s + r : 16 * s + r + 1]
+            down = columns[:, 16 * s + 4 + r : 16 * s + 5 + r]
+            part = part_ref[r * 128 : (r + 1) * 128, :].astype(f32)
+            line = up * scale_ref[0:1, :] - down * part
+            rows_ref[s * tokens + r * 128 : s * tokens + (r + 1) * 128, :] = line.astype(bf16)
+    for s in range(2):
+        fetch(s).wait()
+    for j in range(parts):
+        cut = slice(j * units, (j + 1) * units)
+        result_ref[j] = lax.dot_general(
+            held_ref[0, :, cut], rows_ref[:tokens, :], TN, preferred_element_type=f32
+        ) + lax.dot_general(
+            held_ref[1, :, cut], rows_ref[tokens:, :], TN, preferred_element_type=f32
         )
-        columns = jnp.transpose(packs)
-        for s, part_ref in enumerate((own_ref, other_ref)):
-            for r in range(tokens // 128):
-                up = columns[:, 16 * s + r : 16 * s + r + 1]
-                down = columns[:, 16 * s + 4 + r : 16 * s + 5 + r]
-                part = part_ref[r * 128 : (r + 1) * 128, :].astype(f32)
-                line = up * scale_ref[0:1, :] - down * part
-                rows_ref[s * tokens + r * 128 : s * tokens + (r + 1) * 128, :] = line.astype(bf16)
-
-    block = out_ref.shape[0]
-    part = pl.ds(pl.multiple_of(pl.program_id(0) * block, block), block)
-    out_ref[...] = lax.dot_general(
-        own_hidden_ref[:, part], rows_ref[:tokens, :], TN, preferred_element_type=f32
-    ) + lax.dot_general(
-        other_hidden_ref[:, part], rows_ref[tokens:, :], TN, preferred_element_type=f32
-    )
-
-
-def weight_gradient(own_hidden, other_hidden, own_pack, other_pack, own, other, scale):
-    tokens, units = own_hidden.shape
+        send(j).start()
+    for j in range(parts):
+        send(j).wait()
+
+
+def weight_gradient(own_pack, other_pack, own, other, scale, hidden, other_hidden):
+    tokens, units = hidden.shape
     width = own.shape[1]
-    block = units // 2
+    parts = 2
     return pl.pallas_call(
         weight_kernel,
-        grid=(units // block,),
-        in_specs=[INSIDE] * 7,
-        out_specs=[
-            pl.BlockSpec((block, width), lambda i: (i, 0)),
-            pl.BlockSpec(memory_space=pltpu.SMEM),
+        in_specs=[INSIDE] * 5 + [OUTSIDE] * 2,
+        out_specs=[pl.BlockSpec(memory_space=pltpu.HBM), pl.BlockSpec(memory_space=pltpu.SMEM)],
+        out_shape=[pltpu.HBM((units, width), f32), jax.ShapeDtypeStruct((1, 1), f32)],
+        scratch_shapes=[
+            pltpu.VMEM((2, tokens, units), bf16),
+            pltpu.VMEM((2 * tokens, width), bf16),
+            pltpu.VMEM((parts, units // parts, width), f32),
+            pltpu.SemaphoreType.DMA((2,)),
+            pltpu.SemaphoreType.DMA((parts,)),
         ],
-        out_shape=[
-            jax.ShapeDtypeStruct((units, width), f32),
-            jax.ShapeDtypeStruct((1, 1), f32),
-        ],
-        scratch_shapes=[pltpu.VMEM((2 * tokens, width), bf16)],
         compiler_params=kernel_params(),
         cost_estimate=pl.CostEstimate(
             flops=4 * units * tokens * width, bytes_accessed=8 * units * width, transcendentals=0
         ),
         name="weight_gradient",
-    )(*near(own_hidden, other_hidden), own_pack, other_pack, *near(own, other), scale)
+    )(own_pack, other_pack, own, other, scale, far(hidden), far(other_hidden))
 
 
 def neighbours():
@@ -339,7 +404,7 @@
     section_rows = 8 * rows_each
 
     hidden = lax.all_to_all(spread(hidden_act, 16), PLANE, 0, 0, tiled=True)
-    other_weight = lax.ppermute(down_weight, "core", SWAP)
+    other_weight = hold(lax.ppermute(down_weight, "core", SWAP))
 
     chip_scale = lax.dynamic_slice_in_dim(gain * head_weight, yh * chip, chip, 0)
     own_scale = lax.dynamic_slice_in_dim(chip_scale, core * width, width, 0)
@@ -371,40 +436,44 @@
     )
     returns = own_old + returns_of(behavior, frozen, old_values, judge_ratings, lengths, token)
     returns, own_old = returns.reshape(4, 128), own_old.reshape(4, 128)
-    hidden, returns, own_old = lax.optimization_barrier((hidden, returns, own_old))
+    hidden, returns, own_old, other_weight = lax.optimization_barrier(
+        (hidden, returns, own_old, other_weight)
+    )
 
     away = forward(hidden, down_weight, other_weight, 1 - parity, bf16)
     met = lax.ppermute(away, ("core", "zh", "zl"), neighbours())
     kept_half = forward(hidden, down_weight, other_weight, parity, f32)
+    hidden, kept_half = lax.optimization_barrier((hidden.reshape(group, units), kept_half))
+    far_hidden = lax.ppermute(hidden, "core", SWAP)
     pair = (kept_half + met.astype(f32)).astype(bf16)
     parts = lax.all_to_all(pair.reshape(8, rows_each, chip), "zh", 0, 0, tiled=True)
     combined = (jnp.sum(parts.astype(f32), axis=0) + stream.astype(f32)).astype(bf16)
     combined = lax.all_gather(combined, ("zh", "zl"), axis=0, tiled=True)
     own_columns, other_columns = combined[:, :width], combined[:, width:]
 
-    payload = back(combined, down_weight, other_weight, scale_rows, base, 16)
+    sums = token_sums(combined, scale_rows, base, 16)
+    sums = lax.all_to_all(sums, PLANE, 0, 0, tiled=True)
+    payload = back(combined, down_weight, other_weight, 16)
+    sums, payload = lax.optimization_barrier((sums, payload))
     arrived = lax.all_to_all(payload, PLANE, 0, 0, tiled=True)
     far_columns = lax.ppermute(other_columns, "core", SWAP)
-    hidden = hidden.reshape(group, units)
-    far_hidden = lax.ppermute(hidden, "core", SWAP)
-    arrived, far_columns, far_hidden = lax.optimization_barrier((arrived, far_columns, far_hidden))
-
-    hidden_grad, pack = token_terms(spot, arrived, own_old, returns, combined, units)
+    pack = token_terms(sums, own_old, returns, combined)
+    hidden_grad = hidden_gradient(spot, arrived, pack)
     other_pack = lax.ppermute(pack, "core", SWAP)
+    weight_grad, total_loss = weight_gradient(
+        pack, other_pack, own_columns, far_columns, own_scale.reshape(1, -1), hidden, far_hidden
+    )
     own_head = pack[8:10] + other_pack[10:12]
     other_head = pack[10:12] + other_pack[8:10]
     head_chip = jnp.concatenate(
         [jnp.where(core == 0, own_head, other_head), jnp.where(core == 0, other_head, own_head)]
     )
     head_far = lax.ppermute(head_chip, "yh", SWAP)
+    head_far, total_loss = lax.optimization_barrier((head_far, total_loss))
     head_sum = jnp.concatenate(
         [jnp.where(yh == 0, head_chip, head_far), jnp.where(yh == 0, head_far, head_chip)]
     )
     head_grad = gain * head_sum.reshape(-1)
-
-    weight_grad, total_loss = weight_gradient(
-        hidden, far_hidden, pack, other_pack, own_columns, far_columns, own_scale.reshape(1, -1)
-    )
     return (total_loss[0, 0], head_grad, weight_grad, hidden_grad)
 
 

time: 158 us -> 153 us (0.968)
  starting transfers between devices: 79.4 us -> 74.9 us
  waiting for transfers between devices: 29.3 us -> 26.2 us
  local copies, waits for them, and re-layouts: 2.17 us -> 4.02 us
    ppermute x1, starting transfers between devices: 12.4 us -> 3.27 us  [on_device(): far_hidden = lax.ppermute(hidden, 'core', SWAP)]
    all_to_all x0 -> x1, starting transfers between devices: none -> 3.52 us  [on_device(): sums = lax.all_to_all(sums, PLANE, 0, 0, tiled=True)]
    all_to_all x1, waiting for transfers between devices: 14.3 us -> 11 us  [on_device(): lax.all_to_all(pair.reshape(8, rows_each, chip), 'zh', 0, 0, tiled=True)]
    all_to_all x0 -> x1, waiting for transfers between devices: none -> 3.17 us  [on_device(): sums = lax.all_to_all(sums, PLANE, 0, 0, tiled=True)]
    pallas_call x3 -> x6, Pallas kernels: 10.6 us -> 13.5 us  [the longest x1 4.98 us: weight_gradient(): pl.pallas_call(weight_kernel, in_specs=[INSIDE] * 5 + [OUTSIDE] * 2, out_...]
    pallas_call x2, Pallas kernels: 3.64 us -> 1.27 us  [forward(): pl.pallas_call(forward_kernel, in_specs=[pl.BlockSpec(memory_space=pltpu....]
    unnamed x18 -> x22, local copies, waits for them, and re-layouts: 0.94 us -> 2.79 us
    ppermute x1, waiting for transfers between devices: 1.78 us -> 0.01 us  [on_device(): far_columns = lax.ppermute(other_columns, 'core', SWAP)]
  transfers between devices with their start and end apart: 10 -> 11, of which waited for: 6 -> 4; matrix products, arithmetic and copies ran while one was open for 4% -> 5% of each run, Pallas kernels for 5% -> 8%
where the time goes in v4:
time: 153 us; the launch traced here: 152 us
  starting transfers between devices  74.9 us (49%)
  waiting for transfers between devices  26.2 us (17%)
  blocking collectives  23.8 us (16%)
  Pallas kernels  16.3 us (11%)
  other arithmetic  4.19 us (3%)
  local copies, waits for them, and re-layouts  4.02 us (3%)
  matrix products  1.95 us (1%)
    all_gather x1, blocking collectives, on_device(): combined = lax.all_gather(combined, ('zh', 'zl'), axis=0, tiled=True)  23.8 us
    ppermute x1, starting transfers between devices, on_device(): met = lax.ppermute(away, ('core', 'zh', 'zl'), neighbours())  15.8 us
    ppermute x1, starting transfers between devices, on_device(): other_pack = lax.ppermute(pack, 'core', SWAP)  15.1 us
    all_to_all x1, waiting for transfers between devices, on_device(): lax.all_to_all(pair.reshape(8, rows_each, chip), 'zh', 0, 0, tiled=True)  11 us
    all_to_all x1, waiting for transfers between devices, on_device(): hidden = lax.all_to_all(spread(hidden_act, 16), PLANE, 0, 0, tiled=True)  8.97 us
    all_to_all x1, starting transfers between devices, on_device(): lax.all_to_all(pair.reshape(8, rows_each, chip), 'zh', 0, 0, tiled=True)  8.26 us
    all_to_all x1, starting transfers between devices, on_device(): hidden = lax.all_to_all(spread(hidden_act, 16), PLANE, 0, 0, tiled=True)  7.73 us
    ppermute x1, starting transfers between devices, on_device(): stream = jnp.where(yh == z // 8, mine, lax.ppermute(sent, 'yh', SWAP))  5.01 us
  transfers between devices with their start and end apart: 11, of which 4 were waited for; matrix products, arithmetic and copies ran while one was open for 5% of the time, Pallas kernels for 8%

profile of v4, /device:TPU:1, one launch (start us, length us, event | category | flops | bytes accessed | tf_op | source)
XLA Modules:
  0.0 152.4 jit_solution(13720054240615979986)
XLA Ops:
  1.5 1.5 spread.1
  3.1 7.7 %all-to-all-start = ((bf16[16,32,1792]{2,1,0:T(8,128)(2,1)}), bf16[16,32,1792]{2,1,0:T(8,128)(2,1)S(1)}, u32[]{:S(2)}, u32[]{:S(2)}) async-start(bf16[16,32,1792]{2,1,0:T(8,128)(2,1)} %spread.1), calls=%async_computation | async-start | bytes 3670016 | tf_op jit(solution)/shard_map/all_to_all | solution.py:406
  10.9 4.9 %collective-permute-start = (bf16[1792,256]{1,0:T(8,128)(2,1)S(1)}, bf16[1792,256]{1,0:T(8,128)(2,1)}, u32[]{:S(2)}, u32[]{:S(2)}) collective-permute-start(bf16[1792,256]{1,0:T(8,128)(2,1)S(1)} %copy-done.1), channel_id=1, source_target_pairs={{0,128},{128,0},{1,129},{129,1},{2,130},{130,2},{3,131},{131,3},{4... | collective-permute-start | bytes 2752520 | tf_op jit(solution)/shard_map/ppermute | solution.py:407
  16.7 5.0 %collective-permute-start.2 = (bf16[32,512]{1,0:T(8,128)(2,1)S(1)}, bf16[32,512]{1,0:T(8,128)(2,1)S(1)}, u32[]{:S(2)}, u32[]{:S(2)}) collective-permute-start(bf16[32,512]{1,0:T(8,128)(2,1)S(1)} %dynamic_slice.27), channel_id=1, source_target_pairs={{0,256},{256,0},{1,257},{257,1},{2,258},{258,2},{3,259},{259,3},{4... | collective-permute-start | bytes 98312 | tf_op jit(solution)/shard_map/ppermute | solution.py:417
  23.8 1.2 hold.1.other_ref
  25.0 9.0 %all-to-all-done = bf16[16,32,1792]{2,1,0:T(8,128)(2,1)S(1)} async-done(((bf16[16,32,1792]{2,1,0:T(8,128)(2,1)}), bf16[16,32,1792]{2,1,0:T(8,128)(2,1)S(1)}, u32[]{:S(2)}, u32[]{:S(2)}) %all-to-all-start) | async-done | bytes 1835040 | tf_op jit(solution)/shard_map/all_to_all | solution.py:406
  34.0 1.8 %copy-done.2 = bf16[1792,256]{1,0:T(8,128)(2,1)S(1)} copy-done((bf16[1792,256]{1,0:T(8,128)(2,1)S(1)}, bf16[1792,256]{1,0:T(8,128)(2,1)}, u32[]{:S(2)}) %copy-start.2) | copy-done | bytes 917528
  36.5 15.8 %collective-permute-start.1 = (bf16[256,512]{1,0:T(8,128)(2,1)S(1)}, bf16[256,512]{1,0:T(8,128)(2,1)S(1)}, u32[]{:S(2)}, u32[]{:S(2)}) collective-permute-start(bf16[256,512]{1,0:T(8,128)(2,1)S(1)} %forward.3), channel_id=1, source_target_pairs={{0,1},{1,0},{2,3},{3,2},{4,5},{5,4},{6,7},{7,6},{8,9},{9,8},{10,11... | collective-permute-start | bytes 786440 | tf_op jit(solution)/shard_map/ppermute | solution.py:444
  53.0 3.0 %collective-permute-done.1 = bf16[256,512]{1,0:T(8,128)(2,1)S(1)} collective-permute-done((bf16[256,512]{1,0:T(8,128)(2,1)S(1)}, bf16[256,512]{1,0:T(8,128)(2,1)S(1)}, u32[]{:S(2)}, u32[]{:S(2)}) %collective-permute-start.1) | collective-permute-done | bytes 262176 | tf_op jit(solution)/shard_map/ppermute | solution.py:444
  56.8 8.3 %all-to-all-start.1 = ((bf16[8,32,512]{2,1,0:T(8,128)(2,1)}), bf16[8,32,512]{2,1,0:T(8,128)(2,1)S(1)}, u32[]{:S(2)}, u32[]{:S(2)}) async-start(bf16[8,32,512]{2,1,0:T(8,128)(2,1)} %bitcast.8), calls=%async_computation.1 | async-start | bytes 524288 | tf_op jit(solution)/shard_map/all_to_all | solution.py:449
  65.1 1.5 %fusion.10 = f32[16,1792]{1,0:T(8,128)S(1)} fusion(bf16[1792,256]{1,0:T(8,128)(2,1)} %outer_ref.1, bf16[16,512]{1,0:T(8,128)(2,1)S(1)} %fusion.8.scale_ref), kind=kOutput, calls=%fused_computation.25 | convolution fusion | flops 14680064 | bytes 1040384 | tf_op jit(solution)/shard_map/dot_general | solution.py:424
  68.0 3.3 %collective-permute-start.6 = (bf16[512,1792]{1,0:T(8,128)(2,1)S(1)}, bf16[512,1792]{1,0:T(8,128)(2,1)}, u32[]{:S(2)}, u32[]{:S(2)}) collective-permute-start(bf16[512,1792]{1,0:T(8,128)(2,1)S(1)} %bitcast.27), channel_id=1, source_target_pairs={{0,128},{128,0},{1,129},{129,1},{2,130},{130,2},{3,131},{131,3},{4... | collective-permute-start | bytes 5505032 | tf_op jit(solution)/shard_map/ppermute | solution.py:447
  71.3 11.0 %all-to-all-done.1 = bf16[8,32,512]{2,1,0:T(8,128)(2,1)S(1)} async-done(((bf16[8,32,512]{2,1,0:T(8,128)(2,1)}), bf16[8,32,512]{2,1,0:T(8,128)(2,1)S(1)}, u32[]{:S(2)}, u32[]{:S(2)}) %all-to-all-start.1) | async-done | bytes 262176 | tf_op jit(solution)/shard_map/all_to_all | solution.py:449
  82.3 23.8 %all_gather.3.combined_ref = bf16[512,512]{1,0:T(8,128)(2,1)S(1)} all-gather(bf16[32,512]{1,0:T(8,128)(2,1)S(1)} %add_convert_fusion.1), channel_id=1, replica_groups=mesh['yh'=2,'core'=2,'x'=4,'yl'=2,'zh'=8,'zl'=2] {'zh','zl'}, dimensions={0}, use_global_device_ids=true | all-gather | bytes 557056 | tf_op jit(solution)/shard_map/all_gather | solution.py:451
  106.1 1.2 token_sums.1
  107.4 3.5 %all-to-all-start.2 = ((bf16[16,32,128]{2,1,0:T(8,128)(2,1)}), bf16[16,32,128]{2,1,0:T(8,128)(2,1)S(1)}, u32[]{:S(2)}, u32[]{:S(2)}) async-start(bf16[16,32,128]{2,1,0:T(8,128)(2,1)} %token_sums.1), calls=%async_computation.2 | async-start | bytes 262144 | tf_op jit(solution)/shard_map/all_to_all | solution.py:455
  110.9 3.5 %back.1 = bf16[16,32,1792]{2,1,0:T(8,128)(2,1)} custom-call(bf16[512,512]{1,0:T(8,128)(2,1)S(1)} %all_gather.3.combined_ref, bf16[1792,256]{1,0:T(8,128)(2,1)} %outer_ref.1, bf16[1792,256]{1,0:T(8,128)(2,1)S(1)} %hold.1.other_ref), custom_call_target="tpu_custom_call" | custom-call | flops 939524096 | bytes 3670016 | tf_op jit(solution)/shard_map/back/pallas_call | solution.py:209
  114.4 3.2 %all-to-all-done.2.sums_ref = bf16[16,32,128]{2,1,0:T(8,128)(2,1)S(1)} async-done(((bf16[16,32,128]{2,1,0:T(8,128)(2,1)}), bf16[16,32,128]{2,1,0:T(8,128)(2,1)S(1)}, u32[]{:S(2)}, u32[]{:S(2)}) %all-to-all-start.2) | async-done | bytes 131104 | tf_op jit(solution)/shard_map/all_to_all | solution.py:455
  117.6 4.4 %all-to-all-start.3 = ((bf16[16,32,1792]{2,1,0:T(8,128)(2,1)}), bf16[16,32,1792]{2,1,0:T(8,128)(2,1)}, u32[]{:S(2)}, u32[]{:S(2)}) async-start(bf16[16,32,1792]{2,1,0:T(8,128)(2,1)} %back.1), calls=%async_computation.3 | async-start | bytes 3670016 | tf_op jit(solution)/shard_map/all_to_all | solution.py:458
  122.2 15.1 %collective-permute-start.3 = (f32[32,128]{1,0:T(8,128)S(1)}, f32[32,128]{1,0:T(8,128)S(1)}, u32[]{:S(2)}, u32[]{:S(2)}) collective-permute-start(f32[32,128]{1,0:T(8,128)S(1)} %token_terms.1.own_pack_ref.pack_ref), channel_id=1, source_target_pairs={{0,128},{128,0},{1,129},{129,1},{2,130},{130,2},{3,131},{131,3},{4... | collective-permute-start | bytes 49160 | tf_op jit(solution)/shard_map/ppermute | solution.py:462
  137.4 1.9 %collective-permute-start.5 = (bf16[512,256]{1,0:T(8,128)(2,1)S(1)}, bf16[512,256]{1,0:T(8,128)(2,1)S(1)}, u32[]{:S(2)}, u32[]{:S(2)}) collective-permute-start(bf16[512,256]{1,0:T(8,128)(2,1)S(1)} %get-tuple-element.28), channel_id=1, source_target_pairs={{0,128},{128,0},{1,129},{129,1},{2,130},{130,2},{3,131},{131,3},{4... | collective-permute-start | bytes 786440 | tf_op jit(solution)/shard_map/ppermute | solution.py:459
  139.4 4.9 %collective-permute-start.4 = (f32[4,128]{1,0:T(4,128)S(1)}, f32[4,128]{1,0:T(4,128)S(1)}, u32[]{:S(2)}, u32[]{:S(2)}) collective-permute-start(f32[4,128]{1,0:T(4,128)S(1)} %pad_maximum_fusion.2), channel_id=1, source_target_pairs={{0,256},{256,0},{1,257},{257,1},{2,258},{258,2},{3,259},{259,3},{4... | collective-permute-start | bytes 6152 | tf_op jit(solution)/shard_map/ppermute | solution.py:471
  144.4 5.0 %weight_gradient.1 = (f32[1792,256]{1,0:T(8,128)}, f32[1,1]{1,0:T(1,128)}) custom-call(f32[32,128]{1,0:T(8,128)S(1)} %token_terms.1.own_pack_ref.pack_ref, f32[32,128]{1,0:T(8,128)S(1)} %collective-permute-done.3.other_pack_ref, bf16[512,256]{1,0:T(8,128)(2,1)S(1)} %get-tuple-element.29.own_ref, bf16[512,256]{1,0:T(8,128)(2,1)S(1)} %collective-permute-done.5.other_ref, ...), custom_call_target="tpu_custom_call" | custom-call | flops 939524096 | bytes 3670016 | tf_op jit(solution)/shard_map/weight_gradient/pallas_call | solution.py:359
  150.0 2.4 %hidden_gradient.1 = bf16[32,1792]{1,0:T(8,128)(2,1)} custom-call(s32[1]{0:T(128)} %bitcast.14.spot_ref, bf16[16,32,1792]{2,1,0:T(8,128)(2,1)} %all-to-all-done.3.arrived_ref, f32[32,128]{1,0:T(8,128)S(1)} %token_terms.1.own_pack_ref.pack_ref), custom_call_target="tpu_custom_call" | custom-call | flops 3670016 | bytes 1835008 | tf_op jit(solution)/shard_map/hidden_gradient/pallas_call | solution.py:298
  (62 shorter events, 8.3 us)
Async XLA Ops:
  0.6 0.9 copy-start.3
  3.0 7.8 %copy-start.1 = (bf16[1792,256]{1,0:T(8,128)(2,1)S(1)}, bf16[1792,256]{1,0:T(8,128)(2,1)}, u32[]{:S(2)}) copy-start(bf16[1792,256]{1,0:T(8,128)(2,1)} %outer_ref.1) | copy-start | bytes 2752516
  3.0 18.7 %copy-start.9 = (s32[16]{0:T(128)S(1)}, s32[16]{0:T(128)}, u32[]{:S(2)}) copy-start(s32[16]{0:T(128)} %param.19) | copy-start | bytes 196
  3.0 18.9 %copy-start.4 = (f32[1024]{0:T(1024)S(1)}, f32[1024]{0:T(1024)}, u32[]{:S(2)}) copy-start(f32[1024]{0:T(1024)} %param.17) | copy-start | bytes 12292
  3.0 19.3 %copy-start.5 = (f32[1024]{0:T(1024)S(1)}, f32[1024]{0:T(1024)}, u32[]{:S(2)}) copy-start(f32[1024]{0:T(1024)} %param.14) | copy-start | bytes 12292
  3.1 19.3 %copy-start.6 = (f32[1024]{0:T(1024)S(1)}, f32[1024]{0:T(1024)}, u32[]{:S(2)}) copy-start(f32[1024]{0:T(1024)} %param.13) | copy-start | bytes 12292
  3.1 19.4 %copy-start.10 = (f32[16]{0:T(128)S(1)}, f32[16]{0:T(128)}, u32[]{:S(2)}) copy-start(f32[16]{0:T(128)} %param.18) | copy-start | bytes 196
  3.1 19.5 %copy-start.7 = (f32[1024]{0:T(1024)S(1)}, f32[1024]{0:T(1024)}, u32[]{:S(2)}) copy-start(f32[1024]{0:T(1024)} %param.15) | copy-start | bytes 12292
  3.1 19.5 %copy-start.8 = (f32[1024]{0:T(1024)S(1)}, f32[1024]{0:T(1024)}, u32[]{:S(2)}) copy-start(f32[1024]{0:T(1024)} %param.16) | copy-start | bytes 12292
  3.1 30.9 %all-to-all-start = ((bf16[16,32,1792]{2,1,0:T(8,128)(2,1)}), bf16[16,32,1792]{2,1,0:T(8,128)(2,1)S(1)}, u32[]{:S(2)}, u32[]{:S(2)}) async-start(bf16[16,32,1792]{2,1,0:T(8,128)(2,1)} %spread.1), calls=%async_computation | async-start | bytes 3670016 | tf_op jit(solution)/shard_map/all_to_all | solution.py:406
  10.9 13.0 %collective-permute-start = (bf16[1792,256]{1,0:T(8,128)(2,1)S(1)}, bf16[1792,256]{1,0:T(8,128)(2,1)}, u32[]{:S(2)}, u32[]{:S(2)}) collective-permute-start(bf16[1792,256]{1,0:T(8,128)(2,1)S(1)} %copy-done.1), channel_id=1, source_target_pairs={{0,128},{128,0},{1,129},{129,1},{2,130},{130,2},{3,131},{131,3},{4... | collective-permute-start | bytes 2752520 | tf_op jit(solution)/shard_map/ppermute | solution.py:407
  16.7 49.9 %collective-permute-start.2 = (bf16[32,512]{1,0:T(8,128)(2,1)S(1)}, bf16[32,512]{1,0:T(8,128)(2,1)S(1)}, u32[]{:S(2)}, u32[]{:S(2)}) collective-permute-start(bf16[32,512]{1,0:T(8,128)(2,1)S(1)} %dynamic_slice.27), channel_id=1, source_target_pairs={{0,256},{256,0},{1,257},{257,1},{2,258},{258,2},{3,259},{259,3},{4... | collective-permute-start | bytes 98312 | tf_op jit(solution)/shard_map/ppermute | solution.py:417
  34.0 34.0 %copy-start = (bf16[16,32,1792]{2,1,0:T(8,128)(2,1)}, bf16[16,32,1792]{2,1,0:T(8,128)(2,1)S(1)}, u32[]{:S(2)}) copy-start(bf16[16,32,1792]{2,1,0:T(8,128)(2,1)S(1)} %all-to-all-done) | copy-start | bytes 5505028
  34.0 1.8 %copy-start.2 = (bf16[1792,256]{1,0:T(8,128)(2,1)S(1)}, bf16[1792,256]{1,0:T(8,128)(2,1)}, u32[]{:S(2)}) copy-start(bf16[1792,256]{1,0:T(8,128)(2,1)} %outer_ref.1) | copy-start | bytes 2752516
  36.5 19.5 %collective-permute-start.1 = (bf16[256,512]{1,0:T(8,128)(2,1)S(1)}, bf16[256,512]{1,0:T(8,128)(2,1)S(1)}, u32[]{:S(2)}, u32[]{:S(2)}) collective-permute-start(bf16[256,512]{1,0:T(8,128)(2,1)S(1)} %forward.3), channel_id=1, source_target_pairs={{0,1},{1,0},{2,3},{3,2},{4,5},{5,4},{6,7},{7,6},{8,9},{9,8},{10,11... | collective-permute-start | bytes 786440 | tf_op jit(solution)/shard_map/ppermute | solution.py:444
  56.8 25.5 %all-to-all-start.1 = ((bf16[8,32,512]{2,1,0:T(8,128)(2,1)}), bf16[8,32,512]{2,1,0:T(8,128)(2,1)S(1)}, u32[]{:S(2)}, u32[]{:S(2)}) async-start(bf16[8,32,512]{2,1,0:T(8,128)(2,1)} %bitcast.8), calls=%async_computation.1 | async-start | bytes 524288 | tf_op jit(solution)/shard_map/all_to_all | solution.py:449
  68.0 76.4 %collective-permute-start.6 = (bf16[512,1792]{1,0:T(8,128)(2,1)S(1)}, bf16[512,1792]{1,0:T(8,128)(2,1)}, u32[]{:S(2)}, u32[]{:S(2)}) collective-permute-start(bf16[512,1792]{1,0:T(8,128)(2,1)S(1)} %bitcast.27), channel_id=1, source_target_pairs={{0,128},{128,0},{1,129},{129,1},{2,130},{130,2},{3,131},{131,3},{4... | collective-permute-start | bytes 5505032 | tf_op jit(solution)/shard_map/ppermute | solution.py:447
  107.4 10.2 %all-to-all-start.2 = ((bf16[16,32,128]{2,1,0:T(8,128)(2,1)}), bf16[16,32,128]{2,1,0:T(8,128)(2,1)S(1)}, u32[]{:S(2)}, u32[]{:S(2)}) async-start(bf16[16,32,128]{2,1,0:T(8,128)(2,1)} %token_sums.1), calls=%async_computation.2 | async-start | bytes 262144 | tf_op jit(solution)/shard_map/all_to_all | solution.py:455
  117.6 32.4 %all-to-all-start.3 = ((bf16[16,32,1792]{2,1,0:T(8,128)(2,1)}), bf16[16,32,1792]{2,1,0:T(8,128)(2,1)}, u32[]{:S(2)}, u32[]{:S(2)}) async-start(bf16[16,32,1792]{2,1,0:T(8,128)(2,1)} %back.1), calls=%async_computation.3 | async-start | bytes 3670016 | tf_op jit(solution)/shard_map/all_to_all | solution.py:458
  122.2 17.1 %collective-permute-start.3 = (f32[32,128]{1,0:T(8,128)S(1)}, f32[32,128]{1,0:T(8,128)S(1)}, u32[]{:S(2)}, u32[]{:S(2)}) collective-permute-start(f32[32,128]{1,0:T(8,128)S(1)} %token_terms.1.own_pack_ref.pack_ref), channel_id=1, source_target_pairs={{0,128},{128,0},{1,129},{129,1},{2,130},{130,2},{3,131},{131,3},{4... | collective-permute-start | bytes 49160 | tf_op jit(solution)/shard_map/ppermute | solution.py:462
  137.4 6.9 %collective-permute-start.5 = (bf16[512,256]{1,0:T(8,128)(2,1)S(1)}, bf16[512,256]{1,0:T(8,128)(2,1)S(1)}, u32[]{:S(2)}, u32[]{:S(2)}) collective-permute-start(bf16[512,256]{1,0:T(8,128)(2,1)S(1)} %get-tuple-element.28), channel_id=1, source_target_pairs={{0,128},{128,0},{1,129},{129,1},{2,130},{130,2},{3,131},{131,3},{4... | collective-permute-start | bytes 786440 | tf_op jit(solution)/shard_map/ppermute | solution.py:459
  139.4 9.9 %collective-permute-start.4 = (f32[4,128]{1,0:T(4,128)S(1)}, f32[4,128]{1,0:T(4,128)S(1)}, u32[]{:S(2)}, u32[]{:S(2)}) collective-permute-start(f32[4,128]{1,0:T(4,128)S(1)} %pad_maximum_fusion.2), channel_id=1, source_target_pairs={{0,256},{256,0},{1,257},{257,1},{2,258},{258,2},{3,259},{259,3},{4... | collective-permute-start | bytes 6152 | tf_op jit(solution)/shard_map/ppermute | solution.py:471

commit v5 on v4

--- a/solution.py
+++ b/solution.py
@@ -373,7 +373,7 @@
             flops=4 * units * tokens * width, bytes_accessed=8 * units * width, transcendentals=0
         ),
         name="weight_gradient",
-    )(own_pack, other_pack, own, other, scale, far(hidden), far(other_hidden))
+    )(own_pack, other_pack, own, other, scale, hidden, other_hidden)
 
 
 def neighbours():

time: 153 us -> 153 us (level)
  no operation moved by 1% of the time
where the time goes in v5:
time: 153 us; the launch traced here: 151 us
  starting transfers between devices  74.9 us (49%)
  waiting for transfers between devices  26.2 us (17%)
  blocking collectives  23.8 us (16%)
  Pallas kernels  15.8 us (10%)
  other arithmetic  4.19 us (3%)
  local copies, waits for them, and re-layouts  3.35 us (2%)
  matrix products  1.95 us (1%)
    all_gather x1, blocking collectives, on_device(): combined = lax.all_gather(combined, ('zh', 'zl'), axis=0, tiled=True)  23.8 us
    ppermute x1, starting transfers between devices, on_device(): met = lax.ppermute(away, ('core', 'zh', 'zl'), neighbours())  15.8 us
    ppermute x1, starting transfers between devices, on_device(): other_pack = lax.ppermute(pack, 'core', SWAP)  15.2 us
    all_to_all x1, waiting for transfers between devices, on_device(): lax.all_to_all(pair.reshape(8, rows_each, chip), 'zh', 0, 0, tiled=True)  11 us
    all_to_all x1, waiting for transfers between devices, on_device(): hidden = lax.all_to_all(spread(hidden_act, 16), PLANE, 0, 0, tiled=True)  8.97 us
    all_to_all x1, starting transfers between devices, on_device(): lax.all_to_all(pair.reshape(8, rows_each, chip), 'zh', 0, 0, tiled=True)  8.26 us
    all_to_all x1, starting transfers between devices, on_device(): hidden = lax.all_to_all(spread(hidden_act, 16), PLANE, 0, 0, tiled=True)  7.73 us
    ppermute x1, starting transfers between devices, on_device(): stream = jnp.where(yh == z // 8, mine, lax.ppermute(sent, 'yh', SWAP))  5.01 us
  transfers between devices with their start and end apart: 11, of which 4 were waited for; matrix products, arithmetic and copies ran while one was open for 5% of the time, Pallas kernels for 8%

profile of v5, /device:TPU:1, one launch (start us, length us, event | category | flops | bytes accessed | tf_op | source)
XLA Modules:
  0.0 151.3 jit_solution(3287982678309837153)
XLA Ops:
  1.5 1.5 spread.1
  3.1 7.7 %all-to-all-start = ((bf16[16,32,1792]{2,1,0:T(8,128)(2,1)}), bf16[16,32,1792]{2,1,0:T(8,128)(2,1)S(1)}, u32[]{:S(2)}, u32[]{:S(2)}) async-start(bf16[16,32,1792]{2,1,0:T(8,128)(2,1)} %spread.1), calls=%async_computation | async-start | bytes 3670016 | tf_op jit(solution)/shard_map/all_to_all | solution.py:406
  10.9 4.9 %collective-permute-start = (bf16[1792,256]{1,0:T(8,128)(2,1)S(1)}, bf16[1792,256]{1,0:T(8,128)(2,1)}, u32[]{:S(2)}, u32[]{:S(2)}) collective-permute-start(bf16[1792,256]{1,0:T(8,128)(2,1)S(1)} %copy-done), channel_id=1, source_target_pairs={{0,128},{128,0},{1,129},{129,1},{2,130},{130,2},{3,131},{131,3},{4... | collective-permute-start | bytes 2752520 | tf_op jit(solution)/shard_map/ppermute | solution.py:407
  16.7 5.0 %collective-permute-start.2 = (bf16[32,512]{1,0:T(8,128)(2,1)S(1)}, bf16[32,512]{1,0:T(8,128)(2,1)S(1)}, u32[]{:S(2)}, u32[]{:S(2)}) collective-permute-start(bf16[32,512]{1,0:T(8,128)(2,1)S(1)} %dynamic_slice.27), channel_id=1, source_target_pairs={{0,256},{256,0},{1,257},{257,1},{2,258},{258,2},{3,259},{259,3},{4... | collective-permute-start | bytes 98312 | tf_op jit(solution)/shard_map/ppermute | solution.py:417
  22.6 1.2 multiply_reduce_fusion
  23.8 1.2 hold.1.other_ref
  25.0 9.0 %all-to-all-done = bf16[16,32,1792]{2,1,0:T(8,128)(2,1)S(1)} async-done(((bf16[16,32,1792]{2,1,0:T(8,128)(2,1)}), bf16[16,32,1792]{2,1,0:T(8,128)(2,1)S(1)}, u32[]{:S(2)}, u32[]{:S(2)}) %all-to-all-start) | async-done | bytes 1835040 | tf_op jit(solution)/shard_map/all_to_all | solution.py:406
  35.8 15.8 %collective-permute-start.1 = (bf16[256,512]{1,0:T(8,128)(2,1)S(1)}, bf16[256,512]{1,0:T(8,128)(2,1)S(1)}, u32[]{:S(2)}, u32[]{:S(2)}) collective-permute-start(bf16[256,512]{1,0:T(8,128)(2,1)S(1)} %forward.3), channel_id=1, source_target_pairs={{0,1},{1,0},{2,3},{3,2},{4,5},{5,4},{6,7},{7,6},{8,9},{9,8},{10,11... | collective-permute-start | bytes 786440 | tf_op jit(solution)/shard_map/ppermute | solution.py:444
  52.3 3.0 %collective-permute-done.1 = bf16[256,512]{1,0:T(8,128)(2,1)S(1)} collective-permute-done((bf16[256,512]{1,0:T(8,128)(2,1)S(1)}, bf16[256,512]{1,0:T(8,128)(2,1)S(1)}, u32[]{:S(2)}, u32[]{:S(2)}) %collective-permute-start.1) | collective-permute-done | bytes 262176 | tf_op jit(solution)/shard_map/ppermute | solution.py:444
  56.1 8.3 %all-to-all-start.1 = ((bf16[8,32,512]{2,1,0:T(8,128)(2,1)}), bf16[8,32,512]{2,1,0:T(8,128)(2,1)S(1)}, u32[]{:S(2)}, u32[]{:S(2)}) async-start(bf16[8,32,512]{2,1,0:T(8,128)(2,1)} %bitcast.8), calls=%async_computation.1 | async-start | bytes 524288 | tf_op jit(solution)/shard_map/all_to_all | solution.py:449
  64.4 1.5 %fusion.10 = f32[16,1792]{1,0:T(8,128)S(1)} fusion(bf16[1792,256]{1,0:T(8,128)(2,1)} %outer_ref.1, bf16[16,512]{1,0:T(8,128)(2,1)S(1)} %fusion.8.scale_ref), kind=kOutput, calls=%fused_computation.25 | convolution fusion | flops 14680064 | bytes 1040384 | tf_op jit(solution)/shard_map/dot_general | solution.py:424
  67.3 3.3 %collective-permute-start.6 = (bf16[512,1792]{1,0:T(8,128)(2,1)S(1)}, bf16[512,1792]{1,0:T(8,128)(2,1)}, u32[]{:S(2)}, u32[]{:S(2)}) collective-permute-start(bf16[512,1792]{1,0:T(8,128)(2,1)S(1)} %bitcast.27), channel_id=1, source_target_pairs={{0,128},{128,0},{1,129},{129,1},{2,130},{130,2},{3,131},{131,3},{4... | collective-permute-start | bytes 5505032 | tf_op jit(solution)/shard_map/ppermute | solution.py:447
  70.6 11.0 %all-to-all-done.1 = bf16[8,32,512]{2,1,0:T(8,128)(2,1)S(1)} async-done(((bf16[8,32,512]{2,1,0:T(8,128)(2,1)}), bf16[8,32,512]{2,1,0:T(8,128)(2,1)S(1)}, u32[]{:S(2)}, u32[]{:S(2)}) %all-to-all-start.1) | async-done | bytes 262176 | tf_op jit(solution)/shard_map/all_to_all | solution.py:449
  81.6 23.8 %all_gather.3.combined_ref = bf16[512,512]{1,0:T(8,128)(2,1)S(1)} all-gather(bf16[32,512]{1,0:T(8,128)(2,1)S(1)} %add_convert_fusion.1), channel_id=1, replica_groups=mesh['yh'=2,'core'=2,'x'=4,'yl'=2,'zh'=8,'zl'=2] {'zh','zl'}, dimensions={0}, use_global_device_ids=true | all-gather | bytes 557056 | tf_op jit(solution)/shard_map/all_gather | solution.py:451
  105.5 1.2 token_sums.1
  106.7 3.5 %all-to-all-start.2 = ((bf16[16,32,128]{2,1,0:T(8,128)(2,1)}), bf16[16,32,128]{2,1,0:T(8,128)(2,1)S(1)}, u32[]{:S(2)}, u32[]{:S(2)}) async-start(bf16[16,32,128]{2,1,0:T(8,128)(2,1)} %token_sums.1), calls=%async_computation.2 | async-start | bytes 262144 | tf_op jit(solution)/shard_map/all_to_all | solution.py:455
  110.3 3.5 %back.1 = bf16[16,32,1792]{2,1,0:T(8,128)(2,1)} custom-call(bf16[512,512]{1,0:T(8,128)(2,1)S(1)} %all_gather.3.combined_ref, bf16[1792,256]{1,0:T(8,128)(2,1)} %outer_ref.1, bf16[1792,256]{1,0:T(8,128)(2,1)S(1)} %hold.1.other_ref), custom_call_target="tpu_custom_call" | custom-call | flops 939524096 | bytes 3670016 | tf_op jit(solution)/shard_map/back/pallas_call | solution.py:209
  113.7 3.2 %all-to-all-done.2.sums_ref = bf16[16,32,128]{2,1,0:T(8,128)(2,1)S(1)} async-done(((bf16[16,32,128]{2,1,0:T(8,128)(2,1)}), bf16[16,32,128]{2,1,0:T(8,128)(2,1)S(1)}, u32[]{:S(2)}, u32[]{:S(2)}) %all-to-all-start.2) | async-done | bytes 131104 | tf_op jit(solution)/shard_map/all_to_all | solution.py:455
  116.9 4.4 %all-to-all-start.3 = ((bf16[16,32,1792]{2,1,0:T(8,128)(2,1)}), bf16[16,32,1792]{2,1,0:T(8,128)(2,1)}, u32[]{:S(2)}, u32[]{:S(2)}) async-start(bf16[16,32,1792]{2,1,0:T(8,128)(2,1)} %back.1), calls=%async_computation.3 | async-start | bytes 3670016 | tf_op jit(solution)/shard_map/all_to_all | solution.py:458
  121.6 15.2 %collective-permute-start.3 = (f32[32,128]{1,0:T(8,128)S(1)}, f32[32,128]{1,0:T(8,128)S(1)}, u32[]{:S(2)}, u32[]{:S(2)}) collective-permute-start(f32[32,128]{1,0:T(8,128)S(1)} %token_terms.1.own_pack_ref.pack_ref), channel_id=1, source_target_pairs={{0,128},{128,0},{1,129},{129,1},{2,130},{130,2},{3,131},{131,3},{4... | collective-permute-start | bytes 49160 | tf_op jit(solution)/shard_map/ppermute | solution.py:462
  136.8 1.9 %collective-permute-start.5 = (bf16[512,256]{1,0:T(8,128)(2,1)S(1)}, bf16[512,256]{1,0:T(8,128)(2,1)S(1)}, u32[]{:S(2)}, u32[]{:S(2)}) collective-permute-start(bf16[512,256]{1,0:T(8,128)(2,1)S(1)} %get-tuple-element.28), channel_id=1, source_target_pairs={{0,128},{128,0},{1,129},{129,1},{2,130},{130,2},{3,131},{131,3},{4... | collective-permute-start | bytes 786440 | tf_op jit(solution)/shard_map/ppermute | solution.py:459
  138.8 4.9 %collective-permute-start.4 = (f32[4,128]{1,0:T(4,128)S(1)}, f32[4,128]{1,0:T(4,128)S(1)}, u32[]{:S(2)}, u32[]{:S(2)}) collective-permute-start(f32[4,128]{1,0:T(4,128)S(1)} %pad_maximum_fusion.2), channel_id=1, source_target_pairs={{0,256},{256,0},{1,257},{257,1},{2,258},{258,2},{3,259},{259,3},{4... | collective-permute-start | bytes 6152 | tf_op jit(solution)/shard_map/ppermute | solution.py:471
  143.7 4.5 %weight_gradient.1 = (f32[1792,256]{1,0:T(8,128)}, f32[1,1]{1,0:T(1,128)}) custom-call(f32[32,128]{1,0:T(8,128)S(1)} %token_terms.1.own_pack_ref.pack_ref, f32[32,128]{1,0:T(8,128)S(1)} %collective-permute-done.3.other_pack_ref, bf16[512,256]{1,0:T(8,128)(2,1)S(1)} %get-tuple-element.29.own_ref, bf16[512,256]{1,0:T(8,128)(2,1)S(1)} %collective-permute-done.5.other_ref, ...), custom_call_target="tpu_custom_call" | custom-call | flops 939524096 | bytes 3670016 | tf_op jit(solution)/shard_map/weight_gradient/pallas_call | solution.py:359
  148.9 2.4 %hidden_gradient.1 = bf16[32,1792]{1,0:T(8,128)(2,1)} custom-call(s32[1]{0:T(128)} %bitcast.14.spot_ref, bf16[16,32,1792]{2,1,0:T(8,128)(2,1)} %all-to-all-done.3.arrived_ref, f32[32,128]{1,0:T(8,128)S(1)} %token_terms.1.own_pack_ref.pack_ref), custom_call_target="tpu_custom_call" | custom-call | flops 3670016 | bytes 1835008 | tf_op jit(solution)/shard_map/hidden_gradient/pallas_call | solution.py:298
  (60 shorter events, 8.3 us)
Async XLA Ops:
  0.6 0.9 copy-start.2
  3.0 7.8 %copy-start = (bf16[1792,256]{1,0:T(8,128)(2,1)S(1)}, bf16[1792,256]{1,0:T(8,128)(2,1)}, u32[]{:S(2)}) copy-start(bf16[1792,256]{1,0:T(8,128)(2,1)} %outer_ref.1) | copy-start | bytes 2752516
  3.0 18.7 %copy-start.8 = (s32[16]{0:T(128)S(1)}, s32[16]{0:T(128)}, u32[]{:S(2)}) copy-start(s32[16]{0:T(128)} %param.19) | copy-start | bytes 196
  3.0 18.9 %copy-start.3 = (f32[1024]{0:T(1024)S(1)}, f32[1024]{0:T(1024)}, u32[]{:S(2)}) copy-start(f32[1024]{0:T(1024)} %param.17) | copy-start | bytes 12292
  3.0 19.3 %copy-start.4 = (f32[1024]{0:T(1024)S(1)}, f32[1024]{0:T(1024)}, u32[]{:S(2)}) copy-start(f32[1024]{0:T(1024)} %param.14) | copy-start | bytes 12292
  3.1 19.3 %copy-start.5 = (f32[1024]{0:T(1024)S(1)}, f32[1024]{0:T(1024)}, u32[]{:S(2)}) copy-start(f32[1024]{0:T(1024)} %param.13) | copy-start | bytes 12292
  3.1 19.4 %copy-start.9 = (f32[16]{0:T(128)S(1)}, f32[16]{0:T(128)}, u32[]{:S(2)}) copy-start(f32[16]{0:T(128)} %param.18) | copy-start | bytes 196
  3.1 19.5 %copy-start.6 = (f32[1024]{0:T(1024)S(1)}, f32[1024]{0:T(1024)}, u32[]{:S(2)}) copy-start(f32[1024]{0:T(1024)} %param.15) | copy-start | bytes 12292
  3.1 19.5 %copy-start.7 = (f32[1024]{0:T(1024)S(1)}, f32[1024]{0:T(1024)}, u32[]{:S(2)}) copy-start(f32[1024]{0:T(1024)} %param.16) | copy-start | bytes 12292
  3.1 30.9 %all-to-all-start = ((bf16[16,32,1792]{2,1,0:T(8,128)(2,1)}), bf16[16,32,1792]{2,1,0:T(8,128)(2,1)S(1)}, u32[]{:S(2)}, u32[]{:S(2)}) async-start(bf16[16,32,1792]{2,1,0:T(8,128)(2,1)} %spread.1), calls=%async_computation | async-start | bytes 3670016 | tf_op jit(solution)/shard_map/all_to_all | solution.py:406
  10.9 13.0 %collective-permute-start = (bf16[1792,256]{1,0:T(8,128)(2,1)S(1)}, bf16[1792,256]{1,0:T(8,128)(2,1)}, u32[]{:S(2)}, u32[]{:S(2)}) collective-permute-start(bf16[1792,256]{1,0:T(8,128)(2,1)S(1)} %copy-done), channel_id=1, source_target_pairs={{0,128},{128,0},{1,129},{129,1},{2,130},{130,2},{3,131},{131,3},{4... | collective-permute-start | bytes 2752520 | tf_op jit(solution)/shard_map/ppermute | solution.py:407
  16.7 49.3 %collective-permute-start.2 = (bf16[32,512]{1,0:T(8,128)(2,1)S(1)}, bf16[32,512]{1,0:T(8,128)(2,1)S(1)}, u32[]{:S(2)}, u32[]{:S(2)}) collective-permute-start(bf16[32,512]{1,0:T(8,128)(2,1)S(1)} %dynamic_slice.27), channel_id=1, source_target_pairs={{0,256},{256,0},{1,257},{257,1},{2,258},{258,2},{3,259},{259,3},{4... | collective-permute-start | bytes 98312 | tf_op jit(solution)/shard_map/ppermute | solution.py:417
  34.0 1.2 copy-start.1
  35.8 19.5 %collective-permute-start.1 = (bf16[256,512]{1,0:T(8,128)(2,1)S(1)}, bf16[256,512]{1,0:T(8,128)(2,1)S(1)}, u32[]{:S(2)}, u32[]{:S(2)}) collective-permute-start(bf16[256,512]{1,0:T(8,128)(2,1)S(1)} %forward.3), channel_id=1, source_target_pairs={{0,1},{1,0},{2,3},{3,2},{4,5},{5,4},{6,7},{7,6},{8,9},{9,8},{10,11... | collective-permute-start | bytes 786440 | tf_op jit(solution)/shard_map/ppermute | solution.py:444
  56.1 25.5 %all-to-all-start.1 = ((bf16[8,32,512]{2,1,0:T(8,128)(2,1)}), bf16[8,32,512]{2,1,0:T(8,128)(2,1)S(1)}, u32[]{:S(2)}, u32[]{:S(2)}) async-start(bf16[8,32,512]{2,1,0:T(8,128)(2,1)} %bitcast.8), calls=%async_computation.1 | async-start | bytes 524288 | tf_op jit(solution)/shard_map/all_to_all | solution.py:449
  67.3 76.4 %collective-permute-start.6 = (bf16[512,1792]{1,0:T(8,128)(2,1)S(1)}, bf16[512,1792]{1,0:T(8,128)(2,1)}, u32[]{:S(2)}, u32[]{:S(2)}) collective-permute-start(bf16[512,1792]{1,0:T(8,128)(2,1)S(1)} %bitcast.27), channel_id=1, source_target_pairs={{0,128},{128,0},{1,129},{129,1},{2,130},{130,2},{3,131},{131,3},{4... | collective-permute-start | bytes 5505032 | tf_op jit(solution)/shard_map/ppermute | solution.py:447
  106.7 10.2 %all-to-all-start.2 = ((bf16[16,32,128]{2,1,0:T(8,128)(2,1)}), bf16[16,32,128]{2,1,0:T(8,128)(2,1)S(1)}, u32[]{:S(2)}, u32[]{:S(2)}) async-start(bf16[16,32,128]{2,1,0:T(8,128)(2,1)} %token_sums.1), calls=%async_computation.2 | async-start | bytes 262144 | tf_op jit(solution)/shard_map/all_to_all | solution.py:455
  116.9 32.0 %all-to-all-start.3 = ((bf16[16,32,1792]{2,1,0:T(8,128)(2,1)}), bf16[16,32,1792]{2,1,0:T(8,128)(2,1)}, u32[]{:S(2)}, u32[]{:S(2)}) async-start(bf16[16,32,1792]{2,1,0:T(8,128)(2,1)} %back.1), calls=%async_computation.3 | async-start | bytes 3670016 | tf_op jit(solution)/shard_map/all_to_all | solution.py:458
  121.6 17.2 %collective-permute-start.3 = (f32[32,128]{1,0:T(8,128)S(1)}, f32[32,128]{1,0:T(8,128)S(1)}, u32[]{:S(2)}, u32[]{:S(2)}) collective-permute-start(f32[32,128]{1,0:T(8,128)S(1)} %token_terms.1.own_pack_ref.pack_ref), channel_id=1, source_target_pairs={{0,128},{128,0},{1,129},{129,1},{2,130},{130,2},{3,131},{131,3},{4... | collective-permute-start | bytes 49160 | tf_op jit(solution)/shard_map/ppermute | solution.py:462
  136.8 6.9 %collective-permute-start.5 = (bf16[512,256]{1,0:T(8,128)(2,1)S(1)}, bf16[512,256]{1,0:T(8,128)(2,1)S(1)}, u32[]{:S(2)}, u32[]{:S(2)}) collective-permute-start(bf16[512,256]{1,0:T(8,128)(2,1)S(1)} %get-tuple-element.28), channel_id=1, source_target_pairs={{0,128},{128,0},{1,129},{129,1},{2,130},{130,2},{3,131},{131,3},{4... | collective-permute-start | bytes 786440 | tf_op jit(solution)/shard_map/ppermute | solution.py:459
  138.8 9.5 %collective-permute-start.4 = (f32[4,128]{1,0:T(4,128)S(1)}, f32[4,128]{1,0:T(4,128)S(1)}, u32[]{:S(2)}, u32[]{:S(2)}) collective-permute-start(f32[4,128]{1,0:T(4,128)S(1)} %pad_maximum_fusion.2), channel_id=1, source_target_pairs={{0,256},{256,0},{1,257},{257,1},{2,258},{258,2},{3,259},{259,3},{4... | collective-permute-start | bytes 6152 | tf_op jit(solution)/shard_map/ppermute | solution.py:471

commit v6 on v5

--- a/solution.py
+++ b/solution.py
@@ -11,7 +11,7 @@
 CLIP_RANGE = 0.2
 EPSILON = 1e-05
 
-PLANE = ("yh", "x", "yl")
+SECTION = ("yh", "core", "x", "yl")
 SWAP = [(0, 1), (1, 0)]
 f32, bf16 = jnp.float32, jnp.bfloat16
 
@@ -31,7 +31,8 @@
     gap = position[None, :] - rows[:, None]
     inside = (row_seg[:, None] == segment[None, :]) & (gap >= 0)
     powers = jnp.power(jnp.float32(TRACE_DECAY), jnp.maximum(gap, 0).astype(f32))
-    return jnp.sum(jnp.where(inside, powers, 0.0) * delta[None, :], axis=1)
+    here = jnp.sum(jnp.where(gap == 0, old_values[None, :], 0.0), axis=1)
+    return here, jnp.sum(jnp.where(inside, powers, 0.0) * delta[None, :], axis=1)
 
 
 def pieces(x, count):
@@ -376,6 +377,34 @@
     )(own_pack, other_pack, own, other, scale, hidden, other_hidden)
 
 
+def place_of(yh, core, x, yl):
+    return ((yh * 2 + core) * 4 + x) * 2 + yl
+
+
+def lines(first):
+    groups = []
+    for core in range(2):
+        if (core == 0) == first:
+            groups += [[place_of(yh, core, x, yl) for x in range(4)] for yh in range(2) for yl in range(2)]
+        else:
+            groups += [[place_of(yh, core, x, yl) for yh in range(2) for yl in range(2)] for x in range(4)]
+    return groups
+
+
+def planes():
+    along_y = [(yh, yl) for yh in range(2) for yl in range(2)]
+    return [
+        [place_of(yh, 0, x, yl) for yh, yl in along_y for x in range(4)],
+        [place_of(yh, 1, x, yl) for x in range(4) for yh, yl in along_y],
+    ]
+
+
+def block_at(core, index):
+    y = jnp.where(core == 0, index // 4, index % 4)
+    x = jnp.where(core == 0, index % 4, index // 4)
+    return y // 2, x * 2 + y % 2
+
+
 def neighbours():
     pairs = [(z, z ^ 1) for z in range(16)]
     return pairs + [(16 + z, 16 + (z + (1 if z % 2 else -1)) % 16) for z in range(16)]
@@ -396,25 +425,34 @@
     yh, core = lax.axis_index("yh"), lax.axis_index("core")
     parity = lax.axis_index("zl")
     z = 2 * lax.axis_index("zh") + parity
-    spot = lax.axis_index(PLANE)
+    x, y = lax.axis_index("x"), 2 * yh + lax.axis_index("yl")
+    spot = jnp.where(core == 0, y * 4 + x, x * 4 + y)
     rows_each, units = hidden_act.shape
     width = down_weight.shape[1]
     chip = 2 * width
     group = 16 * rows_each
     section_rows = 8 * rows_each
 
-    hidden = lax.all_to_all(spread(hidden_act, 16), PLANE, 0, 0, tiled=True)
-    other_weight = hold(lax.ppermute(down_weight, "core", SWAP))
+    hidden = lax.all_to_all(
+        spread(hidden_act, 4), SECTION, 0, 0, tiled=True, axis_index_groups=lines(True)
+    ).reshape(4 * rows_each, units)
+    far_weight = lax.ppermute(down_weight, "core", SWAP)
+    hidden, far_weight, residual = lax.optimization_barrier((hidden, far_weight, residual))
+    hidden = lax.all_to_all(
+        spread(hidden, 4), SECTION, 0, 0, tiled=True, axis_index_groups=lines(False)
+    ).reshape(16, rows_each, units)
+    other_weight = hold(far_weight)
 
     chip_scale = lax.dynamic_slice_in_dim(gain * head_weight, yh * chip, chip, 0)
     own_scale = lax.dynamic_slice_in_dim(chip_scale, core * width, width, 0)
     other_scale = lax.dynamic_slice_in_dim(chip_scale, (1 - core) * width, width, 0)
     scale = jnp.concatenate([own_scale, other_scale])
 
-    kept = lax.dynamic_slice_in_dim(residual, z % 8 * rows_each, rows_each, 0)
+    holder, phase = block_at(core, z)
+    kept = lax.dynamic_slice_in_dim(residual, phase * rows_each, rows_each, 0)
     sent = lax.dynamic_slice_in_dim(kept, (1 - yh) * chip, chip, 1)
     mine = lax.dynamic_slice_in_dim(kept, yh * chip, chip, 1)
-    stream = jnp.where(yh == z // 8, mine, lax.ppermute(sent, "yh", SWAP))
+    stream = jnp.where(yh == holder, mine, lax.ppermute(sent, "yh", SWAP))
     left, right = stream[:, :width], stream[:, width:]
     stream = jnp.concatenate(
         [jnp.where(core == 0, left, right), jnp.where(core == 0, right, left)], axis=1
@@ -427,14 +465,10 @@
     base = jnp.sum(scale_back, axis=0).reshape(-1, 128)
     base = jnp.pad(base, ((0, 16 - base.shape[0]), (0, 0))).astype(bf16)
     slot = jnp.arange(group, dtype=jnp.int32)
-    token = slot + section_rows * (slot // section_rows + core)
-    own_old = jnp.concatenate(
-        [
-            lax.dynamic_slice_in_dim(old_values, core * section_rows, section_rows, 0),
-            lax.dynamic_slice_in_dim(old_values, (2 + core) * section_rows, section_rows, 0),
-        ]
-    )
-    returns = own_old + returns_of(behavior, frozen, old_values, judge_ratings, lengths, token)
+    owner_yh, phase = block_at(core, slot // rows_each)
+    token = (2 * owner_yh + core) * section_rows + phase * rows_each + slot % rows_each
+    own_old, advantage = returns_of(behavior, frozen, old_values, judge_ratings, lengths, token)
+    returns = own_old + advantage
     returns, own_old = returns.reshape(4, 128), own_old.reshape(4, 128)
     hidden, returns, own_old, other_weight = lax.optimization_barrier(
         (hidden, returns, own_old, other_weight)
@@ -452,10 +486,10 @@
     own_columns, other_columns = combined[:, :width], combined[:, width:]
 
     sums = token_sums(combined, scale_rows, base, 16)
-    sums = lax.all_to_all(sums, PLANE, 0, 0, tiled=True)
+    sums = lax.all_to_all(sums, SECTION, 0, 0, tiled=True, axis_index_groups=planes())
     payload = back(combined, down_weight, other_weight, 16)
     sums, payload = lax.optimization_barrier((sums, payload))
-    arrived = lax.all_to_all(payload, PLANE, 0, 0, tiled=True)
+    arrived = lax.all_to_all(payload, SECTION, 0, 0, tiled=True, axis_index_groups=planes())
     far_columns = lax.ppermute(other_columns, "core", SWAP)
     pack = token_terms(sums, own_old, returns, combined)
     hidden_grad = hidden_gradient(spot, arrived, pack)

time: 153 us -> 152 us (level)
  starting transfers between devices: 74.9 us -> 67.2 us
  blocking collectives: 23.8 us -> 26.5 us
  local copies, waits for them, and re-layouts: 3.35 us -> 5.78 us
    all_to_all x1, waiting for transfers between devices: 11 us -> 0.01 us  [on_device(): lax.all_to_all(pair.reshape(8, rows_each, chip), 'zh', 0, 0, tiled=True)]
    ppermute x1, starting transfers between devices: 15.8 us -> 6.65 us  [on_device(): met = lax.ppermute(away, ('core', 'zh', 'zl'), neighbours())]
    all_to_all x3 -> x4, waiting for transfers between devices: 12.1 us -> 18.5 us  [the longest x1 11 us: on_device(): lax.all_to_all(spread(hidden, 4), SECTION, 0, 0, tiled=True, axis_index_g...]
    ppermute x2, waiting for transfers between devices: 0.01 us -> 3.52 us  [the longest x1 3.52 us: on_device(): stream = jnp.where(yh == holder, mine, lax.ppermute(sent, 'yh', SWAP))]
    all_gather x1, blocking collectives: 23.8 us -> 26.5 us  [on_device(): combined = lax.all_gather(combined, ('zh', 'zl'), axis=0, tiled=True)]
    ppermute x1, starting transfers between devices: 3.27 us -> 5.85 us  [on_device(): far_hidden = lax.ppermute(hidden, 'core', SWAP)]
    ppermute x1, starting transfers between devices: 15.2 us -> 13.5 us  [on_device(): other_pack = lax.ppermute(pack, 'core', SWAP)]
    unnamed x20 -> x18, local copies, waits for them, and re-layouts: 2.12 us -> 3.28 us
  transfers between devices with their start and end apart: 11 -> 12, of which waited for: 4 -> 6; matrix products, arithmetic and copies ran while one was open for 5% -> 6% of each run, Pallas kernels for 8% -> 8%
where the time goes in v6:
time: 152 us; the launch traced here: 149 us
  starting transfers between devices  67.2 us (44%)
  blocking collectives  26.5 us (17%)
  waiting for transfers between devices  25.5 us (17%)
  Pallas kernels  15.9 us (10%)
  local copies, waits for them, and re-layouts  5.78 us (4%)
  other arithmetic  5.08 us (3%)
  matrix products  1.95 us (1%)
    all_gather x1, blocking collectives, on_device(): combined = lax.all_gather(combined, ('zh', 'zl'), axis=0, tiled=True)  26.5 us
    ppermute x1, starting transfers between devices, on_device(): other_pack = lax.ppermute(pack, 'core', SWAP)  13.5 us
    all_to_all x1, waiting for transfers between devices, on_device(): lax.all_to_all(spread(hidden, 4), SECTION, 0, 0, tiled=True, axis_index_g...  11 us
    ppermute x1, starting transfers between devices, on_device(): far_weight = lax.ppermute(down_weight, 'core', SWAP)  8.79 us
    all_to_all x1, starting transfers between devices, on_device(): lax.all_to_all(pair.reshape(8, rows_each, chip), 'zh', 0, 0, tiled=True)  8.26 us
    ppermute x1, starting transfers between devices, on_device(): met = lax.ppermute(away, ('core', 'zh', 'zl'), neighbours())  6.65 us
    ppermute x1, starting transfers between devices, on_device(): far_hidden = lax.ppermute(hidden, 'core', SWAP)  5.85 us
    ppermute x1, starting transfers between devices, on_device(): head_far = lax.ppermute(head_chip, 'yh', SWAP)  4.91 us
  transfers between devices with their start and end apart: 12, of which 6 were waited for; matrix products, arithmetic and copies ran while one was open for 6% of the time, Pallas kernels for 8%

profile of v6, /device:TPU:1, one launch (start us, length us, event | category | flops | bytes accessed | tf_op | source)
XLA Modules:
  0.0 149.0 jit_solution(12434384953662607135)
XLA Ops:
  0.6 8.8 %collective-permute-start = (bf16[1792,256]{1,0:T(8,128)(2,1)}, bf16[1792,256]{1,0:T(8,128)(2,1)S(1)}, u32[]{:S(2)}, u32[]{:S(2)}) collective-permute-start(bf16[1792,256]{1,0:T(8,128)(2,1)} %outer_ref.1), channel_id=1, source_target_pairs={{0,128},{128,0},{1,129},{129,1},{2,130},{130,2},{3,131},{131,3},{4... | collective-permute-start | bytes 2752520 | tf_op jit(solution)/shard_map/ppermute | solution.py:439
  11.2 3.5 %all-to-all-start = ((bf16[4,32,1792]{2,1,0:T(8,128)(2,1)}), bf16[4,32,1792]{2,1,0:T(8,128)(2,1)S(1)}, u32[]{:S(2)}, u32[]{:S(2)}) async-start(bf16[4,32,1792]{2,1,0:T(8,128)(2,1)} %spread.2), calls=%async_computation | async-start | bytes 917504 | tf_op jit(solution)/shard_map/all_to_all | solution.py:436
  17.2 4.4 %all-to-all-done = bf16[4,32,1792]{2,1,0:T(8,128)(2,1)S(1)} async-done(((bf16[4,32,1792]{2,1,0:T(8,128)(2,1)}), bf16[4,32,1792]{2,1,0:T(8,128)(2,1)S(1)}, u32[]{:S(2)}, u32[]{:S(2)}) %all-to-all-start) | async-done | bytes 458784 | tf_op jit(solution)/shard_map/all_to_all | solution.py:436
  21.6 1.6 %spread.3 = bf16[4,128,1792]{2,1,0:T(8,128)(2,1)} custom-call(bf16[128,1792]{1,0:T(8,128)(2,1)S(1)} %bitcast.29), custom_call_target="tpu_custom_call" | custom-call | bytes 1835008 | tf_op jit(solution)/shard_map/spread/pallas_call | solution.py:98
  23.2 3.6 %all-to-all-start.1 = ((bf16[4,128,1792]{2,1,0:T(8,128)(2,1)}), bf16[4,128,1792]{2,1,0:T(8,128)(2,1)S(1)}, u32[]{:S(2)}, u32[]{:S(2)}) async-start(bf16[4,128,1792]{2,1,0:T(8,128)(2,1)} %spread.3), calls=%async_computation.1 | async-start | bytes 3670016 | tf_op jit(solution)/shard_map/all_to_all | solution.py:441
  27.2 1.4 select_reduce_fusion
  30.0 11.0 %all-to-all-done.1 = bf16[4,128,1792]{2,1,0:T(8,128)(2,1)S(1)} async-done(((bf16[4,128,1792]{2,1,0:T(8,128)(2,1)}), bf16[4,128,1792]{2,1,0:T(8,128)(2,1)S(1)}, u32[]{:S(2)}, u32[]{:S(2)}) %all-to-all-start.1) | async-done | bytes 1835040 | tf_op jit(solution)/shard_map/all_to_all | solution.py:441
  42.9 6.7 %collective-permute-start.1 = (bf16[256,512]{1,0:T(8,128)(2,1)S(1)}, bf16[256,512]{1,0:T(8,128)(2,1)S(1)}, u32[]{:S(2)}, u32[]{:S(2)}) collective-permute-start(bf16[256,512]{1,0:T(8,128)(2,1)S(1)} %forward.3), channel_id=1, source_target_pairs={{0,1},{1,0},{2,3},{3,2},{4,5},{5,4},{6,7},{7,6},{8,9},{9,8},{10,11... | collective-permute-start | bytes 786440 | tf_op jit(solution)/shard_map/ppermute | solution.py:478
  50.3 3.0 %collective-permute-done.1 = bf16[256,512]{1,0:T(8,128)(2,1)S(1)} collective-permute-done((bf16[256,512]{1,0:T(8,128)(2,1)S(1)}, bf16[256,512]{1,0:T(8,128)(2,1)S(1)}, u32[]{:S(2)}, u32[]{:S(2)}) %collective-permute-start.1) | collective-permute-done | bytes 262176 | tf_op jit(solution)/shard_map/ppermute | solution.py:478
  54.1 8.3 %all-to-all-start.2 = ((bf16[8,32,512]{2,1,0:T(8,128)(2,1)}), bf16[8,32,512]{2,1,0:T(8,128)(2,1)S(1)}, u32[]{:S(2)}, u32[]{:S(2)}) async-start(bf16[8,32,512]{2,1,0:T(8,128)(2,1)} %bitcast.9), calls=%async_computation.2 | async-start | bytes 524288 | tf_op jit(solution)/shard_map/all_to_all | solution.py:483
  62.4 1.5 %fusion.11 = f32[16,1792]{1,0:T(8,128)S(1)} fusion(bf16[1792,256]{1,0:T(8,128)(2,1)} %outer_ref.1, bf16[16,512]{1,0:T(8,128)(2,1)S(1)} %fusion.9.scale_ref), kind=kOutput, calls=%fused_computation.27 | convolution fusion | flops 14680064 | bytes 1040384 | tf_op jit(solution)/shard_map/dot_general | solution.py:462
  64.8 2.2 %collective-permute-start.2 = (bf16[32,512]{1,0:T(8,128)(2,1)S(1)}, bf16[32,512]{1,0:T(8,128)(2,1)S(1)}, u32[]{:S(2)}, u32[]{:S(2)}) collective-permute-start(bf16[32,512]{1,0:T(8,128)(2,1)S(1)} %dynamic_slice.19), channel_id=1, source_target_pairs={{0,256},{256,0},{1,257},{257,1},{2,258},{258,2},{3,259},{259,3},{4... | collective-permute-start | bytes 98312 | tf_op jit(solution)/shard_map/ppermute | solution.py:455
  67.5 3.5 %collective-permute-done.2 = bf16[32,512]{1,0:T(8,128)(2,1)S(1)} collective-permute-done((bf16[32,512]{1,0:T(8,128)(2,1)S(1)}, bf16[32,512]{1,0:T(8,128)(2,1)S(1)}, u32[]{:S(2)}, u32[]{:S(2)}) %collective-permute-start.2) | collective-permute-done | bytes 32800 | tf_op jit(solution)/shard_map/ppermute | solution.py:455
  71.9 5.9 %collective-permute-start.6 = (bf16[512,1792]{1,0:T(8,128)(2,1)S(1)}, bf16[512,1792]{1,0:T(8,128)(2,1)}, u32[]{:S(2)}, u32[]{:S(2)}) collective-permute-start(bf16[512,1792]{1,0:T(8,128)(2,1)S(1)} %bitcast.27), channel_id=1, source_target_pairs={{0,128},{128,0},{1,129},{129,1},{2,130},{130,2},{3,131},{131,3},{4... | collective-permute-start | bytes 5505032 | tf_op jit(solution)/shard_map/ppermute | solution.py:481
  77.8 26.5 %all_gather.3.combined_ref = bf16[512,512]{1,0:T(8,128)(2,1)S(1)} all-gather(bf16[32,512]{1,0:T(8,128)(2,1)S(1)} %add_convert_fusion.1), channel_id=1, replica_groups=mesh['yh'=2,'core'=2,'x'=4,'yl'=2,'zh'=8,'zl'=2] {'zh','zl'}, dimensions={0}, use_global_device_ids=true | all-gather | bytes 557056 | tf_op jit(solution)/shard_map/all_gather | solution.py:485
  105.7 3.5 %all-to-all-start.3 = ((bf16[16,32,128]{2,1,0:T(8,128)(2,1)}), bf16[16,32,128]{2,1,0:T(8,128)(2,1)S(1)}, u32[]{:S(2)}, u32[]{:S(2)}) async-start(bf16[16,32,128]{2,1,0:T(8,128)(2,1)} %token_sums.1), calls=%async_computation.3 | async-start | bytes 262144 | tf_op jit(solution)/shard_map/all_to_all | solution.py:489
  109.2 3.5 %back.1 = bf16[16,32,1792]{2,1,0:T(8,128)(2,1)} custom-call(bf16[512,512]{1,0:T(8,128)(2,1)S(1)} %all_gather.3.combined_ref, bf16[1792,256]{1,0:T(8,128)(2,1)} %outer_ref.1, bf16[1792,256]{1,0:T(8,128)(2,1)S(1)} %hold.1.other_ref), custom_call_target="tpu_custom_call" | custom-call | flops 939524096 | bytes 3670016 | tf_op jit(solution)/shard_map/back/pallas_call | solution.py:210
  112.7 3.1 %all-to-all-done.3.sums_ref = bf16[16,32,128]{2,1,0:T(8,128)(2,1)S(1)} async-done(((bf16[16,32,128]{2,1,0:T(8,128)(2,1)}), bf16[16,32,128]{2,1,0:T(8,128)(2,1)S(1)}, u32[]{:S(2)}, u32[]{:S(2)}) %all-to-all-start.3) | async-done | bytes 131104 | tf_op jit(solution)/shard_map/all_to_all | solution.py:489
  115.8 4.4 %all-to-all-start.4 = ((bf16[16,32,1792]{2,1,0:T(8,128)(2,1)}), bf16[16,32,1792]{2,1,0:T(8,128)(2,1)}, u32[]{:S(2)}, u32[]{:S(2)}) async-start(bf16[16,32,1792]{2,1,0:T(8,128)(2,1)} %back.1), calls=%async_computation.4 | async-start | bytes 3670016 | tf_op jit(solution)/shard_map/all_to_all | solution.py:492
  120.5 13.5 %collective-permute-start.3 = (f32[32,128]{1,0:T(8,128)S(1)}, f32[32,128]{1,0:T(8,128)S(1)}, u32[]{:S(2)}, u32[]{:S(2)}) collective-permute-start(f32[32,128]{1,0:T(8,128)S(1)} %token_terms.1.own_pack_ref.pack_ref), channel_id=1, source_target_pairs={{0,128},{128,0},{1,129},{129,1},{2,130},{130,2},{3,131},{131,3},{4... | collective-permute-start | bytes 49160 | tf_op jit(solution)/shard_map/ppermute | solution.py:496
  134.1 1.9 %collective-permute-start.5 = (bf16[512,256]{1,0:T(8,128)(2,1)S(1)}, bf16[512,256]{1,0:T(8,128)(2,1)S(1)}, u32[]{:S(2)}, u32[]{:S(2)}) collective-permute-start(bf16[512,256]{1,0:T(8,128)(2,1)S(1)} %get-tuple-element.36), channel_id=1, source_target_pairs={{0,128},{128,0},{1,129},{129,1},{2,130},{130,2},{3,131},{131,3},{4... | collective-permute-start | bytes 786440 | tf_op jit(solution)/shard_map/ppermute | solution.py:493
  136.0 4.9 %collective-permute-start.4 = (f32[4,128]{1,0:T(4,128)S(1)}, f32[4,128]{1,0:T(4,128)S(1)}, u32[]{:S(2)}, u32[]{:S(2)}) collective-permute-start(f32[4,128]{1,0:T(4,128)S(1)} %pad_maximum_fusion.1), channel_id=1, source_target_pairs={{0,256},{256,0},{1,257},{257,1},{2,258},{258,2},{3,259},{259,3},{4... | collective-permute-start | bytes 6152 | tf_op jit(solution)/shard_map/ppermute | solution.py:505
  141.0 4.5 %weight_gradient.1 = (f32[1792,256]{1,0:T(8,128)}, f32[1,1]{1,0:T(1,128)}) custom-call(f32[32,128]{1,0:T(8,128)S(1)} %token_terms.1.own_pack_ref.pack_ref, f32[32,128]{1,0:T(8,128)S(1)} %collective-permute-done.3.other_pack_ref, bf16[512,256]{1,0:T(8,128)(2,1)S(1)} %get-tuple-element.37.own_ref, bf16[512,256]{1,0:T(8,128)(2,1)S(1)} %collective-permute-done.5.other_ref, ...), custom_call_target="tpu_custom_call" | custom-call | flops 939524096 | bytes 3670016 | tf_op jit(solution)/shard_map/weight_gradient/pallas_call | solution.py:360
  146.6 2.4 %hidden_gradient.1 = bf16[32,1792]{1,0:T(8,128)(2,1)} custom-call(s32[1]{0:T(128)} %bitcast.15.spot_ref, bf16[16,32,1792]{2,1,0:T(8,128)(2,1)} %all-to-all-done.4.arrived_ref, f32[32,128]{1,0:T(8,128)S(1)} %token_terms.1.own_pack_ref.pack_ref), custom_call_target="tpu_custom_call" | custom-call | flops 3670016 | bytes 1835008 | tf_op jit(solution)/shard_map/hidden_gradient/pallas_call | solution.py:299
  (60 shorter events, 14.2 us)
Async XLA Ops:
  0.6 21.0 %collective-permute-start = (bf16[1792,256]{1,0:T(8,128)(2,1)}, bf16[1792,256]{1,0:T(8,128)(2,1)S(1)}, u32[]{:S(2)}, u32[]{:S(2)}) collective-permute-start(bf16[1792,256]{1,0:T(8,128)(2,1)} %outer_ref.1), channel_id=1, source_target_pairs={{0,128},{128,0},{1,129},{129,1},{2,130},{130,2},{3,131},{131,3},{4... | collective-permute-start | bytes 2752520 | tf_op jit(solution)/shard_map/ppermute | solution.py:439
  9.4 0.9 copy-start.3
  11.2 10.3 %all-to-all-start = ((bf16[4,32,1792]{2,1,0:T(8,128)(2,1)}), bf16[4,32,1792]{2,1,0:T(8,128)(2,1)S(1)}, u32[]{:S(2)}, u32[]{:S(2)}) async-start(bf16[4,32,1792]{2,1,0:T(8,128)(2,1)} %spread.2), calls=%async_computation | async-start | bytes 917504 | tf_op jit(solution)/shard_map/all_to_all | solution.py:436
  21.6 1.6 %copy-start.1 = (bf16[1792,256]{1,0:T(8,128)(2,1)}, bf16[1792,256]{1,0:T(8,128)(2,1)S(1)}, u32[]{:S(2)}) copy-start(bf16[1792,256]{1,0:T(8,128)(2,1)S(1)} %collective-permute-done.in_ref) | copy-start | bytes 2752516
  23.2 3.9 %copy-start.8 = (f32[16]{0:T(128)S(1)}, f32[16]{0:T(128)}, u32[]{:S(2)}) copy-start(f32[16]{0:T(128)} %param.18) | copy-start | bytes 196
  23.2 4.0 %copy-start.5 = (f32[1024]{0:T(1024)S(1)}, f32[1024]{0:T(1024)}, u32[]{:S(2)}) copy-start(f32[1024]{0:T(1024)} %param.17) | copy-start | bytes 12292
  23.2 4.0 %copy-start.6 = (f32[1024]{0:T(1024)S(1)}, f32[1024]{0:T(1024)}, u32[]{:S(2)}) copy-start(f32[1024]{0:T(1024)} %param.15) | copy-start | bytes 12292
  23.2 4.0 %copy-start.7 = (f32[1024]{0:T(1024)S(1)}, f32[1024]{0:T(1024)}, u32[]{:S(2)}) copy-start(f32[1024]{0:T(1024)} %param.16) | copy-start | bytes 12292
  23.2 17.8 %all-to-all-start.1 = ((bf16[4,128,1792]{2,1,0:T(8,128)(2,1)}), bf16[4,128,1792]{2,1,0:T(8,128)(2,1)S(1)}, u32[]{:S(2)}, u32[]{:S(2)}) async-start(bf16[4,128,1792]{2,1,0:T(8,128)(2,1)} %spread.3), calls=%async_computation.1 | async-start | bytes 3670016 | tf_op jit(solution)/shard_map/all_to_all | solution.py:441
  28.6 1.2 copy-start.2
  41.0 1.2 copy-start
  42.9 10.4 %collective-permute-start.1 = (bf16[256,512]{1,0:T(8,128)(2,1)S(1)}, bf16[256,512]{1,0:T(8,128)(2,1)S(1)}, u32[]{:S(2)}, u32[]{:S(2)}) collective-permute-start(bf16[256,512]{1,0:T(8,128)(2,1)S(1)} %forward.3), channel_id=1, source_target_pairs={{0,1},{1,0},{2,3},{3,2},{4,5},{5,4},{6,7},{7,6},{8,9},{9,8},{10,11... | collective-permute-start | bytes 786440 | tf_op jit(solution)/shard_map/ppermute | solution.py:478
  54.1 23.7 %all-to-all-start.2 = ((bf16[8,32,512]{2,1,0:T(8,128)(2,1)}), bf16[8,32,512]{2,1,0:T(8,128)(2,1)S(1)}, u32[]{:S(2)}, u32[]{:S(2)}) async-start(bf16[8,32,512]{2,1,0:T(8,128)(2,1)} %bitcast.9), calls=%async_computation.2 | async-start | bytes 524288 | tf_op jit(solution)/shard_map/all_to_all | solution.py:483
  64.8 6.2 %collective-permute-start.2 = (bf16[32,512]{1,0:T(8,128)(2,1)S(1)}, bf16[32,512]{1,0:T(8,128)(2,1)S(1)}, u32[]{:S(2)}, u32[]{:S(2)}) collective-permute-start(bf16[32,512]{1,0:T(8,128)(2,1)S(1)} %dynamic_slice.19), channel_id=1, source_target_pairs={{0,256},{256,0},{1,257},{257,1},{2,258},{258,2},{3,259},{259,3},{4... | collective-permute-start | bytes 98312 | tf_op jit(solution)/shard_map/ppermute | solution.py:455
  71.9 69.1 %collective-permute-start.6 = (bf16[512,1792]{1,0:T(8,128)(2,1)S(1)}, bf16[512,1792]{1,0:T(8,128)(2,1)}, u32[]{:S(2)}, u32[]{:S(2)}) collective-permute-start(bf16[512,1792]{1,0:T(8,128)(2,1)S(1)} %bitcast.27), channel_id=1, source_target_pairs={{0,128},{128,0},{1,129},{129,1},{2,130},{130,2},{3,131},{131,3},{4... | collective-permute-start | bytes 5505032 | tf_op jit(solution)/shard_map/ppermute | solution.py:481
  105.7 10.2 %all-to-all-start.3 = ((bf16[16,32,128]{2,1,0:T(8,128)(2,1)}), bf16[16,32,128]{2,1,0:T(8,128)(2,1)S(1)}, u32[]{:S(2)}, u32[]{:S(2)}) async-start(bf16[16,32,128]{2,1,0:T(8,128)(2,1)} %token_sums.1), calls=%async_computation.3 | async-start | bytes 262144 | tf_op jit(solution)/shard_map/all_to_all | solution.py:489
  115.8 30.8 %all-to-all-start.4 = ((bf16[16,32,1792]{2,1,0:T(8,128)(2,1)}), bf16[16,32,1792]{2,1,0:T(8,128)(2,1)}, u32[]{:S(2)}, u32[]{:S(2)}) async-start(bf16[16,32,1792]{2,1,0:T(8,128)(2,1)} %back.1), calls=%async_computation.4 | async-start | bytes 3670016 | tf_op jit(solution)/shard_map/all_to_all | solution.py:492
  120.5 15.5 %collective-permute-start.3 = (f32[32,128]{1,0:T(8,128)S(1)}, f32[32,128]{1,0:T(8,128)S(1)}, u32[]{:S(2)}, u32[]{:S(2)}) collective-permute-start(f32[32,128]{1,0:T(8,128)S(1)} %token_terms.1.own_pack_ref.pack_ref), channel_id=1, source_target_pairs={{0,128},{128,0},{1,129},{129,1},{2,130},{130,2},{3,131},{131,3},{4... | collective-permute-start | bytes 49160 | tf_op jit(solution)/shard_map/ppermute | solution.py:496
  134.1 6.9 %collective-permute-start.5 = (bf16[512,256]{1,0:T(8,128)(2,1)S(1)}, bf16[512,256]{1,0:T(8,128)(2,1)S(1)}, u32[]{:S(2)}, u32[]{:S(2)}) collective-permute-start(bf16[512,256]{1,0:T(8,128)(2,1)S(1)} %get-tuple-element.36), channel_id=1, source_target_pairs={{0,128},{128,0},{1,129},{129,1},{2,130},{130,2},{3,131},{131,3},{4... | collective-permute-start | bytes 786440 | tf_op jit(solution)/shard_map/ppermute | solution.py:493
  136.0 9.9 %collective-permute-start.4 = (f32[4,128]{1,0:T(4,128)S(1)}, f32[4,128]{1,0:T(4,128)S(1)}, u32[]{:S(2)}, u32[]{:S(2)}) collective-permute-start(f32[4,128]{1,0:T(4,128)S(1)} %pad_maximum_fusion.1), channel_id=1, source_target_pairs={{0,256},{256,0},{1,257},{257,1},{2,258},{258,2},{3,259},{259,3},{4... | collective-permute-start | bytes 6152 | tf_op jit(solution)/shard_map/ppermute | solution.py:505
  141.0 5.0 %copy-start.4 = (f32[1024]{0:T(1024)S(1)}, f32[1024]{0:T(1024)}, u32[]{:S(2)}) copy-start(f32[1024]{0:T(1024)} %param.14) | copy-start | bytes 12292

commit v7 on v6

--- a/solution.py
+++ b/solution.py
@@ -436,12 +436,13 @@
     hidden = lax.all_to_all(
         spread(hidden_act, 4), SECTION, 0, 0, tiled=True, axis_index_groups=lines(True)
     ).reshape(4 * rows_each, units)
-    far_weight = lax.ppermute(down_weight, "core", SWAP)
-    hidden, far_weight, residual = lax.optimization_barrier((hidden, far_weight, residual))
+    hidden, moved_weight, residual, old_values = lax.optimization_barrier(
+        (hidden, down_weight, residual, old_values)
+    )
     hidden = lax.all_to_all(
         spread(hidden, 4), SECTION, 0, 0, tiled=True, axis_index_groups=lines(False)
     ).reshape(16, rows_each, units)
-    other_weight = hold(far_weight)
+    other_weight = hold(lax.ppermute(moved_weight, "core", SWAP))
 
     chip_scale = lax.dynamic_slice_in_dim(gain * head_weight, yh * chip, chip, 0)
     own_scale = lax.dynamic_slice_in_dim(chip_scale, core * width, width, 0)

time: 152 us -> 153 us (level)
  the two profiles are of different devices: /device:TPU:1 before, /device:TPU:32 now
where the time goes in v7:
time: 153 us; the launch traced here: 152 us
  starting transfers between devices  54.4 us (36%)
  waiting for transfers between devices  38.5 us (25%)
  blocking collectives  31.3 us (20%)
  Pallas kernels  15.8 us (10%)
  other arithmetic  5.08 us (3%)
  local copies, waits for them, and re-layouts  3.91 us (3%)
  matrix products  1.95 us (1%)
    all_gather x1, blocking collectives, on_device(): combined = lax.all_gather(combined, ('zh', 'zl'), axis=0, tiled=True)  31.3 us
    all_to_all x1, starting transfers between devices, on_device(): lax.all_to_all(pair.reshape(8, rows_each, chip), 'zh', 0, 0, tiled=True)  12.5 us
    all_to_all x1, waiting for transfers between devices, on_device(): lax.all_to_all(spread(hidden, 4), SECTION, 0, 0, tiled=True, axis_index_g...  10.4 us
    all_to_all x1, starting transfers between devices, on_device(): lax.all_to_all(payload, SECTION, 0, 0, tiled=True, axis_index_groups=plan...  7.93 us
    all_to_all x1, waiting for transfers between devices, on_device(): lax.all_to_all(spread(hidden_act, 4), SECTION, 0, 0, tiled=True, axis_ind...  6.05 us
    ppermute x1, starting transfers between devices, on_device(): met = lax.ppermute(away, ('core', 'zh', 'zl'), neighbours())  5.63 us
    ppermute x1, starting transfers between devices, on_device(): head_far = lax.ppermute(head_chip, 'yh', SWAP)  5.27 us
    all_to_all x1, waiting for transfers between devices, on_device(): lax.all_to_all(pair.reshape(8, rows_each, chip), 'zh', 0, 0, tiled=True)  5.2 us
  transfers between devices with their start and end apart: 12, of which 8 were waited for; matrix products, arithmetic and copies ran while one was open for 5% of the time, Pallas kernels for 7%

profile of v7, /device:TPU:32, one launch (start us, length us, event | category | flops | bytes accessed | tf_op | source)
XLA Modules:
  0.0 152.1 jit_solution(15025587504990432256)
XLA Ops:
  2.5 4.3 %all-to-all-start = ((bf16[4,32,1792]{2,1,0:T(8,128)(2,1)}), bf16[4,32,1792]{2,1,0:T(8,128)(2,1)S(1)}, u32[]{:S(2)}, u32[]{:S(2)}) async-start(bf16[4,32,1792]{2,1,0:T(8,128)(2,1)} %spread.2), calls=%async_computation | async-start | bytes 917504 | tf_op jit(solution)/shard_map/all_to_all | solution.py:436
  8.4 6.0 %all-to-all-done = bf16[4,32,1792]{2,1,0:T(8,128)(2,1)S(1)} async-done(((bf16[4,32,1792]{2,1,0:T(8,128)(2,1)}), bf16[4,32,1792]{2,1,0:T(8,128)(2,1)S(1)}, u32[]{:S(2)}, u32[]{:S(2)}) %all-to-all-start) | async-done | bytes 458784 | tf_op jit(solution)/shard_map/all_to_all | solution.py:436
  16.1 4.6 %all-to-all-start.1 = ((bf16[4,128,1792]{2,1,0:T(8,128)(2,1)}), bf16[4,128,1792]{2,1,0:T(8,128)(2,1)S(1)}, u32[]{:S(2)}, u32[]{:S(2)}) async-start(bf16[4,128,1792]{2,1,0:T(8,128)(2,1)} %spread.3), calls=%async_computation.1 | async-start | bytes 3670016 | tf_op jit(solution)/shard_map/all_to_all | solution.py:442
  20.8 1.9 %collective-permute-start = (bf16[1792,256]{1,0:T(8,128)(2,1)S(1)}, bf16[1792,256]{1,0:T(8,128)(2,1)S(1)}, u32[]{:S(2)}, u32[]{:S(2)}) collective-permute-start(bf16[1792,256]{1,0:T(8,128)(2,1)S(1)} %copy-done), channel_id=1, source_target_pairs={{0,128},{128,0},{1,129},{129,1},{2,130},{130,2},{3,131},{131,3},{4... | collective-permute-start | bytes 2752520 | tf_op jit(solution)/shard_map/ppermute | solution.py:445
  25.4 10.4 %all-to-all-done.1 = bf16[4,128,1792]{2,1,0:T(8,128)(2,1)S(1)} async-done(((bf16[4,128,1792]{2,1,0:T(8,128)(2,1)}), bf16[4,128,1792]{2,1,0:T(8,128)(2,1)S(1)}, u32[]{:S(2)}, u32[]{:S(2)}) %all-to-all-start.1) | async-done | bytes 1835040 | tf_op jit(solution)/shard_map/all_to_all | solution.py:442
  37.6 5.6 %collective-permute-start.1 = (bf16[256,512]{1,0:T(8,128)(2,1)S(1)}, bf16[256,512]{1,0:T(8,128)(2,1)S(1)}, u32[]{:S(2)}, u32[]{:S(2)}) collective-permute-start(bf16[256,512]{1,0:T(8,128)(2,1)S(1)} %forward.3), channel_id=1, source_target_pairs={{0,1},{1,0},{2,3},{3,2},{4,5},{5,4},{6,7},{7,6},{8,9},{9,8},{10,11... | collective-permute-start | bytes 786440 | tf_op jit(solution)/shard_map/ppermute | solution.py:479
  44.0 3.6 %collective-permute-done.1 = bf16[256,512]{1,0:T(8,128)(2,1)S(1)} collective-permute-done((bf16[256,512]{1,0:T(8,128)(2,1)S(1)}, bf16[256,512]{1,0:T(8,128)(2,1)S(1)}, u32[]{:S(2)}, u32[]{:S(2)}) %collective-permute-start.1) | collective-permute-done | bytes 262176 | tf_op jit(solution)/shard_map/ppermute | solution.py:479
  48.4 12.5 %all-to-all-start.2 = ((bf16[8,32,512]{2,1,0:T(8,128)(2,1)}), bf16[8,32,512]{2,1,0:T(8,128)(2,1)S(1)}, u32[]{:S(2)}, u32[]{:S(2)}) async-start(bf16[8,32,512]{2,1,0:T(8,128)(2,1)} %bitcast.9), calls=%async_computation.2 | async-start | bytes 524288 | tf_op jit(solution)/shard_map/all_to_all | solution.py:484
  61.8 2.5 %collective-permute-start.2 = (bf16[32,512]{1,0:T(8,128)(2,1)S(1)}, bf16[32,512]{1,0:T(8,128)(2,1)S(1)}, u32[]{:S(2)}, u32[]{:S(2)}) collective-permute-start(bf16[32,512]{1,0:T(8,128)(2,1)S(1)} %dynamic_slice.19), channel_id=1, source_target_pairs={{0,256},{256,0},{1,257},{257,1},{2,258},{258,2},{3,259},{259,3},{4... | collective-permute-start | bytes 98312 | tf_op jit(solution)/shard_map/ppermute | solution.py:456
  64.3 1.5 %fusion.11 = f32[16,1792]{1,0:T(8,128)S(1)} fusion(bf16[1792,256]{1,0:T(8,128)(2,1)} %outer_ref.1, bf16[16,512]{1,0:T(8,128)(2,1)S(1)} %fusion.9.scale_ref), kind=kOutput, calls=%fused_computation.27 | convolution fusion | flops 14680064 | bytes 1040384 | tf_op jit(solution)/shard_map/dot_general | solution.py:463
  65.9 3.3 %collective-permute-done.2 = bf16[32,512]{1,0:T(8,128)(2,1)S(1)} collective-permute-done((bf16[32,512]{1,0:T(8,128)(2,1)S(1)}, bf16[32,512]{1,0:T(8,128)(2,1)S(1)}, u32[]{:S(2)}, u32[]{:S(2)}) %collective-permute-start.2) | collective-permute-done | bytes 32800 | tf_op jit(solution)/shard_map/ppermute | solution.py:456
  70.5 1.9 %collective-permute-start.6 = (bf16[512,1792]{1,0:T(8,128)(2,1)S(1)}, bf16[512,1792]{1,0:T(8,128)(2,1)}, u32[]{:S(2)}, u32[]{:S(2)}) collective-permute-start(bf16[512,1792]{1,0:T(8,128)(2,1)S(1)} %bitcast.27), channel_id=1, source_target_pairs={{0,128},{128,0},{1,129},{129,1},{2,130},{130,2},{3,131},{131,3},{4... | collective-permute-start | bytes 5505032 | tf_op jit(solution)/shard_map/ppermute | solution.py:482
  72.4 5.2 %all-to-all-done.2 = bf16[8,32,512]{2,1,0:T(8,128)(2,1)S(1)} async-done(((bf16[8,32,512]{2,1,0:T(8,128)(2,1)}), bf16[8,32,512]{2,1,0:T(8,128)(2,1)S(1)}, u32[]{:S(2)}, u32[]{:S(2)}) %all-to-all-start.2) | async-done | bytes 262176 | tf_op jit(solution)/shard_map/all_to_all | solution.py:484
  77.7 31.3 %all_gather.3.combined_ref = bf16[512,512]{1,0:T(8,128)(2,1)S(1)} all-gather(bf16[32,512]{1,0:T(8,128)(2,1)S(1)} %add_convert_fusion.1), channel_id=1, replica_groups=mesh['yh'=2,'core'=2,'x'=4,'yl'=2,'zh'=8,'zl'=2] {'zh','zl'}, dimensions={0}, use_global_device_ids=true | all-gather | bytes 557056 | tf_op jit(solution)/shard_map/all_gather | solution.py:486
  110.2 3.5 %all-to-all-start.3 = ((bf16[16,32,128]{2,1,0:T(8,128)(2,1)}), bf16[16,32,128]{2,1,0:T(8,128)(2,1)S(1)}, u32[]{:S(2)}, u32[]{:S(2)}) async-start(bf16[16,32,128]{2,1,0:T(8,128)(2,1)} %token_sums.1), calls=%async_computation.3 | async-start | bytes 262144 | tf_op jit(solution)/shard_map/all_to_all | solution.py:490
  113.7 3.5 %back.1 = bf16[16,32,1792]{2,1,0:T(8,128)(2,1)} custom-call(bf16[512,512]{1,0:T(8,128)(2,1)S(1)} %all_gather.3.combined_ref, bf16[1792,256]{1,0:T(8,128)(2,1)} %outer_ref.1, bf16[1792,256]{1,0:T(8,128)(2,1)S(1)} %hold.1.other_ref), custom_call_target="tpu_custom_call" | custom-call | flops 939524096 | bytes 3670016 | tf_op jit(solution)/shard_map/back/pallas_call | solution.py:210
  117.2 5.2 %all-to-all-done.3.sums_ref = bf16[16,32,128]{2,1,0:T(8,128)(2,1)S(1)} async-done(((bf16[16,32,128]{2,1,0:T(8,128)(2,1)}), bf16[16,32,128]{2,1,0:T(8,128)(2,1)S(1)}, u32[]{:S(2)}, u32[]{:S(2)}) %all-to-all-start.3) | async-done | bytes 131104 | tf_op jit(solution)/shard_map/all_to_all | solution.py:490
  122.4 7.9 %all-to-all-start.4 = ((bf16[16,32,1792]{2,1,0:T(8,128)(2,1)}), bf16[16,32,1792]{2,1,0:T(8,128)(2,1)}, u32[]{:S(2)}, u32[]{:S(2)}) async-start(bf16[16,32,1792]{2,1,0:T(8,128)(2,1)} %back.1), calls=%async_computation.4 | async-start | bytes 3670016 | tf_op jit(solution)/shard_map/all_to_all | solution.py:493
  130.6 1.9 %collective-permute-start.3 = (f32[32,128]{1,0:T(8,128)S(1)}, f32[32,128]{1,0:T(8,128)S(1)}, u32[]{:S(2)}, u32[]{:S(2)}) collective-permute-start(f32[32,128]{1,0:T(8,128)S(1)} %token_terms.1.own_pack_ref.pack_ref), channel_id=1, source_target_pairs={{0,128},{128,0},{1,129},{129,1},{2,130},{130,2},{3,131},{131,3},{4... | collective-permute-start | bytes 49160 | tf_op jit(solution)/shard_map/ppermute | solution.py:497
  132.5 2.4 %collective-permute-start.5 = (bf16[512,256]{1,0:T(8,128)(2,1)S(1)}, bf16[512,256]{1,0:T(8,128)(2,1)S(1)}, u32[]{:S(2)}, u32[]{:S(2)}) collective-permute-start(bf16[512,256]{1,0:T(8,128)(2,1)S(1)} %get-tuple-element.38), channel_id=1, source_target_pairs={{0,128},{128,0},{1,129},{129,1},{2,130},{130,2},{3,131},{131,3},{4... | collective-permute-start | bytes 786440 | tf_op jit(solution)/shard_map/ppermute | solution.py:494
  135.0 5.3 %collective-permute-start.4 = (f32[4,128]{1,0:T(4,128)S(1)}, f32[4,128]{1,0:T(4,128)S(1)}, u32[]{:S(2)}, u32[]{:S(2)}) collective-permute-start(f32[4,128]{1,0:T(4,128)S(1)} %pad_maximum_fusion.1), channel_id=1, source_target_pairs={{0,256},{256,0},{1,257},{257,1},{2,258},{258,2},{3,259},{259,3},{4... | collective-permute-start | bytes 6152 | tf_op jit(solution)/shard_map/ppermute | solution.py:506
  140.3 4.5 %weight_gradient.1 = (f32[1792,256]{1,0:T(8,128)}, f32[1,1]{1,0:T(1,128)}) custom-call(f32[32,128]{1,0:T(8,128)S(1)} %token_terms.1.own_pack_ref.pack_ref, f32[32,128]{1,0:T(8,128)S(1)} %collective-permute-done.3.other_pack_ref, bf16[512,256]{1,0:T(8,128)(2,1)S(1)} %get-tuple-element.39.own_ref, bf16[512,256]{1,0:T(8,128)(2,1)S(1)} %collective-permute-done.5.other_ref, ...), custom_call_target="tpu_custom_call" | custom-call | flops 939524096 | bytes 3670016 | tf_op jit(solution)/shard_map/weight_gradient/pallas_call | solution.py:360
  145.5 4.2 %all-to-all-done.4.arrived_ref = bf16[16,32,1792]{2,1,0:T(8,128)(2,1)} async-done(((bf16[16,32,1792]{2,1,0:T(8,128)(2,1)}), bf16[16,32,1792]{2,1,0:T(8,128)(2,1)}, u32[]{:S(2)}, u32[]{:S(2)}) %all-to-all-start.4) | async-done | bytes 1835040 | tf_op jit(solution)/shard_map/all_to_all | solution.py:493
  149.6 2.4 %hidden_gradient.1 = bf16[32,1792]{1,0:T(8,128)(2,1)} custom-call(s32[1]{0:T(128)} %bitcast.15.spot_ref, bf16[16,32,1792]{2,1,0:T(8,128)(2,1)} %all-to-all-done.4.arrived_ref, f32[32,128]{1,0:T(8,128)S(1)} %token_terms.1.own_pack_ref.pack_ref), custom_call_target="tpu_custom_call" | custom-call | flops 3670016 | bytes 1835008 | tf_op jit(solution)/shard_map/hidden_gradient/pallas_call | solution.py:299
  (58 shorter events, 15.5 us)
Async XLA Ops:
  0.6 0.9 copy-start.2
  2.5 12.0 %all-to-all-start = ((bf16[4,32,1792]{2,1,0:T(8,128)(2,1)}), bf16[4,32,1792]{2,1,0:T(8,128)(2,1)S(1)}, u32[]{:S(2)}, u32[]{:S(2)}) async-start(bf16[4,32,1792]{2,1,0:T(8,128)(2,1)} %spread.2), calls=%async_computation | async-start | bytes 917504 | tf_op jit(solution)/shard_map/all_to_all | solution.py:436
  16.0 4.8 %copy-start = (bf16[1792,256]{1,0:T(8,128)(2,1)S(1)}, bf16[1792,256]{1,0:T(8,128)(2,1)}, u32[]{:S(2)}) copy-start(bf16[1792,256]{1,0:T(8,128)(2,1)} %outer_ref.1) | copy-start | bytes 2752516
  16.0 6.8 %copy-start.7 = (f32[16]{0:T(128)S(1)}, f32[16]{0:T(128)}, u32[]{:S(2)}) copy-start(f32[16]{0:T(128)} %param.18) | copy-start | bytes 196
  16.1 6.9 %copy-start.4 = (f32[1024]{0:T(1024)S(1)}, f32[1024]{0:T(1024)}, u32[]{:S(2)}) copy-start(f32[1024]{0:T(1024)} %param.17) | copy-start | bytes 12292
  16.1 7.0 %copy-start.5 = (f32[1024]{0:T(1024)S(1)}, f32[1024]{0:T(1024)}, u32[]{:S(2)}) copy-start(f32[1024]{0:T(1024)} %param.15) | copy-start | bytes 12292
  16.1 6.9 %copy-start.6 = (f32[1024]{0:T(1024)S(1)}, f32[1024]{0:T(1024)}, u32[]{:S(2)}) copy-start(f32[1024]{0:T(1024)} %param.16) | copy-start | bytes 12292
  16.1 19.7 %all-to-all-start.1 = ((bf16[4,128,1792]{2,1,0:T(8,128)(2,1)}), bf16[4,128,1792]{2,1,0:T(8,128)(2,1)S(1)}, u32[]{:S(2)}, u32[]{:S(2)}) async-start(bf16[4,128,1792]{2,1,0:T(8,128)(2,1)} %spread.3), calls=%async_computation.1 | async-start | bytes 3670016 | tf_op jit(solution)/shard_map/all_to_all | solution.py:442
  20.8 4.4 %collective-permute-start = (bf16[1792,256]{1,0:T(8,128)(2,1)S(1)}, bf16[1792,256]{1,0:T(8,128)(2,1)S(1)}, u32[]{:S(2)}, u32[]{:S(2)}) collective-permute-start(bf16[1792,256]{1,0:T(8,128)(2,1)S(1)} %copy-done), channel_id=1, source_target_pairs={{0,128},{128,0},{1,129},{129,1},{2,130},{130,2},{3,131},{131,3},{4... | collective-permute-start | bytes 2752520 | tf_op jit(solution)/shard_map/ppermute | solution.py:445
  35.8 1.2 copy-start.1
  37.6 10.0 %collective-permute-start.1 = (bf16[256,512]{1,0:T(8,128)(2,1)S(1)}, bf16[256,512]{1,0:T(8,128)(2,1)S(1)}, u32[]{:S(2)}, u32[]{:S(2)}) collective-permute-start(bf16[256,512]{1,0:T(8,128)(2,1)S(1)} %forward.3), channel_id=1, source_target_pairs={{0,1},{1,0},{2,3},{3,2},{4,5},{5,4},{6,7},{7,6},{8,9},{9,8},{10,11... | collective-permute-start | bytes 786440 | tf_op jit(solution)/shard_map/ppermute | solution.py:479
  48.4 29.2 %all-to-all-start.2 = ((bf16[8,32,512]{2,1,0:T(8,128)(2,1)}), bf16[8,32,512]{2,1,0:T(8,128)(2,1)S(1)}, u32[]{:S(2)}, u32[]{:S(2)}) async-start(bf16[8,32,512]{2,1,0:T(8,128)(2,1)} %bitcast.9), calls=%async_computation.2 | async-start | bytes 524288 | tf_op jit(solution)/shard_map/all_to_all | solution.py:484
  61.8 7.3 %collective-permute-start.2 = (bf16[32,512]{1,0:T(8,128)(2,1)S(1)}, bf16[32,512]{1,0:T(8,128)(2,1)S(1)}, u32[]{:S(2)}, u32[]{:S(2)}) collective-permute-start(bf16[32,512]{1,0:T(8,128)(2,1)S(1)} %dynamic_slice.19), channel_id=1, source_target_pairs={{0,256},{256,0},{1,257},{257,1},{2,258},{258,2},{3,259},{259,3},{4... | collective-permute-start | bytes 98312 | tf_op jit(solution)/shard_map/ppermute | solution.py:456
  70.5 69.8 %collective-permute-start.6 = (bf16[512,1792]{1,0:T(8,128)(2,1)S(1)}, bf16[512,1792]{1,0:T(8,128)(2,1)}, u32[]{:S(2)}, u32[]{:S(2)}) collective-permute-start(bf16[512,1792]{1,0:T(8,128)(2,1)S(1)} %bitcast.27), channel_id=1, source_target_pairs={{0,128},{128,0},{1,129},{129,1},{2,130},{130,2},{3,131},{131,3},{4... | collective-permute-start | bytes 5505032 | tf_op jit(solution)/shard_map/ppermute | solution.py:482
  110.2 12.2 %all-to-all-start.3 = ((bf16[16,32,128]{2,1,0:T(8,128)(2,1)}), bf16[16,32,128]{2,1,0:T(8,128)(2,1)S(1)}, u32[]{:S(2)}, u32[]{:S(2)}) async-start(bf16[16,32,128]{2,1,0:T(8,128)(2,1)} %token_sums.1), calls=%async_computation.3 | async-start | bytes 262144 | tf_op jit(solution)/shard_map/all_to_all | solution.py:490
  122.4 27.3 %all-to-all-start.4 = ((bf16[16,32,1792]{2,1,0:T(8,128)(2,1)}), bf16[16,32,1792]{2,1,0:T(8,128)(2,1)}, u32[]{:S(2)}, u32[]{:S(2)}) async-start(bf16[16,32,1792]{2,1,0:T(8,128)(2,1)} %back.1), calls=%async_computation.4 | async-start | bytes 3670016 | tf_op jit(solution)/shard_map/all_to_all | solution.py:493
  130.6 4.4 %collective-permute-start.3 = (f32[32,128]{1,0:T(8,128)S(1)}, f32[32,128]{1,0:T(8,128)S(1)}, u32[]{:S(2)}, u32[]{:S(2)}) collective-permute-start(f32[32,128]{1,0:T(8,128)S(1)} %token_terms.1.own_pack_ref.pack_ref), channel_id=1, source_target_pairs={{0,128},{128,0},{1,129},{129,1},{2,130},{130,2},{3,131},{131,3},{4... | collective-permute-start | bytes 49160 | tf_op jit(solution)/shard_map/ppermute | solution.py:497
  132.5 7.7 %collective-permute-start.5 = (bf16[512,256]{1,0:T(8,128)(2,1)S(1)}, bf16[512,256]{1,0:T(8,128)(2,1)S(1)}, u32[]{:S(2)}, u32[]{:S(2)}) collective-permute-start(bf16[512,256]{1,0:T(8,128)(2,1)S(1)} %get-tuple-element.38), channel_id=1, source_target_pairs={{0,128},{128,0},{1,129},{129,1},{2,130},{130,2},{3,131},{131,3},{4... | collective-permute-start | bytes 786440 | tf_op jit(solution)/shard_map/ppermute | solution.py:494
  135.0 9.9 %collective-permute-start.4 = (f32[4,128]{1,0:T(4,128)S(1)}, f32[4,128]{1,0:T(4,128)S(1)}, u32[]{:S(2)}, u32[]{:S(2)}) collective-permute-start(f32[4,128]{1,0:T(4,128)S(1)} %pad_maximum_fusion.1), channel_id=1, source_target_pairs={{0,256},{256,0},{1,257},{257,1},{2,258},{258,2},{3,259},{259,3},{4... | collective-permute-start | bytes 6152 | tf_op jit(solution)/shard_map/ppermute | solution.py:506
  140.3 4.6 %copy-start.3 = (f32[1024]{0:T(1024)S(1)}, f32[1024]{0:T(1024)}, u32[]{:S(2)}) copy-start(f32[1024]{0:T(1024)} %param.14) | copy-start | bytes 12292
